TPU v7x, 32 devices: a whole 2x2x4 slice. The times are simulated.
32 devices in a mesh: prompt: 8 (over z, core), resp: 4 (over y, x).
Axes of the slice: x: 2, y: 2, z: 4, core: 2. Of those that a mesh axis runs over, the one named last changes fastest.
Arguments:
- answer_asking_tensor: bfloat16 [8, 4, 256, 2048], P('prompt', 'resp'), may hold values from -5 to 5
- answer_lookup_tensor: bfloat16 [8, 4, 256, 512], P('prompt', 'resp'), may hold values from -6 to 6
- answer_content_tensor: bfloat16 [8, 4, 256, 512], P('prompt', 'resp'), may hold values from -6 to 6
- unweighted_mixing_backprop: bfloat16 [8, 4, 256, 2048], P('prompt', 'resp'), may hold values from -6 to 6
- question_lookup_tensor: bfloat16 [8, 256, 512], P('prompt', 'resp'), may hold values from -6 to 6
- question_content_tensor: bfloat16 [8, 256, 512], P('prompt', 'resp'), may hold values from -6 to 6
- kept_rollout_number: int32 [8], P('prompt'), may hold values from 2 to 4, as said below
- spaces_kept_leading: int32 [8, 4], P('prompt'), may hold values from 0 to 3, each once within a row
- answer_span_tilecounts: int32 [8, 4], P('prompt', 'resp'), may hold values from 1 to 2
- rollout_payoffs: float32 [8, 4], P('prompt', 'resp'), may hold values from 0 to 1
Outputs:
- attn_out: bfloat16 [8, 4, 256, 2048], P('prompt', 'resp')
- query_grad: bfloat16 [8, 4, 256, 2048], P('prompt', 'resp')
- key_grad: bfloat16 [8, 4, 256, 512], P('prompt', 'resp')
- value_grad: bfloat16 [8, 4, 256, 512], P('prompt', 'resp')
- prompt_key_gradient: bfloat16 [8, 256, 512], P('prompt', 'resp')
- prompt_value_gradient: bfloat16 [8, 256, 512], P('prompt', 'resp')
Inputs may be any that keep to these rules, and one draw needn't show every extreme that they name: `kept_rollout_number`: at least one prompt keeps all 4 responses. `spaces_kept_leading`: each row is an ordering of the 4 slots; the first survivors entries name the surviving slots.
All inputs are finite; a program needn't handle non-finite values.
Results may differ from a plain program's by a relative error of at most 0.012.
The roundings to bfloat16 on the way count: a program that leaves them out, or rounds other values in their place, can miss the bound.
Values may be sent and summed in bfloat16 or wider, within the bound.
No kernel may reach another device: no remote copies, remote signals or barrier semaphores. Data moves between devices by JAX's collectives and lax.ppermute only.
A program may use at most 64 MiB of HBM per device.

v0:
```python
import jax
import jax.numpy as jnp
from jax import lax
from jax.sharding import PartitionSpec as P

QUERY_HEADS = 16
KEY_VALUE_HEADS = 4
HEAD_SIZE = 128
BLOCK = 128
RESPONSE_TOKENS = 256


def local(
    answer_asking_tensor,
    answer_lookup_tensor,
    answer_content_tensor,
    unweighted_mixing_backprop,
    question_lookup_tensor,
    question_content_tensor,
    kept_rollout_number,
    spaces_kept_leading,
    answer_span_tilecounts,
    rollout_payoffs,
):
    group_queries = QUERY_HEADS // KEY_VALUE_HEADS
    scaling = HEAD_SIZE ** (-0.5)
    member = lax.axis_index("resp")
    rollout_line = spaces_kept_leading[0]
    cohort_breadth = kept_rollout_number[0]
    member_indexes = jnp.arange(rollout_line.shape[0])
    living = jnp.sum(
        jnp.where((member_indexes < cohort_breadth) & (rollout_line == member), 1, 0)
    ).astype(jnp.int32)
    live_length = living * answer_span_tilecounts[0, 0] * BLOCK
    reward = rollout_payoffs[0, 0]
    reward_sum = lax.psum(living.astype(jnp.float32) * reward, "resp")
    batch_live = lax.psum(cohort_breadth.astype(jnp.float32), "prompt")
    slot_weight = (reward - reward_sum / cohort_breadth.astype(jnp.float32)) / batch_live
    whole_keys, whole_values = (
        lax.all_gather(question_lookup_tensor, "resp", axis=1, tiled=True),
        lax.all_gather(question_content_tensor, "resp", axis=1, tiled=True),
    )
    prefix_len = whole_keys.shape[1]
    key_total = prefix_len + RESPONSE_TOKENS
    joined_keys = jnp.concatenate([whole_keys[0], answer_lookup_tensor[0, 0]], 0)
    joined_values = jnp.concatenate([whole_values[0], answer_content_tensor[0, 0]], 0)
    is_valid = jnp.arange(RESPONSE_TOKENS) < live_length
    output_cotangent = jnp.where(
        is_valid[:, None], unweighted_mixing_backprop[0, 0].astype(jnp.float32) * slot_weight, 0.0
    ).astype(jnp.bfloat16)
    query_segments = (
        answer_asking_tensor[0, 0]
        .reshape(RESPONSE_TOKENS, KEY_VALUE_HEADS, group_queries, HEAD_SIZE)
        .transpose(1, 0, 2, 3)
    )
    cotangent_pieces = output_cotangent.reshape(
        RESPONSE_TOKENS, KEY_VALUE_HEADS, group_queries, HEAD_SIZE
    ).transpose(1, 0, 2, 3)
    key_segments = joined_keys.reshape(key_total, KEY_VALUE_HEADS, HEAD_SIZE).transpose(1, 0, 2)
    value_segments = joined_values.reshape(key_total, KEY_VALUE_HEADS, HEAD_SIZE).transpose(1, 0, 2)
    row_index = jnp.arange(RESPONSE_TOKENS)[:, None]
    col_index = jnp.arange(key_total)[None, :]
    allowed = (col_index < prefix_len) | (col_index - prefix_len <= row_index)

    def attend_core(query_segment, cotangent_piece, key_segment, value_segment):
        scores = (
            jnp.einsum(
                "wkb,xb->kwx", query_segment, key_segment, preferred_element_type=jnp.float32
            )
            * scaling
        )
        scores = jnp.where(allowed, scores, -1e30)
        highest = jnp.max(scores, axis=-1, keepdims=True)
        expo = jnp.exp(scores - highest)
        probs = expo / jnp.sum(expo, axis=-1, keepdims=True)
        probability_lower = probs.astype(jnp.bfloat16)
        attended = jnp.einsum(
            "nwh,hy->wny", probability_lower, value_segment, preferred_element_type=jnp.float32
        )
        attn_part = jnp.where(is_valid[:, None, None], attended, 0.0).astype(jnp.bfloat16)
        probability_grad = jnp.einsum(
            "wkb,xb->kwx", cotangent_piece, value_segment, preferred_element_type=jnp.float32
        )
        delta = jnp.sum(cotangent_piece.astype(jnp.float32) * attended, axis=-1).T
        score_gradient = (probs * (probability_grad - delta[:, :, None]) * scaling).astype(
            jnp.bfloat16
        )
        query_part_grad = jnp.einsum(
            "nwh,hy->wny", score_gradient, key_segment, preferred_element_type=jnp.float32
        ).astype(jnp.bfloat16)
        return (attn_part, query_part_grad, score_gradient, probability_lower)

    def join_heads(stacked_arrays):
        return stacked_arrays.transpose(1, 0, 2, 3).reshape(
            RESPONSE_TOKENS, QUERY_HEADS * HEAD_SIZE
        )

    def join_keys(stacked_arrays):
        return stacked_arrays.transpose(1, 0, 2).reshape(
            stacked_arrays.shape[1], KEY_VALUE_HEADS * HEAD_SIZE
        )

    def attend_whole(inputs):
        query_segment, cotangent_piece, key_segment, value_segment = inputs
        attn_part, query_part_grad, score_gradient, probability_lower = attend_core(
            query_segment, cotangent_piece, key_segment, value_segment
        )
        key_contribution = jnp.einsum(
            "yof,oyp->fp", score_gradient, query_segment, preferred_element_type=jnp.float32
        )
        value_contribution = jnp.einsum(
            "yof,oyp->fp", probability_lower, cotangent_piece, preferred_element_type=jnp.float32
        )
        return (attn_part, query_part_grad, key_contribution, value_contribution)

    attn_all, query_all_grad, key_terms, value_terms = lax.map(
        attend_whole, (query_segments, cotangent_pieces, key_segments, value_segments)
    )
    key_terms = join_keys(key_terms)
    value_terms = join_keys(value_terms)
    own_key_grad = key_terms[prefix_len:].astype(jnp.bfloat16)
    own_value_grad = value_terms[prefix_len:].astype(jnp.bfloat16)
    partial_value = jnp.concatenate([key_terms[:prefix_len], value_terms[:prefix_len]], 1)
    summed_values = lax.psum_scatter(
        partial_value.astype(jnp.bfloat16), "resp", scatter_dimension=0, tiled=True
    ).astype(jnp.float32)
    attn_out = join_heads(attn_all)[None, None]
    query_grad = join_heads(query_all_grad)[None, None]
    prompt_key_gradient = summed_values[:, : KEY_VALUE_HEADS * HEAD_SIZE].astype(jnp.bfloat16)[None]
    prompt_value_gradient = summed_values[:, KEY_VALUE_HEADS * HEAD_SIZE :].astype(jnp.bfloat16)[
        None
    ]
    return (
        attn_out,
        query_grad,
        own_key_grad[None, None],
        own_value_grad[None, None],
        prompt_key_gradient,
        prompt_value_gradient,
    )


def solution(mesh):
    placed = (
        P("prompt", "resp", None, None),
        P("prompt", "resp", None, None),
        P("prompt", "resp", None, None),
        P("prompt", "resp", None, None),
        P("prompt", "resp", None),
        P("prompt", "resp", None),
        P("prompt"),
        P("prompt", None),
        P("prompt", "resp"),
        P("prompt", "resp"),
    )
    return jax.shard_map(
        local,
        mesh=mesh,
        in_specs=placed,
        out_specs=(
            P("prompt", "resp", None, None),
            P("prompt", "resp", None, None),
            P("prompt", "resp", None, None),
            P("prompt", "resp", None, None),
            P("prompt", "resp", None),
            P("prompt", "resp", None),
        ),
        check_vma=False,
    )
```

profile of v0, /device:TPU:0, one launch (start us, length us, event | category | flops | bytes accessed | tf_op | source)
XLA Modules:
  0.0 142.7 jit_solution(7690019299466985344)
XLA Ops:
  10.5 11.9 %psum.14 = f32[]{:T(128)} all-reduce(f32[]{:T(128)S(6)} %mul.36), channel_id=1, replica_groups=mesh['prompt'=8,'resp'=4] {'resp'}, use_global_device_ids=true, to_apply=%region_1.2 | all-reduce | flops 1 | bytes 8 | tf_op jit(solution)/shard_map/psum | solution.py:36
  22.4 15.1 %psum.15 = f32[]{:T(128)} all-reduce(f32[]{:T(128)S(6)} %convert_element_type.62), channel_id=1, replica_groups=mesh['prompt'=8,'resp'=4] {'prompt'}, use_global_device_ids=true, to_apply=%region_2.3 | all-reduce | flops 1 | bytes 8 | tf_op jit(solution)/shard_map/psum | solution.py:37
  42.3 8.0 %all_gather.6 = bf16[1,256,512]{2,1,0:T(8,128)(2,1)S(1)} all-gather(bf16[1,64,512]{2,1,0:T(8,128)(2,1)S(1)} %copy-done.9), channel_id=1, replica_groups=mesh['prompt'=8,'resp'=4] {'resp'}, dimensions={1}, use_global_device_ids=true | all-gather | bytes 327680 | tf_op jit(solution)/shard_map/all_gather | solution.py:41
  50.5 9.2 %all_gather.7 = bf16[1,256,512]{2,1,0:T(8,128)(2,1)S(1)} all-gather(bf16[1,64,512]{2,1,0:T(8,128)(2,1)S(1)} %copy-done.10), channel_id=1, replica_groups=mesh['prompt'=8,'resp'=4] {'resp'}, dimensions={1}, use_global_device_ids=true | all-gather | bytes 327680 | tf_op jit(solution)/shard_map/all_gather | solution.py:40
  60.5 1.8 %copy.58 = bf16[1,1,256,512]{2,3,1,0:T(8,128)(2,1)} copy(bf16[1,1,256,512]{3,2,1,0:T(8,128)(2,1)} %param.14) | data formatting | bytes 524288 | tf_op args[2]
  65.7 43.3 %while.17 = (s32[]{:T(128)}, bf16[4,256,4,128]{1,3,2,0:T(8,128)(2,1)}, bf16[4,256,4,128]{1,3,2,0:T(8,128)(2,1)}, bf16[4,512,128]{2,1,0:T(8,128)(2,1)}, bf16[4,51...) while((s32[]{:T(128)}, ...), condition=%wide.region_7.8_spmd.clone, body=%wide.region_3.7_spmd.clone.sunk | while | flops 1084623616 | bytes 16813500 | solution.py:116
  65.9 2.2 %fusion.127 = (f32[4,256]{1,0:T(4,128)S(1)}, f32[4,256,512]{1,2,0:T(8,128)}) fusion(pred[256,512]{0,1:T(8,128)(4,1)S(1)} %fusion.126, bf16[4,256,4,128]{1,3,2,0:T(8,128)(2,1)S(1)} %get-tuple-element.274, s32[]{:T(128)} %get-tuple-element.254, bf16[4,512,128]{1,2,0:T(8,128)(2,1)S(1)} %get-tuple-element.273), kind=kOutput, calls=%fused_computation.78.clone.1 | convolution fusion | flops 136315392 | bytes 2626560 | tf_op jit(solution)/shard_map/while/body/eval_jaxpr/sub | solution.py:74
  68.1 2.8 %fusion.128 = (bf16[4,256,4,128]{1,3,2,0:T(8,128)(2,1)}, f32[256,4,128]{0,2,1:T(8,128)S(1)}) fusion(bf16[4,256,4,128]{1,3,2,0:T(8,128)(2,1)} %get-tuple-element.255, s32[]{:T(128)} %get-tuple-element.254, pred[256]{0:T(512)(128)(4,1)S(1)} %iota_compare_fusion.5, f32[4,256]{1,0:T(4,128)S(1)} %get-tuple-element.237, ...), kind=kOutput, calls=%fused_computation.28.clone.1 | convolution fusion | flops 271189504 | bytes 1448448 | tf_op jit(solution)/shard_map/while/body/eval_jaxpr/nwh,hy->wny/dot_general | solution.py:77
  70.9 2.2 %fusion.129 = bf16[4,256,512]{1,2,0:T(8,128)(2,1)S(1)} fusion(f32[4,256]{1,0:T(4,128)S(1)} %bitcast.232, f32[4,256,512]{1,2,0:T(8,128)} %get-tuple-element.240, f32[4,256]{1,0:T(4,128)S(1)} %get-tuple-element.237, bf16[4,256,4,128]{1,3,2,0:T(8,128)(2,1)S(1)} %get-tuple-element.275, s32[]{:T(128)} %get-tuple-element.254, ...), kind=kOutput, calls=%fused_computation.6.clone.1 | convolution fusion | flops 136839168 | bytes 3548160 | tf_op jit(solution)/shard_map/while/body/eval_jaxpr/wkb,xb->kwx/dot_general | solution.py:81
  74.7 1.8 %fusion.132 = bf16[4,512,128]{2,1,0:T(8,128)(2,1)} fusion(bf16[4,512,128]{2,1,0:T(8,128)(2,1)} %get-tuple-element.258, s32[]{:T(128)} %get-tuple-element.254, bf16[4,256,4,128]{1,3,2,0:T(8,128)(2,1)S(1)} %get-tuple-element.275, f32[4,256]{1,0:T(4,128)S(1)} %get-tuple-element.237, pred[256,512]{0,1:T(8,128)(4,1)S(1)} %fusion.126, ...), kind=kOutput, calls=%fused_computation.15.clone.1 | convolution fusion | flops 271058432 | bytes 1054720 | tf_op jit(solution)/shard_map/while/body/eval_jaxpr/yof,oyp->fp/dot_general | solution.py:111
  76.7 2.2 %fusion.127 = (f32[4,256]{1,0:T(4,128)S(1)}, f32[4,256,512]{1,2,0:T(8,128)}) fusion(pred[256,512]{0,1:T(8,128)(4,1)S(1)} %fusion.126, bf16[4,256,4,128]{1,3,2,0:T(8,128)(2,1)S(1)} %get-tuple-element.274, s32[]{:T(128)} %get-tuple-element.254, bf16[4,512,128]{1,2,0:T(8,128)(2,1)S(1)} %get-tuple-element.273), kind=kOutput, calls=%fused_computation.78.clone.1 | convolution fusion | flops 136315392 | bytes 2626560 | tf_op jit(solution)/shard_map/while/body/eval_jaxpr/sub | solution.py:74
  78.9 2.8 %fusion.128 = (bf16[4,256,4,128]{1,3,2,0:T(8,128)(2,1)}, f32[256,4,128]{0,2,1:T(8,128)S(1)}) fusion(bf16[4,256,4,128]{1,3,2,0:T(8,128)(2,1)} %get-tuple-element.255, s32[]{:T(128)} %get-tuple-element.254, pred[256]{0:T(512)(128)(4,1)S(1)} %iota_compare_fusion.5, f32[4,256]{1,0:T(4,128)S(1)} %get-tuple-element.237, ...), kind=kOutput, calls=%fused_computation.28.clone.1 | convolution fusion | flops 271189504 | bytes 1448448 | tf_op jit(solution)/shard_map/while/body/eval_jaxpr/nwh,hy->wny/dot_general | solution.py:77
  81.8 2.2 %fusion.129 = bf16[4,256,512]{1,2,0:T(8,128)(2,1)S(1)} fusion(f32[4,256]{1,0:T(4,128)S(1)} %bitcast.232, f32[4,256,512]{1,2,0:T(8,128)} %get-tuple-element.240, f32[4,256]{1,0:T(4,128)S(1)} %get-tuple-element.237, bf16[4,256,4,128]{1,3,2,0:T(8,128)(2,1)S(1)} %get-tuple-element.275, s32[]{:T(128)} %get-tuple-element.254, ...), kind=kOutput, calls=%fused_computation.6.clone.1 | convolution fusion | flops 136839168 | bytes 3548160 | tf_op jit(solution)/shard_map/while/body/eval_jaxpr/wkb,xb->kwx/dot_general | solution.py:81
  85.5 1.8 %fusion.132 = bf16[4,512,128]{2,1,0:T(8,128)(2,1)} fusion(bf16[4,512,128]{2,1,0:T(8,128)(2,1)} %get-tuple-element.258, s32[]{:T(128)} %get-tuple-element.254, bf16[4,256,4,128]{1,3,2,0:T(8,128)(2,1)S(1)} %get-tuple-element.275, f32[4,256]{1,0:T(4,128)S(1)} %get-tuple-element.237, pred[256,512]{0,1:T(8,128)(4,1)S(1)} %fusion.126, ...), kind=kOutput, calls=%fused_computation.15.clone.1 | convolution fusion | flops 271058432 | bytes 1054720 | tf_op jit(solution)/shard_map/while/body/eval_jaxpr/yof,oyp->fp/dot_general | solution.py:111
  87.6 2.2 %fusion.127 = (f32[4,256]{1,0:T(4,128)S(1)}, f32[4,256,512]{1,2,0:T(8,128)}) fusion(pred[256,512]{0,1:T(8,128)(4,1)S(1)} %fusion.126, bf16[4,256,4,128]{1,3,2,0:T(8,128)(2,1)S(1)} %get-tuple-element.274, s32[]{:T(128)} %get-tuple-element.254, bf16[4,512,128]{1,2,0:T(8,128)(2,1)S(1)} %get-tuple-element.273), kind=kOutput, calls=%fused_computation.78.clone.1 | convolution fusion | flops 136315392 | bytes 2626560 | tf_op jit(solution)/shard_map/while/body/eval_jaxpr/sub | solution.py:74
  89.8 2.8 %fusion.128 = (bf16[4,256,4,128]{1,3,2,0:T(8,128)(2,1)}, f32[256,4,128]{0,2,1:T(8,128)S(1)}) fusion(bf16[4,256,4,128]{1,3,2,0:T(8,128)(2,1)} %get-tuple-element.255, s32[]{:T(128)} %get-tuple-element.254, pred[256]{0:T(512)(128)(4,1)S(1)} %iota_compare_fusion.5, f32[4,256]{1,0:T(4,128)S(1)} %get-tuple-element.237, ...), kind=kOutput, calls=%fused_computation.28.clone.1 | convolution fusion | flops 271189504 | bytes 1448448 | tf_op jit(solution)/shard_map/while/body/eval_jaxpr/nwh,hy->wny/dot_general | solution.py:77
  92.6 2.2 %fusion.129 = bf16[4,256,512]{1,2,0:T(8,128)(2,1)S(1)} fusion(f32[4,256]{1,0:T(4,128)S(1)} %bitcast.232, f32[4,256,512]{1,2,0:T(8,128)} %get-tuple-element.240, f32[4,256]{1,0:T(4,128)S(1)} %get-tuple-element.237, bf16[4,256,4,128]{1,3,2,0:T(8,128)(2,1)S(1)} %get-tuple-element.275, s32[]{:T(128)} %get-tuple-element.254, ...), kind=kOutput, calls=%fused_computation.6.clone.1 | convolution fusion | flops 136839168 | bytes 3548160 | tf_op jit(solution)/shard_map/while/body/eval_jaxpr/wkb,xb->kwx/dot_general | solution.py:81
  96.3 1.8 %fusion.132 = bf16[4,512,128]{2,1,0:T(8,128)(2,1)} fusion(bf16[4,512,128]{2,1,0:T(8,128)(2,1)} %get-tuple-element.258, s32[]{:T(128)} %get-tuple-element.254, bf16[4,256,4,128]{1,3,2,0:T(8,128)(2,1)S(1)} %get-tuple-element.275, f32[4,256]{1,0:T(4,128)S(1)} %get-tuple-element.237, pred[256,512]{0,1:T(8,128)(4,1)S(1)} %fusion.126, ...), kind=kOutput, calls=%fused_computation.15.clone.1 | convolution fusion | flops 271058432 | bytes 1054720 | tf_op jit(solution)/shard_map/while/body/eval_jaxpr/yof,oyp->fp/dot_general | solution.py:111
  98.4 2.2 %fusion.127 = (f32[4,256]{1,0:T(4,128)S(1)}, f32[4,256,512]{1,2,0:T(8,128)}) fusion(pred[256,512]{0,1:T(8,128)(4,1)S(1)} %fusion.126, bf16[4,256,4,128]{1,3,2,0:T(8,128)(2,1)S(1)} %get-tuple-element.274, s32[]{:T(128)} %get-tuple-element.254, bf16[4,512,128]{1,2,0:T(8,128)(2,1)S(1)} %get-tuple-element.273), kind=kOutput, calls=%fused_computation.78.clone.1 | convolution fusion | flops 136315392 | bytes 2626560 | tf_op jit(solution)/shard_map/while/body/eval_jaxpr/sub | solution.py:74
  100.6 2.8 %fusion.128 = (bf16[4,256,4,128]{1,3,2,0:T(8,128)(2,1)}, f32[256,4,128]{0,2,1:T(8,128)S(1)}) fusion(bf16[4,256,4,128]{1,3,2,0:T(8,128)(2,1)} %get-tuple-element.255, s32[]{:T(128)} %get-tuple-element.254, pred[256]{0:T(512)(128)(4,1)S(1)} %iota_compare_fusion.5, f32[4,256]{1,0:T(4,128)S(1)} %get-tuple-element.237, ...), kind=kOutput, calls=%fused_computation.28.clone.1 | convolution fusion | flops 271189504 | bytes 1448448 | tf_op jit(solution)/shard_map/while/body/eval_jaxpr/nwh,hy->wny/dot_general | solution.py:77
  103.4 2.2 %fusion.129 = bf16[4,256,512]{1,2,0:T(8,128)(2,1)S(1)} fusion(f32[4,256]{1,0:T(4,128)S(1)} %bitcast.232, f32[4,256,512]{1,2,0:T(8,128)} %get-tuple-element.240, f32[4,256]{1,0:T(4,128)S(1)} %get-tuple-element.237, bf16[4,256,4,128]{1,3,2,0:T(8,128)(2,1)S(1)} %get-tuple-element.275, s32[]{:T(128)} %get-tuple-element.254, ...), kind=kOutput, calls=%fused_computation.6.clone.1 | convolution fusion | flops 136839168 | bytes 3548160 | tf_op jit(solution)/shard_map/while/body/eval_jaxpr/wkb,xb->kwx/dot_general | solution.py:81
  107.2 1.8 %fusion.132 = bf16[4,512,128]{2,1,0:T(8,128)(2,1)} fusion(bf16[4,512,128]{2,1,0:T(8,128)(2,1)} %get-tuple-element.258, s32[]{:T(128)} %get-tuple-element.254, bf16[4,256,4,128]{1,3,2,0:T(8,128)(2,1)S(1)} %get-tuple-element.275, f32[4,256]{1,0:T(4,128)S(1)} %get-tuple-element.237, pred[256,512]{0,1:T(8,128)(4,1)S(1)} %fusion.126, ...), kind=kOutput, calls=%fused_computation.15.clone.1 | convolution fusion | flops 271058432 | bytes 1054720 | tf_op jit(solution)/shard_map/while/body/eval_jaxpr/yof,oyp->fp/dot_general | solution.py:111
  117.0 17.3 %reduce-scatter.2.cloned.1.call-done = bf16[64,1024]{1,0:T(8,128)(2,1)} async-done(((bf16[256,1024]{1,0:T(8,128)(2,1)}), bf16[64,1024]{1,0:T(8,128)(2,1)}) %reduce-scatter.2.cloned.1.call-update) | async-done | bytes 131088 | tf_op jit(solution)/shard_map/reduce_scatter | solution.py:124
  134.3 1.5 %slice_bitcast_fusion.2 = (bf16[1,64,512]{2,1,0:T(8,128)(2,1)}, bf16[1,64,512]{2,1,0:T(8,128)(2,1)}) fusion(bf16[64,1024]{1,0:T(8,128)(2,1)} %reduce-scatter.2.cloned.1.call-done), kind=kLoop, calls=%fused_computation.70 | loop fusion | bytes 262144 | tf_op jit(solution)/shard_map/broadcast_in_dim | solution.py:130
  (83 shorter events, 22.8 us)
Async XLA Ops:
  7.2 127.2 %reduce-scatter.2.cloned.1.call-start = ((), (), s32[]{:S(2)}) async-start(), calls=%async_computation.1 | async-start | bytes 655360 | tf_op jit(solution)/shard_map/reduce_scatter | solution.py:124
  38.8 3.4 %copy-start.9 = (bf16[1,64,512]{2,1,0:T(8,128)(2,1)S(1)}, bf16[1,64,512]{2,1,0:T(8,128)(2,1)}, u32[]{:S(2)}) copy-start(bf16[1,64,512]{2,1,0:T(8,128)(2,1)} %param.17) | copy-start | bytes 196612
  38.9 11.6 %copy-start.10 = (bf16[1,64,512]{2,1,0:T(8,128)(2,1)S(1)}, bf16[1,64,512]{2,1,0:T(8,128)(2,1)}, u32[]{:S(2)}) copy-start(bf16[1,64,512]{2,1,0:T(8,128)(2,1)} %param.16) | copy-start | bytes 196612
  40.3 22.8 %copy-start = (bf16[1,1,256,2048]{3,2,1,0:T(8,128)(2,1)S(1)}, bf16[1,1,256,2048]{3,2,1,0:T(8,128)(2,1)}, u32[]{:S(2)}) copy-start(bf16[1,1,256,2048]{3,2,1,0:T(8,128)(2,1)} %param.12) | copy-start | bytes 3145732
  40.9 21.4 %copy-start.8 = (bf16[1,1,256,512]{3,2,1,0:T(8,128)(2,1)S(1)}, bf16[1,1,256,512]{3,2,1,0:T(8,128)(2,1)}, u32[]{:S(2)}) copy-start(bf16[1,1,256,512]{3,2,1,0:T(8,128)(2,1)} %param.13) | copy-start | bytes 786436
  63.7 1.0 copy-start.3
  63.7 1.0 copy-start.4
  63.7 1.1 copy-start.5
  70.9 3.3 %copy-start.6 = (bf16[4,512,128]{2,1,0:T(8,128)(2,1)S(1)}, bf16[4,512,128]{2,1,0:T(8,128)(2,1)}, u32[]{:S(2)}) copy-start(bf16[4,512,128]{2,1,0:T(8,128)(2,1)} %get-tuple-element.257) | copy-start | bytes 1572868 | tf_op jit(solution)/shard_map/while
  74.7 1.8 %copy-start.7 = (bf16[4,512,128]{2,1,0:T(8,128)(2,1)}, bf16[4,512,128]{2,1,0:T(8,128)(2,1)S(1)}, u32[]{:S(2)}) copy-start(bf16[4,512,128]{2,1,0:T(8,128)(2,1)S(1)} %fusion.131) | copy-start | bytes 1572868 | tf_op jit(solution)/shard_map/while
  81.8 3.3 %copy-start.6 = (bf16[4,512,128]{2,1,0:T(8,128)(2,1)S(1)}, bf16[4,512,128]{2,1,0:T(8,128)(2,1)}, u32[]{:S(2)}) copy-start(bf16[4,512,128]{2,1,0:T(8,128)(2,1)} %get-tuple-element.257) | copy-start | bytes 1572868 | tf_op jit(solution)/shard_map/while
  85.5 1.8 %copy-start.7 = (bf16[4,512,128]{2,1,0:T(8,128)(2,1)}, bf16[4,512,128]{2,1,0:T(8,128)(2,1)S(1)}, u32[]{:S(2)}) copy-start(bf16[4,512,128]{2,1,0:T(8,128)(2,1)S(1)} %fusion.131) | copy-start | bytes 1572868 | tf_op jit(solution)/shard_map/while
  92.6 3.3 %copy-start.6 = (bf16[4,512,128]{2,1,0:T(8,128)(2,1)S(1)}, bf16[4,512,128]{2,1,0:T(8,128)(2,1)}, u32[]{:S(2)}) copy-start(bf16[4,512,128]{2,1,0:T(8,128)(2,1)} %get-tuple-element.257) | copy-start | bytes 1572868 | tf_op jit(solution)/shard_map/while
  96.3 1.8 %copy-start.7 = (bf16[4,512,128]{2,1,0:T(8,128)(2,1)}, bf16[4,512,128]{2,1,0:T(8,128)(2,1)S(1)}, u32[]{:S(2)}) copy-start(bf16[4,512,128]{2,1,0:T(8,128)(2,1)S(1)} %fusion.131) | copy-start | bytes 1572868 | tf_op jit(solution)/shard_map/while
  103.4 3.3 %copy-start.6 = (bf16[4,512,128]{2,1,0:T(8,128)(2,1)S(1)}, bf16[4,512,128]{2,1,0:T(8,128)(2,1)}, u32[]{:S(2)}) copy-start(bf16[4,512,128]{2,1,0:T(8,128)(2,1)} %get-tuple-element.257) | copy-start | bytes 1572868 | tf_op jit(solution)/shard_map/while
  107.2 1.8 %copy-start.7 = (bf16[4,512,128]{2,1,0:T(8,128)(2,1)}, bf16[4,512,128]{2,1,0:T(8,128)(2,1)S(1)}, u32[]{:S(2)}) copy-start(bf16[4,512,128]{2,1,0:T(8,128)(2,1)S(1)} %fusion.131) | copy-start | bytes 1572868 | tf_op jit(solution)/shard_map/while
  111.2 3.0 %copy-start.1 = (bf16[4,256,4,128]{1,3,2,0:T(8,128)(2,1)S(1)}, bf16[4,256,4,128]{1,3,2,0:T(8,128)(2,1)}, u32[]{:S(2)}) copy-start(bf16[4,256,4,128]{1,3,2,0:T(8,128)(2,1)} %get-tuple-element.66) | copy-start | bytes 3145732
  112.2 3.5 %copy-start.2 = (bf16[4,256,4,128]{1,3,2,0:T(8,128)(2,1)S(1)}, bf16[4,256,4,128]{1,3,2,0:T(8,128)(2,1)}, u32[]{:S(2)}) copy-start(bf16[4,256,4,128]{1,3,2,0:T(8,128)(2,1)} %get-tuple-element.67) | copy-start | bytes 3145732
Sparse Core Ops, SparseCore 0:
  112.3 21.9 reduce-scatter.1
where the time goes:
time: 143 us
  blocking collectives  44.2 us (31%)
  matrix products  42 us (29%)
  between operations  18.9 us (13%)
  waiting for transfers between devices  17.3 us (12%)
  local copies, waits for them, and re-layouts  14.2 us (10%)
  other arithmetic  5.82 us (4%)
    reduce_scatter x1, waiting for transfers between devices, local(): lax.psum_scatter(partial_value.astype(jnp.bfloat16), 'resp', scatter_dime...  17.3 us
    psum x1, blocking collectives, local(): batch_live = lax.psum(cohort_breadth.astype(jnp.float32), 'prompt')  15.1 us
    psum x1, blocking collectives, local(): reward_sum = lax.psum(living.astype(jnp.float32) * reward, 'resp')  11.9 us
    dot_general x4, matrix products, attend_core(): jnp.einsum('nwh,hy->wny', probability_lower, value_segment, preferred_ele...  11.1 us
    all_gather x1, blocking collectives, local(): lax.all_gather(question_lookup_tensor, 'resp', axis=1, tiled=True)  9.2 us
    dot_general x4, matrix products, attend_core(): jnp.einsum('wkb,xb->kwx', cotangent_piece, value_segment, preferred_eleme...  8.87 us
    sub x4, matrix products, attend_core(): expo = jnp.exp(scores - highest)  8.77 us
    all_gather x1, blocking collectives, local(): lax.all_gather(question_content_tensor, 'resp', axis=1, tiled=True)  8.05 us
  transfers between devices with their start and end apart: 1, of which 1 were waited for; matrix products, arithmetic and copies ran while one was open for 3% of the time, Pallas kernels for 0%

commit v1 on v0

v1 whole, which is shorter than its diff:
```python
import functools
import jax
import jax.numpy as jnp
from jax import lax
from jax.experimental import pallas as pl
from jax.experimental.pallas import tpu as pltpu
from jax.sharding import PartitionSpec as P

HEAD_SIZE = 128
BLOCK = 128
LOG2E = 1.4426950408889634
f32 = jnp.float32
bf16 = jnp.bfloat16


def dot(a, b, ca, cb):
    return lax.dot_general(a, b, (((ca,), (cb,)), ((), ())), preferred_element_type=f32)


def swap(x, axis, n, k):
    return lax.ppermute(x, axis, [(i, i ^ k) for i in range(n)])


def tree_sum(x, axis, n):
    k = 1
    while k < n:
        x = x + swap(x, axis, n, k)
        k *= 2
    return x


def attend_kernel(n, tokens, group, *refs):
    length_ref, weight_ref, q_ref, u_ref, ko_ref, vo_ref = refs[:6]
    kp_refs, vp_refs = refs[6 : 6 + n], refs[6 + n : 6 + 2 * n]
    out_ref, dq_ref, dko_ref, dvo_ref, term_ref = refs[6 + 2 * n :]
    scaling = HEAD_SIZE**-0.5
    weight = weight_ref[0]
    keys = jnp.concatenate([r[...] for r in kp_refs] + [ko_ref[...]], 0)
    values = jnp.concatenate([r[...] for r in vp_refs] + [vo_ref[...]], 0)
    prefix = keys.shape[0] - tokens

    def stack(ref):
        return jnp.concatenate(
            [ref[:, h * HEAD_SIZE : (h + 1) * HEAD_SIZE] for h in range(group)], 0
        )

    def unstack(ref, x):
        for h in range(group):
            ref[:, h * HEAD_SIZE : (h + 1) * HEAD_SIZE] = x[h * tokens : (h + 1) * tokens]

    row = lax.broadcasted_iota(jnp.int32, (tokens, 1), 0)
    valid = jnp.concatenate([row < length_ref[0]] * group, 0)
    causal = lax.broadcasted_iota(jnp.int32, (tokens, tokens), 1) <= row
    causal = jnp.concatenate([causal] * group, 0)

    q = stack(q_ref)
    u = jnp.where(valid, stack(u_ref).astype(f32) * weight, 0.0).astype(bf16)
    s = dot(q, keys, 1, 1)
    s = jnp.concatenate([s[:, :prefix], jnp.where(causal, s[:, prefix:], -1e30)], 1)
    top = jnp.max(s, -1, keepdims=True)
    e = jnp.exp2((s - top) * (scaling * LOG2E))
    p = e * (1.0 / jnp.sum(e, -1, keepdims=True))
    p_low = p.astype(bf16)
    attended = dot(p_low, values, 1, 0)
    unstack(out_ref, jnp.where(valid, attended, 0.0).astype(bf16))
    dp = dot(u, values, 1, 1)
    delta = jnp.sum(u.astype(f32) * attended, -1, keepdims=True)
    ds = (p * (dp - delta) * scaling).astype(bf16)
    unstack(dq_ref, dot(ds, keys, 1, 0).astype(bf16))
    dk = dot(q, ds, 0, 0).T.astype(bf16)
    dv = dot(u, p_low, 0, 0).T.astype(bf16)
    dko_ref[...] = dk[prefix:]
    dvo_ref[...] = dv[prefix:]
    term_ref[0] = dk[:prefix]
    term_ref[1] = dv[:prefix]


def local(q, ko, vo, u, kp, vp, kept, spaces, spans, payoffs):
    n = lax.axis_size("resp")
    n_prompt = lax.axis_size("prompt")
    tokens = q.shape[2]
    kv_heads = ko.shape[3] // HEAD_SIZE
    group = q.shape[3] // ko.shape[3]
    part = kp.shape[1]
    prefix = n * part
    member = lax.axis_index("resp")

    kps = [kp[0]] + [swap(kp, "resp", n, k)[0] for k in range(1, n)]
    vps = [vp[0]] + [swap(vp, "resp", n, k)[0] for k in range(1, n)]

    living = jnp.sum(
        jnp.where((jnp.arange(n) < kept[0]) & (spaces[0] == member), 1, 0)
    ).astype(jnp.int32)
    length = living * spans[0, 0] * BLOCK
    batch_live = tree_sum(kept.astype(f32), "prompt", n_prompt)
    reward_sum = tree_sum(living.astype(f32) * payoffs[0], "resp", n)
    weight = (payoffs[0] - reward_sum / kept.astype(f32)) / batch_live

    def columns(rows, width):
        return pl.BlockSpec((rows, width), lambda g: (0, g))

    scalar = pl.BlockSpec(memory_space=pltpu.SMEM)
    width = group * HEAD_SIZE
    attn_out, dq, dko, dvo, terms = pl.pallas_call(
        functools.partial(attend_kernel, n, tokens, group),
        grid=(kv_heads,),
        in_specs=[scalar, scalar]
        + [columns(tokens, width)] * 2
        + [columns(tokens, HEAD_SIZE)] * 2
        + [columns(part, HEAD_SIZE)] * (2 * n),
        out_specs=[columns(tokens, width)] * 2
        + [columns(tokens, HEAD_SIZE)] * 2
        + [pl.BlockSpec((2, prefix, HEAD_SIZE), lambda g: (0, 0, g))],
        out_shape=[jax.ShapeDtypeStruct(q.shape[2:], bf16)] * 2
        + [jax.ShapeDtypeStruct(ko.shape[2:], bf16)] * 2
        + [jax.ShapeDtypeStruct((2, prefix, kp.shape[2]), bf16)],
        compiler_params=pltpu.CompilerParams(vmem_limit_bytes=56 << 20),
    )(length.reshape(1), weight, q[0, 0], u[0, 0], ko[0, 0], vo[0, 0], *kps, *vps)

    total = terms[:, :part].astype(f32)
    for k in range(1, n):
        total += swap(terms[:, k * part : (k + 1) * part], "resp", n, k).astype(f32)
    total = total.astype(bf16)
    return (
        attn_out[None, None],
        dq[None, None],
        dko[None, None],
        dvo[None, None],
        total[:1],
        total[1:],
    )


def solution(mesh):
    wide = P("prompt", "resp", None, None)
    rows = P("prompt", "resp", None)
    pair = P("prompt", "resp")
    return jax.shard_map(
        local,
        mesh=mesh,
        in_specs=(wide, wide, wide, wide, rows, rows, P("prompt"), P("prompt", None), pair, pair),
        out_specs=(wide, wide, wide, wide, rows, rows),
        check_vma=False,
    )
```

time: 143 us -> 54.4 us (0.38)
  blocking collectives: 44.2 us -> 0 us
  matrix products: 42 us -> 0 us
  starting transfers between devices: 0.04 us -> 25.4 us
  between operations: 18.9 us -> 7.24 us
  local copies, waits for them, and re-layouts: 14.2 us -> 2.98 us
  waiting for transfers between devices: 17.3 us -> 6.68 us
  Pallas kernels: 0 us -> 10.2 us
  other arithmetic: 5.82 us -> 1.6 us
    dot_general x20 -> x0, matrix products: 33.3 us -> none  [the longest x4 11.1 us: attend_core(): jnp.einsum('nwh,hy->wny', probability_lower, value_segment, preferred_ele...]
    psum x2 -> x0, blocking collectives: 27 us -> none  [the longest x1 15.1 us: local(): batch_live = lax.psum(cohort_breadth.astype(jnp.float32), 'prompt')]
    ppermute x0 -> x14, starting transfers between devices: none -> 25.4 us  [swap(): return lax.ppermute(x, axis, [(i, i ^ k) for i in range(n)])]
    reduce_scatter x1 -> x0, waiting for transfers between devices: 17.3 us -> none  [local(): lax.psum_scatter(partial_value.astype(jnp.bfloat16), 'resp', scatter_dime...]
    all_gather x2 -> x0, blocking collectives: 17.3 us -> none  [the longest x1 9.2 us: local(): lax.all_gather(question_lookup_tensor, 'resp', axis=1, tiled=True)]
    pallas_call x0 -> x1, Pallas kernels: none -> 10.2 us  [local(): pl.pallas_call(functools.partial(attend_kernel, n, tokens, group), grid=(...]
    sub x4 -> x0, matrix products: 8.77 us -> none  [attend_core(): expo = jnp.exp(scores - highest)]
    ppermute x0 -> x14, waiting for transfers between devices: none -> 6.68 us  [swap(): return lax.ppermute(x, axis, [(i, i ^ k) for i in range(n)])]
  transfers between devices with their start and end apart: 1 -> 14, of which waited for: 1 -> 7; matrix products, arithmetic and copies ran while one was open for 3% -> 1% of each run, Pallas kernels for 0% -> 0%
where the time goes in v1:
time: 54.4 us; the launch traced here: 54.1 us
  starting transfers between devices  25.4 us (47%)
  Pallas kernels  10.2 us (19%)
  between operations  7.24 us (13%)
  waiting for transfers between devices  6.68 us (12%)
  local copies, waits for them, and re-layouts  2.98 us (5%)
  other arithmetic  1.6 us (3%)
    ppermute x14, starting transfers between devices, swap(): return lax.ppermute(x, axis, [(i, i ^ k) for i in range(n)])  25.4 us
    pallas_call x1, Pallas kernels, local(): pl.pallas_call(functools.partial(attend_kernel, n, tokens, group), grid=(...  10.2 us
    ppermute x14, waiting for transfers between devices, swap(): return lax.ppermute(x, axis, [(i, i ^ k) for i in range(n)])  6.68 us
    unnamed x14, local copies, waits for them, and re-layouts  1.25 us
  transfers between devices with their start and end apart: 14, of which 7 were waited for; matrix products, arithmetic and copies ran while one was open for 1% of the time, Pallas kernels for 0%

profile of v1, /device:TPU:0, one launch (start us, length us, event | category | flops | bytes accessed | tf_op | source)
XLA Modules:
  0.0 54.1 jit_solution(17334213293910988056)
XLA Ops:
  0.6 3.0 %collective-permute-start.5 = (bf16[1,64,512]{2,1,0:T(8,128)(2,1)}, bf16[1,64,512]{2,1,0:T(8,128)(2,1)S(1)}, u32[]{:S(2)}, u32[]{:S(2)}) collective-permute-start(bf16[1,64,512]{2,1,0:T(8,128)(2,1)} %param.14), channel_id=1, source_target_pairs={{0,1},{1,0},{2,3},{3,2},{4,5},{5,4},{6,7},{7,6},{8,9},{9,8},{10,11... | collective-permute-start | bytes 196616 | tf_op jit(solution)/shard_map/ppermute | solution.py:21
  3.6 1.5 %collective-permute-start.7 = (bf16[1,64,512]{2,1,0:T(8,128)(2,1)}, bf16[1,64,512]{2,1,0:T(8,128)(2,1)S(1)}, u32[]{:S(2)}, u32[]{:S(2)}) collective-permute-start(bf16[1,64,512]{2,1,0:T(8,128)(2,1)} %param.14), channel_id=1, source_target_pairs={{0,3},{1,2},{2,1},{3,0},{4,7},{5,6},{6,5},{7,4},{8,11},{9,10},{10,... | collective-permute-start | bytes 196616 | tf_op jit(solution)/shard_map/ppermute | solution.py:21
  6.5 0.6 %copy-done.6 = s32[1,4]{1,0:T(1,128)S(1)} copy-done((s32[1,4]{1,0:T(1,128)S(1)}, s32[1,4]{1,0:T(1,128)}, u32[]{:S(2)}) %copy-start.6) | copy-done | bytes 40
  7.1 0.6 %fusion.1 = s32[]{:T(128)} fusion(s32[1,4]{1,0:T(1,128)S(1)} %copy-done.6, s32[]{:T(128)S(6)} %axis_index.12, s32[]{:T(128)} %bitcast.27), kind=kLoop, calls=%fused_computation.3 | loop fusion | flops 19 | bytes 28 | tf_op jit(solution)/shard_map/reduce_sum | solution.py:91
  8.4 3.3 %collective-permute-start = (f32[1]{0:T(128)}, f32[1]{0:T(128)}, u32[]{:S(2)}, u32[]{:S(2)}) collective-permute-start(f32[1]{0:T(128)} %mul.15), channel_id=1, source_target_pairs={{0,1},{1,0},{2,3},{3,2},{4,5},{5,4},{6,7},{7,6},{8,9},{9,8},{10,11... | collective-permute-start | bytes 20 | tf_op jit(solution)/shard_map/ppermute | solution.py:21
  11.7 0.8 %collective-permute-start.2 = (f32[1]{0:T(128)}, f32[1]{0:T(128)}, u32[]{:S(2)}, u32[]{:S(2)}) collective-permute-start(f32[1]{0:T(128)} %convert_element_type.23), channel_id=1, source_target_pairs={{0,4},{4,0},{8,12},{12,8},{16,20},{20,16},{24,28},{28,24},{1,5},{5... | collective-permute-start | bytes 20 | tf_op jit(solution)/shard_map/ppermute | solution.py:21
  13.6 3.4 %collective-permute-start.3 = (f32[1]{0:T(128)}, f32[1]{0:T(128)}, u32[]{:S(2)}, u32[]{:S(2)}) collective-permute-start(f32[1]{0:T(128)} %add.26), channel_id=1, source_target_pairs={{0,8},{4,12},{8,0},{12,4},{16,24},{20,28},{24,16},{28,20},{1,9},{5... | collective-permute-start | bytes 20 | tf_op jit(solution)/shard_map/ppermute | solution.py:21
  17.6 2.9 %collective-permute-start.1 = (f32[1]{0:T(128)}, f32[1]{0:T(128)}, u32[]{:S(2)}, u32[]{:S(2)}) collective-permute-start(f32[1]{0:T(128)} %add.24), channel_id=1, source_target_pairs={{0,2},{1,3},{2,0},{3,1},{4,6},{5,7},{6,4},{7,5},{8,10},{9,11},{10,... | collective-permute-start | bytes 20 | tf_op jit(solution)/shard_map/ppermute | solution.py:21
  21.3 3.9 %collective-permute-start.4 = (f32[1]{0:T(128)}, f32[1]{0:T(128)}, u32[]{:S(2)}, u32[]{:S(2)}) collective-permute-start(f32[1]{0:T(128)} %add.27), channel_id=1, source_target_pairs={{0,16},{4,20},{8,24},{12,28},{16,0},{20,4},{24,8},{28,12},{1,17},{... | collective-permute-start | bytes 20 | tf_op jit(solution)/shard_map/ppermute | solution.py:21
  25.2 0.5 collective-permute-done.4
  25.7 2.4 %collective-permute-start.10 = (bf16[1,64,512]{2,1,0:T(8,128)(2,1)}, bf16[1,64,512]{2,1,0:T(8,128)(2,1)S(1)}, u32[]{:S(2)}, u32[]{:S(2)}) collective-permute-start(bf16[1,64,512]{2,1,0:T(8,128)(2,1)} %param.15), channel_id=1, source_target_pairs={{0,3},{1,2},{2,1},{3,0},{4,7},{5,6},{6,5},{7,4},{8,11},{9,10},{10,... | collective-permute-start | bytes 196616 | tf_op jit(solution)/shard_map/ppermute | solution.py:21
  28.1 0.5 collective-permute-start.9
  31.4 1.3 %collective-permute-done.9 = bf16[1,64,512]{2,1,0:T(8,128)(2,1)S(1)} collective-permute-done((bf16[1,64,512]{2,1,0:T(8,128)(2,1)}, bf16[1,64,512]{2,1,0:T(8,128)(2,1)S(1)}, u32[]{:S(2)}, u32[]{:S(2)}) %collective-permute-start.9) | collective-permute-done | bytes 65568 | tf_op jit(solution)/shard_map/ppermute | solution.py:21
  32.7 0.6 %copy-done.5 = bf16[1,64,512]{2,1,0:T(8,128)(2,1)} copy-done((bf16[1,64,512]{2,1,0:T(8,128)(2,1)}, bf16[1,64,512]{2,1,0:T(8,128)(2,1)S(1)}, u32[]{:S(2)}) %copy-start.5) | copy-done | bytes 65560
  33.2 10.2 %shard_map.145 = (bf16[256,2048]{1,0:T(8,128)(2,1)}, bf16[256,2048]{1,0:T(8,128)(2,1)}, bf16[256,512]{1,0:T(8,128)(2,1)}, bf16[256,512]{1,0:T(8,128)(2,1)}, bf16[2,256,512]{2,1,0:T(8,128)(2,1)}) custom-call(s32[1]{0:T(128)} %bitcast.3.refs_0_, f32[1]{0:T(128)S(6)} %div.7.refs_1_, bf16[256,2048]{1,0:T(8,128)(2,1)} %bitcast.31, bf16[256,2048]{1,0:T(8,128)(2,1)} %bitcast.32, ...), custom_call_target="tpu_custom_call" | custom-call | tf_op jit(solution)/shard_map/pallas_call | solution.py:104
  43.5 1.1 %fusion.2 = (bf16[2,64,512]{2,1,0:T(8,128)(2,1)S(1)}, bf16[2,64,512]{2,1,0:T(8,128)(2,1)S(1)}, bf16[2,64,512]{2,1,0:T(8,128)(2,1)S(1)}) fusion(bf16[2,256,512]{2,1,0:T(8,128)(2,1)} %get-tuple-element.15), kind=kLoop, calls=%fused_computation.4 | loop fusion | bytes 786432 | tf_op jit(solution)/shard_map/slice | solution.py:122
  44.5 0.7 %collective-permute-start.11 = (bf16[2,64,512]{2,1,0:T(8,128)(2,1)S(1)}, bf16[2,64,512]{2,1,0:T(8,128)(2,1)S(1)}, u32[]{:S(2)}, u32[]{:S(2)}) collective-permute-start(bf16[2,64,512]{2,1,0:T(8,128)(2,1)S(1)} %get-tuple-element.16), channel_id=1, source_target_pairs={{0,1},{1,0},{2,3},{3,2},{4,5},{5,4},{6,7},{7,6},{8,9},{9,8},{10,11... | collective-permute-start | bytes 393224 | tf_op jit(solution)/shard_map/ppermute | solution.py:21
  45.2 1.5 %collective-permute-start.13 = (bf16[2,64,512]{2,1,0:T(8,128)(2,1)S(1)}, bf16[2,64,512]{2,1,0:T(8,128)(2,1)S(1)}, u32[]{:S(2)}, u32[]{:S(2)}) collective-permute-start(bf16[2,64,512]{2,1,0:T(8,128)(2,1)S(1)} %get-tuple-element.17), channel_id=1, source_target_pairs={{0,3},{1,2},{2,1},{3,0},{4,7},{5,6},{6,5},{7,4},{8,11},{9,10},{10,... | collective-permute-start | bytes 393224 | tf_op jit(solution)/shard_map/ppermute | solution.py:21
  46.7 1.4 %collective-permute-start.12 = (bf16[2,64,512]{2,1,0:T(8,128)(2,1)S(1)}, bf16[2,64,512]{2,1,0:T(8,128)(2,1)S(1)}, u32[]{:S(2)}, u32[]{:S(2)}) collective-permute-start(bf16[2,64,512]{2,1,0:T(8,128)(2,1)S(1)} %get-tuple-element.18), channel_id=1, source_target_pairs={{0,2},{1,3},{2,0},{3,1},{4,6},{5,7},{6,4},{7,5},{8,10},{9,11},{10,... | collective-permute-start | bytes 393224 | tf_op jit(solution)/shard_map/ppermute | solution.py:21
  48.1 1.5 %collective-permute-done.11 = bf16[2,64,512]{2,1,0:T(8,128)(2,1)S(1)} collective-permute-done((bf16[2,64,512]{2,1,0:T(8,128)(2,1)S(1)}, bf16[2,64,512]{2,1,0:T(8,128)(2,1)S(1)}, u32[]{:S(2)}, u32[]{:S(2)}) %collective-permute-start.11) | collective-permute-done | bytes 131104 | tf_op jit(solution)/shard_map/ppermute | solution.py:21
  49.6 1.6 %collective-permute-done.13 = bf16[2,64,512]{2,1,0:T(8,128)(2,1)S(1)} collective-permute-done((bf16[2,64,512]{2,1,0:T(8,128)(2,1)S(1)}, bf16[2,64,512]{2,1,0:T(8,128)(2,1)S(1)}, u32[]{:S(2)}, u32[]{:S(2)}) %collective-permute-start.13) | collective-permute-done | bytes 131104 | tf_op jit(solution)/shard_map/ppermute | solution.py:21
  51.2 1.3 %collective-permute-done.12 = bf16[2,64,512]{2,1,0:T(8,128)(2,1)S(1)} collective-permute-done((bf16[2,64,512]{2,1,0:T(8,128)(2,1)S(1)}, bf16[2,64,512]{2,1,0:T(8,128)(2,1)S(1)}, u32[]{:S(2)}, u32[]{:S(2)}) %collective-permute-start.12) | collective-permute-done | bytes 131104 | tf_op jit(solution)/shard_map/ppermute | solution.py:21
  52.5 1.0 %add_convert_fusion = bf16[2,64,512]{2,1,0:T(8,128)(2,1)S(1)} fusion(bf16[2,64,512]{2,1,0:T(8,128)(2,1)S(1)} %collective-permute-done.13, bf16[2,64,512]{2,1,0:T(8,128)(2,1)S(1)} %collective-permute-done.12, bf16[2,64,512]{2,1,0:T(8,128)(2,1)S(1)} %collective-permute-done.11, bf16[2,256,512]{2,1,0:T(8,128)(2,1)} %get-tuple-element.15), kind=kLoop, calls=%fused_computation | loop fusion | flops 524288 | bytes 655360 | tf_op jit(solution)/shard_map/convert_element_type | solution.py:123
  53.5 0.7 %fusion.3 = (bf16[1,64,512]{2,1,0:T(8,128)(2,1)}, bf16[1,64,512]{2,1,0:T(8,128)(2,1)}) fusion(bf16[2,64,512]{2,1,0:T(8,128)(2,1)S(1)} %add_convert_fusion), kind=kLoop, calls=%fused_computation.5 | loop fusion | bytes 262144 | tf_op jit(solution)/shard_map/slice | solution.py:130
  (23 shorter events, 0.7 us)
Async XLA Ops:
  0.6 27.5 %collective-permute-start.5 = (bf16[1,64,512]{2,1,0:T(8,128)(2,1)}, bf16[1,64,512]{2,1,0:T(8,128)(2,1)S(1)}, u32[]{:S(2)}, u32[]{:S(2)}) collective-permute-start(bf16[1,64,512]{2,1,0:T(8,128)(2,1)} %param.14), channel_id=1, source_target_pairs={{0,1},{1,0},{2,3},{3,2},{4,5},{5,4},{6,7},{7,6},{8,9},{9,8},{10,11... | collective-permute-start | bytes 196616 | tf_op jit(solution)/shard_map/ppermute | solution.py:21
  3.6 27.6 %collective-permute-start.7 = (bf16[1,64,512]{2,1,0:T(8,128)(2,1)}, bf16[1,64,512]{2,1,0:T(8,128)(2,1)S(1)}, u32[]{:S(2)}, u32[]{:S(2)}) collective-permute-start(bf16[1,64,512]{2,1,0:T(8,128)(2,1)} %param.14), channel_id=1, source_target_pairs={{0,3},{1,2},{2,1},{3,0},{4,7},{5,6},{6,5},{7,4},{8,11},{9,10},{10,... | collective-permute-start | bytes 196616 | tf_op jit(solution)/shard_map/ppermute | solution.py:21
  5.1 26.2 %collective-permute-start.6 = (bf16[1,64,512]{2,1,0:T(8,128)(2,1)}, bf16[1,64,512]{2,1,0:T(8,128)(2,1)S(1)}, u32[]{:S(2)}, u32[]{:S(2)}) collective-permute-start(bf16[1,64,512]{2,1,0:T(8,128)(2,1)} %param.14), channel_id=1, source_target_pairs={{0,2},{1,3},{2,0},{3,1},{4,6},{5,7},{6,4},{7,5},{8,10},{9,11},{10,... | collective-permute-start | bytes 196616 | tf_op jit(solution)/shard_map/ppermute | solution.py:21
  6.5 0.7 %copy-start.6 = (s32[1,4]{1,0:T(1,128)S(1)}, s32[1,4]{1,0:T(1,128)}, u32[]{:S(2)}) copy-start(s32[1,4]{1,0:T(1,128)} %param.17) | copy-start | bytes 52
  8.4 5.1 %collective-permute-start = (f32[1]{0:T(128)}, f32[1]{0:T(128)}, u32[]{:S(2)}, u32[]{:S(2)}) collective-permute-start(f32[1]{0:T(128)} %mul.15), channel_id=1, source_target_pairs={{0,1},{1,0},{2,3},{3,2},{4,5},{5,4},{6,7},{7,6},{8,9},{9,8},{10,11... | collective-permute-start | bytes 20 | tf_op jit(solution)/shard_map/ppermute | solution.py:21
  11.7 1.1 %collective-permute-start.2 = (f32[1]{0:T(128)}, f32[1]{0:T(128)}, u32[]{:S(2)}, u32[]{:S(2)}) collective-permute-start(f32[1]{0:T(128)} %convert_element_type.23), channel_id=1, source_target_pairs={{0,4},{4,0},{8,12},{12,8},{16,20},{20,16},{24,28},{28,24},{1,5},{5... | collective-permute-start | bytes 20 | tf_op jit(solution)/shard_map/ppermute | solution.py:21
  12.8 18.5 %collective-permute-start.8 = (bf16[1,64,512]{2,1,0:T(8,128)(2,1)}, bf16[1,64,512]{2,1,0:T(8,128)(2,1)S(1)}, u32[]{:S(2)}, u32[]{:S(2)}) collective-permute-start(bf16[1,64,512]{2,1,0:T(8,128)(2,1)} %param.15), channel_id=1, source_target_pairs={{0,1},{1,0},{2,3},{3,2},{4,5},{5,4},{6,7},{7,6},{8,9},{9,8},{10,11... | collective-permute-start | bytes 196616 | tf_op jit(solution)/shard_map/ppermute | solution.py:21
  13.6 4.0 %collective-permute-start.3 = (f32[1]{0:T(128)}, f32[1]{0:T(128)}, u32[]{:S(2)}, u32[]{:S(2)}) collective-permute-start(f32[1]{0:T(128)} %add.26), channel_id=1, source_target_pairs={{0,8},{4,12},{8,0},{12,4},{16,24},{20,28},{24,16},{28,20},{1,9},{5... | collective-permute-start | bytes 20 | tf_op jit(solution)/shard_map/ppermute | solution.py:21
  17.6 3.7 %collective-permute-start.1 = (f32[1]{0:T(128)}, f32[1]{0:T(128)}, u32[]{:S(2)}, u32[]{:S(2)}) collective-permute-start(f32[1]{0:T(128)} %add.24), channel_id=1, source_target_pairs={{0,2},{1,3},{2,0},{3,1},{4,6},{5,7},{6,4},{7,5},{8,10},{9,11},{10,... | collective-permute-start | bytes 20 | tf_op jit(solution)/shard_map/ppermute | solution.py:21
  21.3 4.4 %collective-permute-start.4 = (f32[1]{0:T(128)}, f32[1]{0:T(128)}, u32[]{:S(2)}, u32[]{:S(2)}) collective-permute-start(f32[1]{0:T(128)} %add.27), channel_id=1, source_target_pairs={{0,16},{4,20},{8,24},{12,28},{16,0},{20,4},{24,8},{28,12},{1,17},{... | collective-permute-start | bytes 20 | tf_op jit(solution)/shard_map/ppermute | solution.py:21
  25.7 5.7 %collective-permute-start.10 = (bf16[1,64,512]{2,1,0:T(8,128)(2,1)}, bf16[1,64,512]{2,1,0:T(8,128)(2,1)S(1)}, u32[]{:S(2)}, u32[]{:S(2)}) collective-permute-start(bf16[1,64,512]{2,1,0:T(8,128)(2,1)} %param.15), channel_id=1, source_target_pairs={{0,3},{1,2},{2,1},{3,0},{4,7},{5,6},{6,5},{7,4},{8,11},{9,10},{10,... | collective-permute-start | bytes 196616 | tf_op jit(solution)/shard_map/ppermute | solution.py:21
  28.1 4.5 %copy-start = (bf16[1,64,512]{2,1,0:T(8,128)(2,1)}, bf16[1,64,512]{2,1,0:T(8,128)(2,1)S(1)}, u32[]{:S(2)}) copy-start(bf16[1,64,512]{2,1,0:T(8,128)(2,1)S(1)} %collective-permute-done.5) | copy-start | bytes 196612
  28.1 4.5 %collective-permute-start.9 = (bf16[1,64,512]{2,1,0:T(8,128)(2,1)}, bf16[1,64,512]{2,1,0:T(8,128)(2,1)S(1)}, u32[]{:S(2)}, u32[]{:S(2)}) collective-permute-start(bf16[1,64,512]{2,1,0:T(8,128)(2,1)} %param.15), channel_id=1, source_target_pairs={{0,2},{1,3},{2,0},{3,1},{4,6},{5,7},{6,4},{7,5},{8,10},{9,11},{10,... | collective-permute-start | bytes 196616 | tf_op jit(solution)/shard_map/ppermute | solution.py:21
  31.3 1.3 %copy-start.1 = (bf16[1,64,512]{2,1,0:T(8,128)(2,1)}, bf16[1,64,512]{2,1,0:T(8,128)(2,1)S(1)}, u32[]{:S(2)}) copy-start(bf16[1,64,512]{2,1,0:T(8,128)(2,1)S(1)} %collective-permute-done.7) | copy-start | bytes 196612
  31.3 1.3 %copy-start.2 = (bf16[1,64,512]{2,1,0:T(8,128)(2,1)}, bf16[1,64,512]{2,1,0:T(8,128)(2,1)S(1)}, u32[]{:S(2)}) copy-start(bf16[1,64,512]{2,1,0:T(8,128)(2,1)S(1)} %collective-permute-done.6) | copy-start | bytes 196612
  31.3 1.3 %copy-start.3 = (bf16[1,64,512]{2,1,0:T(8,128)(2,1)}, bf16[1,64,512]{2,1,0:T(8,128)(2,1)S(1)}, u32[]{:S(2)}) copy-start(bf16[1,64,512]{2,1,0:T(8,128)(2,1)S(1)} %collective-permute-done.8) | copy-start | bytes 196612
  31.3 1.3 %copy-start.4 = (bf16[1,64,512]{2,1,0:T(8,128)(2,1)}, bf16[1,64,512]{2,1,0:T(8,128)(2,1)S(1)}, u32[]{:S(2)}) copy-start(bf16[1,64,512]{2,1,0:T(8,128)(2,1)S(1)} %collective-permute-done.10) | copy-start | bytes 196612
  32.6 0.6 %copy-start.5 = (bf16[1,64,512]{2,1,0:T(8,128)(2,1)}, bf16[1,64,512]{2,1,0:T(8,128)(2,1)S(1)}, u32[]{:S(2)}) copy-start(bf16[1,64,512]{2,1,0:T(8,128)(2,1)S(1)} %collective-permute-done.9) | copy-start | bytes 196612
  44.5 5.0 %collective-permute-start.11 = (bf16[2,64,512]{2,1,0:T(8,128)(2,1)S(1)}, bf16[2,64,512]{2,1,0:T(8,128)(2,1)S(1)}, u32[]{:S(2)}, u32[]{:S(2)}) collective-permute-start(bf16[2,64,512]{2,1,0:T(8,128)(2,1)S(1)} %get-tuple-element.16), channel_id=1, source_target_pairs={{0,1},{1,0},{2,3},{3,2},{4,5},{5,4},{6,7},{7,6},{8,9},{9,8},{10,11... | collective-permute-start | bytes 393224 | tf_op jit(solution)/shard_map/ppermute | solution.py:21
  45.2 6.0 %collective-permute-start.13 = (bf16[2,64,512]{2,1,0:T(8,128)(2,1)S(1)}, bf16[2,64,512]{2,1,0:T(8,128)(2,1)S(1)}, u32[]{:S(2)}, u32[]{:S(2)}) collective-permute-start(bf16[2,64,512]{2,1,0:T(8,128)(2,1)S(1)} %get-tuple-element.17), channel_id=1, source_target_pairs={{0,3},{1,2},{2,1},{3,0},{4,7},{5,6},{6,5},{7,4},{8,11},{9,10},{10,... | collective-permute-start | bytes 393224 | tf_op jit(solution)/shard_map/ppermute | solution.py:21
  46.7 5.8 %collective-permute-start.12 = (bf16[2,64,512]{2,1,0:T(8,128)(2,1)S(1)}, bf16[2,64,512]{2,1,0:T(8,128)(2,1)S(1)}, u32[]{:S(2)}, u32[]{:S(2)}) collective-permute-start(bf16[2,64,512]{2,1,0:T(8,128)(2,1)S(1)} %get-tuple-element.18), channel_id=1, source_target_pairs={{0,2},{1,3},{2,0},{3,1},{4,6},{5,7},{6,4},{7,5},{8,10},{9,11},{10,... | collective-permute-start | bytes 393224 | tf_op jit(solution)/shard_map/ppermute | solution.py:21

commit v2 on v1

v2 whole, which is shorter than its diff:
```python
import functools
import jax
import jax.numpy as jnp
from jax import lax
from jax.experimental import pallas as pl
from jax.experimental.pallas import tpu as pltpu
from jax.sharding import PartitionSpec as P

HEAD_SIZE = 128
BLOCK = 128
EXTRA = 16
SCALING = HEAD_SIZE**-0.5
POWER = SCALING * 1.4426950408889634
f32 = jnp.float32
bf16 = jnp.bfloat16


def dot(a, b, ca, cb):
    return lax.dot_general(a, b, (((ca,), (cb,)), ((), ())), preferred_element_type=f32)


def swap(x, n, k):
    return lax.ppermute(x, "resp", [(i, i ^ k) for i in range(n)])


def stack(ref, group):
    return jnp.concatenate([ref[:, h * HEAD_SIZE : (h + 1) * HEAD_SIZE] for h in range(group)], 0)


def unstack(ref, x, group):
    tokens = ref.shape[0]
    for h in range(group):
        ref[:, h * HEAD_SIZE : (h + 1) * HEAD_SIZE] = x[h * tokens : (h + 1) * tokens]


def causal_mask(tokens, group):
    row = lax.broadcasted_iota(jnp.int32, (tokens, tokens), 0)
    col = lax.broadcasted_iota(jnp.int32, (tokens, tokens), 1)
    return jnp.concatenate([col <= row] * group, 0)


def survives(spaces_ref, kept_ref, member):
    hits = [
        jnp.where((i < kept_ref[0]) & (spaces_ref[0, i] == member), 1, 0)
        for i in range(spaces_ref.shape[1])
    ]
    return sum(hits)


def valid_rows(spaces_ref, kept_ref, spans_ref, member, tokens, group):
    length = survives(spaces_ref, kept_ref, member) * spans_ref[0, 0] * BLOCK
    row = lax.broadcasted_iota(jnp.int32, (tokens, 1), 0)
    return jnp.concatenate([row < length] * group, 0)


def own_kernel(group, counts, *refs):
    count_refs, (q_ref, ko_ref, vo_ref, att_ref, stat_ref, part_ref) = refs[:counts], refs[counts:]
    part_ref[0] = sum(r[0] for r in count_refs)
    tokens = q_ref.shape[0]
    s = dot(stack(q_ref, group), ko_ref[...], 1, 1)
    s = jnp.where(causal_mask(tokens, group), s, -1e30)
    top = jnp.max(s, -1, keepdims=True)
    e = jnp.exp2((s - top) * POWER)
    stat_ref[0, :, 0:1] = top
    stat_ref[0, :, 1:2] = jnp.sum(e, -1, keepdims=True)
    att_ref[0] = dot(e.astype(bf16), vo_ref[...], 1, 0)


def prefix_kernel(n, group, *refs):
    (place_ref, kept_ref, spaces_ref, spans_ref, payoff_ref, part_ref, recv_ref) = refs[:7]
    q_ref, u_ref, own_ref, stat_ref = refs[7:11]
    kp_refs, vp_refs = refs[11 : 11 + n], refs[11 + n : 11 + 2 * n]
    pay_refs = refs[11 + 2 * n : 10 + 3 * n]
    out_ref, ds_ref, line_ref, weight_ref, sum_ref = refs[10 + 3 * n : 15 + 3 * n]
    term_refs = refs[15 + 3 * n :]
    tokens = q_ref.shape[0]
    part = kp_refs[0].shape[0]
    member = place_ref[0]
    sum_ref[0] = part_ref[0] + recv_ref[0]

    total = jnp.where(survives(spaces_ref, kept_ref, member) > 0, payoff_ref[0, 0], 0.0)
    total = jnp.full((1, 1), total, f32)
    for k in range(1, n):
        pieces = pay_refs[k - 1][...].astype(f32)
        reward = pieces[0:1, 0:1] + pieces[1:2, 0:1] + pieces[2:3, 0:1]
        total += jnp.where(survives(spaces_ref, kept_ref, member ^ k) > 0, reward, 0.0)
    weight = payoff_ref[0, 0] - total / kept_ref[0].astype(f32)
    weight_ref[...] = jnp.broadcast_to(weight, weight_ref.shape)

    keys = jnp.concatenate([r[...] for r in kp_refs], 0)
    values = jnp.concatenate([r[...] for r in vp_refs], 0)
    valid = valid_rows(spaces_ref, kept_ref, spans_ref, member, tokens, group)
    q = stack(q_ref, group)
    u = jnp.where(valid, stack(u_ref, group), 0.0)
    s = dot(q, keys, 1, 1)
    own_top = stat_ref[0, :, 0:1]
    top = jnp.maximum(jnp.max(s, -1, keepdims=True), own_top)
    e = jnp.exp2((s - top) * POWER)
    shrink = jnp.exp2((own_top - top) * POWER)
    mass = jnp.sum(e, -1, keepdims=True) + shrink * stat_ref[0, :, 1:2]
    inverse = 1.0 / mass
    p = e * inverse
    p_low = p.astype(bf16)
    attended = dot(p_low, values, 1, 0) + own_ref[0] * (shrink * inverse)
    unstack(out_ref, jnp.where(valid, attended, 0.0).astype(bf16), group)
    dp = dot(u, values, 1, 1)
    delta = jnp.sum(u.astype(f32) * attended, -1, keepdims=True)
    ds = (p * (dp - delta)).astype(bf16)
    ds_ref[0] = ds
    line_ref[0, :, 0:1] = top * POWER + jnp.log2(mass)
    line_ref[0, :, 1:2] = delta
    dk = dot(q, ds, 0, 0).T * (weight * SCALING)
    dv = dot(u, p_low, 0, 0).T * weight
    for k, ref in enumerate(term_refs):
        ref[0] = dk[k * part : (k + 1) * part].astype(ref.dtype)
        ref[1] = dv[k * part : (k + 1) * part].astype(ref.dtype)


def rest_kernel(n, group, *refs):
    (place_ref, kept_ref, spaces_ref, spans_ref, sum_ref, recv_ref) = refs[:6]
    weight_ref, q_ref, u_ref, ko_ref, vo_ref, ds_ref, line_ref = refs[6:13]
    kp_refs = refs[13 : 13 + n]
    dq_ref, dko_ref, dvo_ref = refs[13 + n :]
    tokens = q_ref.shape[0]
    batch = (sum_ref[0] + recv_ref[0]).astype(f32)
    weight = weight_ref[0:1, 0:1] / batch
    keys = jnp.concatenate([r[...] for r in kp_refs], 0)
    valid = valid_rows(spaces_ref, kept_ref, spans_ref, place_ref[0], tokens, group)
    q = stack(q_ref, group)
    u = jnp.where(valid, stack(u_ref, group), 0.0)
    s = dot(q, ko_ref[...], 1, 1)
    s = jnp.where(causal_mask(tokens, group), s, -1e30)
    p = jnp.exp2(s * POWER - line_ref[0, :, 0:1])
    dp = dot(u, vo_ref[...], 1, 1)
    ds = (p * (dp - line_ref[0, :, 1:2])).astype(bf16)
    dq = dot(ds_ref[0], keys, 1, 0) + dot(ds, ko_ref[...], 1, 0)
    unstack(dq_ref, (dq * (weight * SCALING)).astype(bf16), group)
    dko_ref[...] = (dot(q, ds, 0, 0).T * (weight * SCALING)).astype(bf16)
    dvo_ref[...] = (dot(u, p.astype(bf16), 0, 0).T * weight).astype(bf16)


def local(q, ko, vo, u, kp, vp, kept, spaces, spans, payoffs):
    n = lax.axis_size("resp")
    n_prompt = lax.axis_size("prompt")
    tokens = q.shape[2]
    kv_width = ko.shape[3]
    kv_heads = kv_width // HEAD_SIZE
    group = q.shape[3] // kv_width
    width = group * HEAD_SIZE
    rows = group * tokens
    part = kp.shape[1]
    prefix = n * part
    q, ko, vo, u = q[0, 0], ko[0, 0], vo[0, 0], u[0, 0]
    place = lax.axis_index("resp").astype(jnp.int32).reshape(1)

    high = payoffs.astype(bf16)
    middle = (payoffs - high.astype(f32)).astype(bf16)
    low = (payoffs - high.astype(f32) - middle.astype(f32)).astype(bf16)
    pieces = jnp.concatenate([high, middle, low, jnp.zeros((EXTRA - 3, 1), bf16)], 0)
    payload = jnp.concatenate([kp[0], vp[0], jnp.broadcast_to(pieces, (EXTRA, kv_width))], 0)
    arrived = [swap(payload, n, k) for k in range(1, n)]

    share = -(-n_prompt // n)
    counts = []
    for a in range(share):
        perm = [
            (p * n + m, (p ^ (m * share + a)) * n + m)
            for p in range(n_prompt)
            for m in range(n)
            if m * share + a < n_prompt
        ]
        counts.append(lax.ppermute(kept, ("prompt", "resp"), perm))

    scalar = pl.BlockSpec(memory_space=pltpu.SMEM)
    one = jax.ShapeDtypeStruct((1,), jnp.int32)

    def columns(height, width, at=0):
        return pl.BlockSpec((height, width), lambda g: (at, g))

    def head(height, width):
        return pl.BlockSpec((1, height, width), lambda g: (g, 0, 0))

    def call(kernel, units, in_specs, out, args):
        return pl.pallas_call(
            kernel,
            grid=(kv_heads,),
            in_specs=in_specs,
            out_specs=[spec for spec, _ in out],
            out_shape=[shape for _, shape in out],
            compiler_params=pltpu.CompilerParams(vmem_limit_bytes=48 << 20),
            cost_estimate=pl.CostEstimate(
                flops=units * 2 * kv_heads * rows * tokens * HEAD_SIZE,
                bytes_accessed=4 << 20,
                transcendentals=kv_heads * rows * tokens,
            ),
        )(*args)

    def shaped(shape, kind):
        return jax.ShapeDtypeStruct(shape, kind)

    stat = (head(rows, 2), shaped((kv_heads, rows, 2), f32))
    wide, slim = columns(tokens, width), columns(tokens, HEAD_SIZE)

    own, own_stat, part_sum = call(
        functools.partial(own_kernel, group, share),
        2,
        [scalar] * share + [wide, slim, slim],
        [(head(rows, HEAD_SIZE), shaped((kv_heads, rows, HEAD_SIZE), f32)), stat, (scalar, one)],
        (*counts, q, ko, vo),
    )
    k = 1
    while 4 * k < n:
        part_sum = part_sum + swap(part_sum, n, k)
        k *= 2
    key_specs = [columns(part, HEAD_SIZE)] * n
    keys = [kp[0]] + arrived
    attn_out, ds, line, weight, batch, *terms = call(
        functools.partial(prefix_kernel, n, group),
        5,
        [scalar] * 7
        + [wide, wide, head(rows, HEAD_SIZE), head(rows, 2)]
        + key_specs
        + [columns(part, HEAD_SIZE)]
        + [columns(part, HEAD_SIZE, 1)] * (n - 1)
        + [pl.BlockSpec((EXTRA, HEAD_SIZE), lambda g: (2 * part // EXTRA, 0))] * (n - 1),
        [
            (wide, shaped(q.shape, bf16)),
            (head(rows, prefix), shaped((kv_heads, rows, prefix), bf16)),
            stat,
            (pl.BlockSpec((8, HEAD_SIZE), lambda g: (0, 0)), shaped((8, HEAD_SIZE), f32)),
            (scalar, one),
        ]
        + [
            (
                pl.BlockSpec((2, part, HEAD_SIZE), lambda g: (0, 0, g)),
                shaped((2, part, kv_width), f32 if i == 0 else bf16),
            )
            for i in range(n)
        ],
        (place, kept, spaces, spans, payoffs, part_sum, swap(part_sum, n, k))
        + (q, u, own, own_stat, *keys, vp[0], *arrived, *arrived),
    )
    other = swap(batch, n, 2 * k)
    received = [swap(t, n, i) for i, t in enumerate(terms) if i > 0]
    dq, dko, dvo = call(
        functools.partial(rest_kernel, n, group),
        6,
        [scalar] * 6
        + [pl.BlockSpec((8, HEAD_SIZE), lambda g: (0, 0))]
        + [wide, wide, slim, slim, head(rows, prefix), head(rows, 2)]
        + key_specs,
        [(wide, shaped(q.shape, bf16))] + [(slim, shaped(ko.shape, bf16))] * 2,
        (place, kept, spaces, spans, batch, other, weight, q, u, ko, vo, ds, line, *keys),
    )
    total = terms[0]
    for t in received:
        total += t.astype(f32)
    total = (total / (batch + other).astype(f32)).astype(bf16)
    return (
        attn_out[None, None],
        dq[None, None],
        dko[None, None],
        dvo[None, None],
        total[:1],
        total[1:],
    )


def solution(mesh):
    wide = P("prompt", "resp", None, None)
    rows = P("prompt", "resp", None)
    pair = P("prompt", "resp")
    return jax.shard_map(
        local,
        mesh=mesh,
        in_specs=(wide, wide, wide, wide, rows, rows, P("prompt"), P("prompt", None), pair, pair),
        out_specs=(wide, wide, wide, wide, rows, rows),
        check_vma=False,
    )
```

time: 54.4 us -> 66.3 us (1.22)
  Pallas kernels: 10.2 us -> 30.5 us
  waiting for transfers between devices: 6.68 us -> 1.7 us
  local copies, waits for them, and re-layouts: 2.98 us -> 7.69 us
  starting transfers between devices: 25.4 us -> 20.7 us
  between operations: 7.24 us -> 4.06 us
    pallas_call x1 -> x3, Pallas kernels: 10.2 us -> 30.5 us  [call(): pl.pallas_call(kernel, grid=(kv_heads,), in_specs=in_specs, out_specs=[sp...]
    unnamed x14 -> x24, local copies, waits for them, and re-layouts: 1.25 us -> 7.02 us
    ppermute x14 -> x10, waiting for transfers between devices: 6.68 us -> 1.7 us  [the longest x8 1.62 us: swap(): return lax.ppermute(x, 'resp', [(i, i ^ k) for i in range(n)])]
    ppermute x14 -> x10, starting transfers between devices: 25.4 us -> 20.7 us  [the longest x8 18.8 us: swap(): return lax.ppermute(x, 'resp', [(i, i ^ k) for i in range(n)])]
    slice x1 -> x0, local copies, waits for them, and re-layouts: 1.07 us -> none  [local(): total += swap(terms[:, k * part:(k + 1) * part], 'resp', n, k).astype(f32)]
    concatenate x0 -> x1, other arithmetic: none -> 0.96 us  [local(): jnp.concatenate([kp[0], vp[0], jnp.broadcast_to(pieces, (EXTRA, kv_width)...]
    convert_element_type x1, other arithmetic: 0.97 us -> 0.08 us  [local(): total = (total / (batch + other).astype(f32)).astype(bf16)]
  transfers between devices with their start and end apart: 14 -> 10, of which waited for: 7 -> 2; matrix products, arithmetic and copies ran while one was open for 1% -> 0% of each run, Pallas kernels for 0% -> 18%
where the time goes in v2:
time: 66.3 us; the launch traced here: 65.8 us
  Pallas kernels  30.5 us (46%)
  starting transfers between devices  20.7 us (31%)
  local copies, waits for them, and re-layouts  7.69 us (12%)
  between operations  4.06 us (6%)
  waiting for transfers between devices  1.7 us (3%)
  other arithmetic  1.12 us (2%)
    pallas_call x3, Pallas kernels, call(): pl.pallas_call(kernel, grid=(kv_heads,), in_specs=in_specs, out_specs=[sp...  30.5 us
    ppermute x8, starting transfers between devices, swap(): return lax.ppermute(x, 'resp', [(i, i ^ k) for i in range(n)])  18.8 us
    unnamed x24, local copies, waits for them, and re-layouts  7.02 us
    ppermute x2, starting transfers between devices, local(): counts.append(lax.ppermute(kept, ('prompt', 'resp'), perm))  1.9 us
    ppermute x8, waiting for transfers between devices, swap(): return lax.ppermute(x, 'resp', [(i, i ^ k) for i in range(n)])  1.62 us
  transfers between devices with their start and end apart: 10, of which 2 were waited for; matrix products, arithmetic and copies ran while one was open for 0% of the time, Pallas kernels for 18%

profile of v2, /device:TPU:0, one launch (start us, length us, event | category | flops | bytes accessed | tf_op | source)
XLA Modules:
  0.0 65.8 jit_solution(15327472958451347957)
XLA Ops:
  1.4 0.1 fusion
  1.5 1.0 %maximum_maximum_fusion = bf16[144,512]{1,0:T(8,128)(2,1)S(1)} fusion(bf16[64,512]{1,0:T(8,128)(2,1)} %bitcast.29, bf16[64,512]{1,0:T(8,128)(2,1)} %bitcast.26, bf16[144]{0:T(256)(128)(2,1)S(1)} %pad.2.clone), kind=kLoop, calls=%fused_computation.1 | loop fusion | flops 442368 | bytes 278816 | tf_op jit(solution)/shard_map/concatenate | solution.py:160
  2.4 4.0 %collective-permute-start.5 = (bf16[144,512]{1,0:T(8,128)(2,1)S(1)}, bf16[144,512]{1,0:T(8,128)(2,1)S(1)}, u32[]{:S(2)}, u32[]{:S(2)}) collective-permute-start(bf16[144,512]{1,0:T(8,128)(2,1)S(1)} %maximum_maximum_fusion), channel_id=1, source_target_pairs={{0,3},{1,2},{2,1},{3,0},{4,7},{5,6},{6,5},{7,4},{8,11},{9,10},{10,... | collective-permute-start | bytes 442376 | tf_op jit(solution)/shard_map/ppermute | solution.py:23
  6.4 0.5 collective-permute-start.4
  6.9 0.1 collective-permute-start.3
  7.0 1.9 %collective-permute-start = (s32[1]{0:T(128)}, s32[1]{0:T(128)}, u32[]{:S(2)}, u32[]{:S(2)}) collective-permute-start(s32[1]{0:T(128)} %param.16), channel_id=1, source_target_pairs={{0,0},{1,9},{2,18},{3,27},{4,4},{5,13},{6,22},{7,31},{8,8},{9,1},{... | collective-permute-start | bytes 20 | tf_op jit(solution)/shard_map/ppermute | solution.py:172
  10.2 0.1 collective-permute-done.1.refs_1_
  10.3 1.2 %copy-done = bf16[1,1,256,2048]{3,2,1,0:T(8,128)(2,1)S(1)} copy-done((bf16[1,1,256,2048]{3,2,1,0:T(8,128)(2,1)S(1)}, bf16[1,1,256,2048]{3,2,1,0:T(8,128)(2,1)}, u32[]{:S(2)}) %copy-start) | copy-done | bytes 1048600
  11.6 0.9 %copy-done.7 = bf16[1,1,256,512]{3,2,1,0:T(8,128)(2,1)S(1)} copy-done((bf16[1,1,256,512]{3,2,1,0:T(8,128)(2,1)S(1)}, bf16[1,1,256,512]{3,2,1,0:T(8,128)(2,1)}, u32[]{:S(2)}) %copy-start.7) | copy-done | bytes 262168
  12.5 0.9 %copy-done.9 = bf16[1,1,256,512]{3,2,1,0:T(8,128)(2,1)S(1)} copy-done((bf16[1,1,256,512]{3,2,1,0:T(8,128)(2,1)S(1)}, bf16[1,1,256,512]{3,2,1,0:T(8,128)(2,1)}, u32[]{:S(2)}) %copy-start.9) | copy-done | bytes 262168
  13.5 4.2 %shard_map.145 = (f32[4,1024,128]{2,1,0:T(8,128)S(1)}, f32[4,1024,2]{2,1,0:T(8,128)S(1)}, s32[1]{0:T(128)}) custom-call(s32[1]{0:T(128)} %collective-permute-done.refs_0_, s32[1]{0:T(128)} %collective-permute-done.1.refs_1_, bf16[256,2048]{1,0:T(8,128)(2,1)S(1)} %bitcast.21, bf16[256,512]{1,0:T(8,128)(2,1)S(1)} %bitcast.31, bf16[256,512]{1,0:T(8,128)(2,1)S(1)} %bitcast.33), custom_call_target="tpu_custom_call" | custom-call | flops 536870912 | bytes 4194304 | tf_op jit(solution)/shard_map/pallas_call | solution.py:184
  17.6 1.3 %copy-done.3 = f32[4,1024,128]{2,1,0:T(8,128)} copy-done((f32[4,1024,128]{2,1,0:T(8,128)}, f32[4,1024,128]{2,1,0:T(8,128)S(1)}, u32[]{:S(2)}) %copy-start.3) | copy-done | bytes 2097176
  18.9 1.3 %copy-done.4 = f32[4,1024,2]{2,1,0:T(8,128)} copy-done((f32[4,1024,2]{2,1,0:T(8,128)}, f32[4,1024,2]{2,1,0:T(8,128)S(1)}, u32[]{:S(2)}) %copy-start.4) | copy-done | bytes 32792
  20.3 5.4 %collective-permute-start.2 = (s32[1]{0:T(128)}, s32[1]{0:T(128)}, u32[]{:S(2)}, u32[]{:S(2)}) collective-permute-start(s32[1]{0:T(128)} %get-tuple-element.21.refs_5_), channel_id=1, source_target_pairs={{0,1},{1,0},{2,3},{3,2},{4,5},{5,4},{6,7},{7,6},{8,9},{9,8},{10,11... | collective-permute-start | bytes 20 | tf_op jit(solution)/shard_map/ppermute | solution.py:23
  25.6 1.6 %collective-permute-done.2.refs_6_ = s32[1]{0:T(128)} collective-permute-done((s32[1]{0:T(128)}, s32[1]{0:T(128)}, u32[]{:S(2)}, u32[]{:S(2)}) %collective-permute-start.2) | collective-permute-done | bytes 36 | tf_op jit(solution)/shard_map/ppermute | solution.py:23
  27.3 1.2 %copy-done.2 = bf16[1,1,256,2048]{3,2,1,0:T(8,128)(2,1)S(1)} copy-done((bf16[1,1,256,2048]{3,2,1,0:T(8,128)(2,1)S(1)}, bf16[1,1,256,2048]{3,2,1,0:T(8,128)(2,1)}, u32[]{:S(2)}) %copy-start.2) | copy-done | bytes 1048600
  28.5 18.9 %shard_map.146 = (bf16[256,2048]{1,0:T(8,128)(2,1)}, bf16[4,1024,256]{2,1,0:T(8,128)(2,1)S(1)}, f32[4,1024,2]{2,1,0:T(8,128)}, f32[8,128]{1,0:T(8,128)S(1)}, s32...) custom-call(s32[1]{0:T(128)} %bitcast.refs_0_, ...), custom_call_target="tpu_custom_call" | custom-call | flops 1342177280 | bytes 4194304 | tf_op jit(solution)/shard_map/pallas_call | solution.py:184
  47.4 5.3 %collective-permute-start.6 = (s32[1]{0:T(128)}, s32[1]{0:T(128)}, u32[]{:S(2)}, u32[]{:S(2)}) collective-permute-start(s32[1]{0:T(128)} %get-tuple-element.25.refs_4_), channel_id=1, source_target_pairs={{0,2},{1,3},{2,0},{3,1},{4,6},{5,7},{6,4},{7,5},{8,10},{9,11},{10,... | collective-permute-start | bytes 20 | tf_op jit(solution)/shard_map/ppermute | solution.py:23
  52.7 2.0 %collective-permute-start.7 = (bf16[2,64,512]{2,1,0:T(8,128)(2,1)S(1)}, bf16[2,64,512]{2,1,0:T(8,128)(2,1)S(1)}, u32[]{:S(2)}, u32[]{:S(2)}) collective-permute-start(bf16[2,64,512]{2,1,0:T(8,128)(2,1)S(1)} %get-tuple-element.33), channel_id=1, source_target_pairs={{0,1},{1,0},{2,3},{3,2},{4,5},{5,4},{6,7},{7,6},{8,9},{9,8},{10,11... | collective-permute-start | bytes 393224 | tf_op jit(solution)/shard_map/ppermute | solution.py:23
  54.8 0.1 collective-permute-start.8
  54.8 1.4 %collective-permute-start.9 = (bf16[2,64,512]{2,1,0:T(8,128)(2,1)S(1)}, bf16[2,64,512]{2,1,0:T(8,128)(2,1)S(1)}, u32[]{:S(2)}, u32[]{:S(2)}) collective-permute-start(bf16[2,64,512]{2,1,0:T(8,128)(2,1)S(1)} %get-tuple-element.35), channel_id=1, source_target_pairs={{0,3},{1,2},{2,1},{3,0},{4,7},{5,6},{6,5},{7,4},{8,11},{9,10},{10,... | collective-permute-start | bytes 393224 | tf_op jit(solution)/shard_map/ppermute | solution.py:23
  57.5 7.5 %shard_map.147 = (bf16[256,2048]{1,0:T(8,128)(2,1)}, bf16[256,512]{1,0:T(8,128)(2,1)}, bf16[256,512]{1,0:T(8,128)(2,1)}) custom-call(s32[1]{0:T(128)} %bitcast.refs_0_, s32[1]{0:T(128)S(6)} %copy.19.refs_1_, s32[1,4]{1,0:T(1,128)S(1)} %copy-done.11, s32[1,1]{1,0:T(1,128)S(6)} %copy.20.refs_3_, s32[1]{0:T(128)} %get-tuple-element.25.refs_4_, ...), custom_call_target="tpu_custom_call" | custom-call | flops 1610612736 | bytes 4194304 | tf_op jit(solution)/shard_map/pallas_call | solution.py:184
  65.0 0.1 divide_convert_fusion
  65.1 0.7 %fusion.1 = (bf16[1,64,512]{2,1,0:T(8,128)(2,1)}, bf16[1,64,512]{2,1,0:T(8,128)(2,1)}) fusion(bf16[2,64,512]{2,1,0:T(8,128)(2,1)S(1)} %divide_convert_fusion), kind=kLoop, calls=%fused_computation.4 | loop fusion | bytes 262144 | tf_op jit(solution)/shard_map/slice | solution.py:265
  (29 shorter events, 0.1 us)
Async XLA Ops:
  0.6 26.6 %copy-start.6 = (bf16[1,64,512]{2,1,0:T(8,128)(2,1)S(1)}, bf16[1,64,512]{2,1,0:T(8,128)(2,1)}, u32[]{:S(2)}) copy-start(bf16[1,64,512]{2,1,0:T(8,128)(2,1)} %param.15) | copy-start | bytes 196612
  0.6 26.6 %copy-start.5 = (bf16[1,64,512]{2,1,0:T(8,128)(2,1)S(1)}, bf16[1,64,512]{2,1,0:T(8,128)(2,1)}, u32[]{:S(2)}) copy-start(bf16[1,64,512]{2,1,0:T(8,128)(2,1)} %param.14) | copy-start | bytes 196612
  0.7 26.6 %copy-start.11 = (s32[1,4]{1,0:T(1,128)S(1)}, s32[1,4]{1,0:T(1,128)}, u32[]{:S(2)}) copy-start(s32[1,4]{1,0:T(1,128)} %refs_2_.3) | copy-start | bytes 52
  2.4 24.8 %collective-permute-start.5 = (bf16[144,512]{1,0:T(8,128)(2,1)S(1)}, bf16[144,512]{1,0:T(8,128)(2,1)S(1)}, u32[]{:S(2)}, u32[]{:S(2)}) collective-permute-start(bf16[144,512]{1,0:T(8,128)(2,1)S(1)} %maximum_maximum_fusion), channel_id=1, source_target_pairs={{0,3},{1,2},{2,1},{3,0},{4,7},{5,6},{6,5},{7,4},{8,11},{9,10},{10,... | collective-permute-start | bytes 442376 | tf_op jit(solution)/shard_map/ppermute | solution.py:23
  6.4 20.8 %collective-permute-start.4 = (bf16[144,512]{1,0:T(8,128)(2,1)S(1)}, bf16[144,512]{1,0:T(8,128)(2,1)S(1)}, u32[]{:S(2)}, u32[]{:S(2)}) collective-permute-start(bf16[144,512]{1,0:T(8,128)(2,1)S(1)} %maximum_maximum_fusion), channel_id=1, source_target_pairs={{0,2},{1,3},{2,0},{3,1},{4,6},{5,7},{6,4},{7,5},{8,10},{9,11},{10,... | collective-permute-start | bytes 442376 | tf_op jit(solution)/shard_map/ppermute | solution.py:23
  6.9 20.3 %collective-permute-start.3 = (bf16[144,512]{1,0:T(8,128)(2,1)S(1)}, bf16[144,512]{1,0:T(8,128)(2,1)S(1)}, u32[]{:S(2)}, u32[]{:S(2)}) collective-permute-start(bf16[144,512]{1,0:T(8,128)(2,1)S(1)} %maximum_maximum_fusion), channel_id=1, source_target_pairs={{0,1},{1,0},{2,3},{3,2},{4,5},{5,4},{6,7},{7,6},{8,9},{9,8},{10,11... | collective-permute-start | bytes 442376 | tf_op jit(solution)/shard_map/ppermute | solution.py:23
  7.0 3.2 %collective-permute-start = (s32[1]{0:T(128)}, s32[1]{0:T(128)}, u32[]{:S(2)}, u32[]{:S(2)}) collective-permute-start(s32[1]{0:T(128)} %param.16), channel_id=1, source_target_pairs={{0,0},{1,9},{2,18},{3,27},{4,4},{5,13},{6,22},{7,31},{8,8},{9,1},{... | collective-permute-start | bytes 20 | tf_op jit(solution)/shard_map/ppermute | solution.py:172
  8.9 1.4 %collective-permute-start.1 = (s32[1]{0:T(128)}, s32[1]{0:T(128)}, u32[]{:S(2)}, u32[]{:S(2)}) collective-permute-start(s32[1]{0:T(128)} %param.16), channel_id=1, source_target_pairs={{0,4},{1,13},{2,22},{3,31},{4,0},{5,9},{6,18},{7,27},{8,12},{9,5},... | collective-permute-start | bytes 20 | tf_op jit(solution)/shard_map/ppermute | solution.py:172
  10.3 1.2 %copy-start = (bf16[1,1,256,2048]{3,2,1,0:T(8,128)(2,1)S(1)}, bf16[1,1,256,2048]{3,2,1,0:T(8,128)(2,1)}, u32[]{:S(2)}) copy-start(bf16[1,1,256,2048]{3,2,1,0:T(8,128)(2,1)} %param.10) | copy-start | bytes 3145732
  11.5 0.9 %copy-start.7 = (bf16[1,1,256,512]{3,2,1,0:T(8,128)(2,1)S(1)}, bf16[1,1,256,512]{3,2,1,0:T(8,128)(2,1)}, u32[]{:S(2)}) copy-start(bf16[1,1,256,512]{3,2,1,0:T(8,128)(2,1)} %param.11) | copy-start | bytes 786436
  12.5 0.9 %copy-start.9 = (bf16[1,1,256,512]{3,2,1,0:T(8,128)(2,1)S(1)}, bf16[1,1,256,512]{3,2,1,0:T(8,128)(2,1)}, u32[]{:S(2)}) copy-start(bf16[1,1,256,512]{3,2,1,0:T(8,128)(2,1)} %param.12) | copy-start | bytes 786436
  13.4 13.8 %copy-start.1 = (bf16[1,1,256,2048]{3,2,1,0:T(8,128)(2,1)S(1)}, bf16[1,1,256,2048]{3,2,1,0:T(8,128)(2,1)}, u32[]{:S(2)}) copy-start(bf16[1,1,256,2048]{3,2,1,0:T(8,128)(2,1)} %param.10) | copy-start | bytes 3145732
  17.6 1.3 %copy-start.3 = (f32[4,1024,128]{2,1,0:T(8,128)}, f32[4,1024,128]{2,1,0:T(8,128)S(1)}, u32[]{:S(2)}) copy-start(f32[4,1024,128]{2,1,0:T(8,128)S(1)} %get-tuple-element.22.refs_9_) | copy-start | bytes 6291460
  18.9 1.3 %copy-start.4 = (f32[4,1024,2]{2,1,0:T(8,128)}, f32[4,1024,2]{2,1,0:T(8,128)S(1)}, u32[]{:S(2)}) copy-start(f32[4,1024,2]{2,1,0:T(8,128)S(1)} %get-tuple-element.23.refs_10_) | copy-start | bytes 98308
  20.3 7.0 %collective-permute-start.2 = (s32[1]{0:T(128)}, s32[1]{0:T(128)}, u32[]{:S(2)}, u32[]{:S(2)}) collective-permute-start(s32[1]{0:T(128)} %get-tuple-element.21.refs_5_), channel_id=1, source_target_pairs={{0,1},{1,0},{2,3},{3,2},{4,5},{5,4},{6,7},{7,6},{8,9},{9,8},{10,11... | collective-permute-start | bytes 20 | tf_op jit(solution)/shard_map/ppermute | solution.py:23
  27.3 1.2 %copy-start.2 = (bf16[1,1,256,2048]{3,2,1,0:T(8,128)(2,1)S(1)}, bf16[1,1,256,2048]{3,2,1,0:T(8,128)(2,1)}, u32[]{:S(2)}) copy-start(bf16[1,1,256,2048]{3,2,1,0:T(8,128)(2,1)} %param.13) | copy-start | bytes 3145732
  28.5 29.0 %copy-start.8 = (bf16[1,1,256,512]{3,2,1,0:T(8,128)(2,1)S(1)}, bf16[1,1,256,512]{3,2,1,0:T(8,128)(2,1)}, u32[]{:S(2)}) copy-start(bf16[1,1,256,512]{3,2,1,0:T(8,128)(2,1)} %param.11) | copy-start | bytes 786436
  28.5 29.0 %copy-start.10 = (bf16[1,1,256,512]{3,2,1,0:T(8,128)(2,1)S(1)}, bf16[1,1,256,512]{3,2,1,0:T(8,128)(2,1)}, u32[]{:S(2)}) copy-start(bf16[1,1,256,512]{3,2,1,0:T(8,128)(2,1)} %param.12) | copy-start | bytes 786436
  47.4 8.8 %collective-permute-start.6 = (s32[1]{0:T(128)}, s32[1]{0:T(128)}, u32[]{:S(2)}, u32[]{:S(2)}) collective-permute-start(s32[1]{0:T(128)} %get-tuple-element.25.refs_4_), channel_id=1, source_target_pairs={{0,2},{1,3},{2,0},{3,1},{4,6},{5,7},{6,4},{7,5},{8,10},{9,11},{10,... | collective-permute-start | bytes 20 | tf_op jit(solution)/shard_map/ppermute | solution.py:23
  52.7 12.3 %collective-permute-start.7 = (bf16[2,64,512]{2,1,0:T(8,128)(2,1)S(1)}, bf16[2,64,512]{2,1,0:T(8,128)(2,1)S(1)}, u32[]{:S(2)}, u32[]{:S(2)}) collective-permute-start(bf16[2,64,512]{2,1,0:T(8,128)(2,1)S(1)} %get-tuple-element.33), channel_id=1, source_target_pairs={{0,1},{1,0},{2,3},{3,2},{4,5},{5,4},{6,7},{7,6},{8,9},{9,8},{10,11... | collective-permute-start | bytes 393224 | tf_op jit(solution)/shard_map/ppermute | solution.py:23
  54.8 10.2 %collective-permute-start.8 = (bf16[2,64,512]{2,1,0:T(8,128)(2,1)S(1)}, bf16[2,64,512]{2,1,0:T(8,128)(2,1)S(1)}, u32[]{:S(2)}, u32[]{:S(2)}) collective-permute-start(bf16[2,64,512]{2,1,0:T(8,128)(2,1)S(1)} %get-tuple-element.34), channel_id=1, source_target_pairs={{0,2},{1,3},{2,0},{3,1},{4,6},{5,7},{6,4},{7,5},{8,10},{9,11},{10,... | collective-permute-start | bytes 393224 | tf_op jit(solution)/shard_map/ppermute | solution.py:23
  54.8 10.2 %collective-permute-start.9 = (bf16[2,64,512]{2,1,0:T(8,128)(2,1)S(1)}, bf16[2,64,512]{2,1,0:T(8,128)(2,1)S(1)}, u32[]{:S(2)}, u32[]{:S(2)}) collective-permute-start(bf16[2,64,512]{2,1,0:T(8,128)(2,1)S(1)} %get-tuple-element.35), channel_id=1, source_target_pairs={{0,3},{1,2},{2,1},{3,0},{4,7},{5,6},{6,5},{7,4},{8,11},{9,10},{10,... | collective-permute-start | bytes 393224 | tf_op jit(solution)/shard_map/ppermute | solution.py:23

commit v3 on v1

v3 whole, which is shorter than its diff:
```python
import functools
import jax
import jax.numpy as jnp
from jax import lax
from jax.experimental import pallas as pl
from jax.experimental.pallas import tpu as pltpu
from jax.sharding import PartitionSpec as P

HEAD_SIZE = 128
BLOCK = 128
SCALING = HEAD_SIZE**-0.5
POWER = SCALING * 1.4426950408889634
VMEM_LIMIT = 32 << 20
f32 = jnp.float32
bf16 = jnp.bfloat16
i32 = jnp.int32


def dot(a, b, ca, cb):
    return lax.dot_general(a, b, (((ca,), (cb,)), ((), ())), preferred_element_type=f32)


def swap(x, n, k):
    return lax.ppermute(x, "resp", [(i, i ^ k) for i in range(n)])


def columns_of(g, width):
    return pl.ds(pl.multiple_of(g * width, width), width)


def stacked(block):
    width = block.shape[1]
    return jnp.concatenate([block[:, i : i + HEAD_SIZE] for i in range(0, width, HEAD_SIZE)], 0)


def unstacked(x, tokens):
    x = x.astype(bf16)
    return jnp.concatenate([x[:, i : i + tokens].T for i in range(0, x.shape[1], tokens)], 1)


def causal_mask(tokens, group):
    key = lax.broadcasted_iota(i32, (tokens, tokens), 0)
    row = lax.broadcasted_iota(i32, (tokens, tokens), 1)
    return jnp.concatenate([key <= row] * group, 1)


def row_of(tile, index):
    row = lax.broadcasted_iota(i32, tile.shape, 0)
    return jnp.sum(jnp.where(row == index, tile, 0.0), 0, keepdims=True)


def pack_kernel(kp_hbm, vp_hbm, payload_ref, sems):
    part = kp_hbm.shape[0]
    copies = [
        pltpu.make_async_copy(kp_hbm, payload_ref.at[:part], sems.at[0, 0]),
        pltpu.make_async_copy(vp_hbm, payload_ref.at[part:], sems.at[1, 0]),
    ]
    for copy in copies:
        copy.start()
    for copy in copies:
        copy.wait()


def own_kernel(n, group, counts, *refs):
    small_hbm, refs = refs[: 4 + counts], refs[4 + counts :]
    q_hbm, u_hbm, ko_hbm, vo_hbm = refs[:4]
    q_ref, u_ref, ko_ref, vo_ref, att_ref, stat_ref, tile_ref, alive_ref = refs[4:12]
    small_refs, sems, small_sems = refs[12:-2], refs[-2], refs[-1]
    heads, tokens, width = q_ref.shape

    def loads(g):
        return [
            pltpu.make_async_copy(ko_hbm.at[:, columns_of(g, HEAD_SIZE)], ko_ref.at[g], sems.at[0, g]),
            pltpu.make_async_copy(q_hbm.at[:, columns_of(g, width)], q_ref.at[g], sems.at[1, g]),
            pltpu.make_async_copy(vo_hbm.at[:, columns_of(g, HEAD_SIZE)], vo_ref.at[g], sems.at[2, g]),
        ]

    def late_load(g):
        return pltpu.make_async_copy(u_hbm.at[:, columns_of(g, width)], u_ref.at[g], sems.at[3, g])

    small = [
        pltpu.make_async_copy(a, b, small_sems.at[i])
        for i, (a, b) in enumerate(zip(small_hbm, small_refs))
    ]
    for copy in small:
        copy.start()
    for g in range(heads):
        for copy in loads(g):
            copy.start()
    for g in range(heads):
        late_load(g).start()

    for copy in small:
        copy.wait()
    kept_ref, spaces_ref, spans_ref, payoff_ref = small_refs[:4]
    member = lax.axis_index("resp")
    kept = kept_ref[0]
    row = lax.broadcasted_iota(i32, tile_ref.shape, 0)
    alive = jnp.zeros(tile_ref.shape, f32)
    own_alive = 0
    for i in range(spaces_ref.shape[1]):
        alive += jnp.where((row == spaces_ref[0, i]) & (i < kept), 1.0, 0.0)
        own_alive += jnp.where((spaces_ref[0, i] == member) & (i < kept), 1, 0)
    alive_ref[...] = alive
    count = sum(r[0] for r in small_refs[4:]).astype(f32)
    tile_ref[...] = jnp.where(row == member, payoff_ref[0, 0], 0.0) + jnp.where(row == n, count, 0.0)
    token = lax.broadcasted_iota(i32, (1, tokens), 1)
    valid = jnp.where(token < own_alive * spans_ref[0, 0] * BLOCK, 1.0, 0.0)
    valid = jnp.concatenate([valid] * group, 1)

    def step(g, carry):
        for copy in loads(g):
            copy.wait()
        s = dot(ko_ref[g], stacked(q_ref[g]), 1, 1)
        s = jnp.where(causal_mask(tokens, group), s, -1e30)
        top = jnp.max(s, 0, keepdims=True)
        e = jnp.exp2((s - top) * POWER)
        stat_ref[g, 0:1] = top
        stat_ref[g, 1:2] = jnp.sum(e, 0, keepdims=True)
        stat_ref[g, 2:3] = valid
        att_ref[g] = dot(vo_ref[g], e.astype(bf16), 0, 0)
        return carry

    lax.fori_loop(0, heads, step, 0)
    for g in range(heads):
        late_load(g).wait()


def prefix_kernel(n, *refs):
    q_ref, u_ref, own_ref, stat_ref, tile_ref, recv_ref = refs[:6]
    pay_refs = refs[6 : 6 + n]
    out_ref, ds_ref, line_ref, sum_ref = refs[6 + n : 10 + n]
    term_refs = refs[10 + n :]
    heads, tokens, width = q_ref.shape
    part = pay_refs[0].shape[0] // 2
    sum_ref[...] = tile_ref[...] + recv_ref[...]

    def step(g, carry):
        cols = columns_of(g, HEAD_SIZE)
        keys = jnp.concatenate([r[:part, cols] for r in pay_refs], 0)
        values = jnp.concatenate([r[part:, cols] for r in pay_refs], 0)
        q = stacked(q_ref[g])
        u = stacked(u_ref[g])
        s = dot(keys, q, 1, 1)
        own_top = stat_ref[g, 0:1]
        valid = stat_ref[g, 2:3] > 0.0
        top = jnp.maximum(jnp.max(s, 0, keepdims=True), own_top)
        e = jnp.exp2((s - top) * POWER)
        shrink = jnp.exp2((own_top - top) * POWER)
        mass = jnp.sum(e, 0, keepdims=True) + shrink * stat_ref[g, 1:2]
        inverse = jnp.where(valid, 1.0 / mass, 0.0)
        p = e * inverse
        p_low = p.astype(bf16)
        attended = dot(values, p_low, 0, 0) + own_ref[g] * (shrink * inverse)
        out_ref[g] = unstacked(attended, tokens)
        dp = dot(values, u, 1, 1)
        delta = jnp.sum(u.T.astype(f32) * attended, 0, keepdims=True)
        ds = (p * (dp - delta)).astype(bf16)
        ds_ref[g] = ds
        line_ref[g, 0:1] = jnp.where(valid, top * POWER + jnp.log2(mass), 1e30)
        line_ref[g, 1:2] = delta
        dk = dot(ds, q, 1, 0) * SCALING
        dv = dot(p_low, u, 1, 0)
        for k, ref in enumerate(term_refs):
            ref[:part, cols] = dk[k * part : (k + 1) * part].astype(ref.dtype)
            ref[part:, cols] = dv[k * part : (k + 1) * part].astype(ref.dtype)
        return carry

    lax.fori_loop(0, heads, step, 0)


def rest_kernel(n, group, *refs):
    q_ref, u_ref, ko_ref, vo_ref, att_ref, ds_ref, line_ref, sum_ref, recv_ref, alive_ref = refs[:10]
    pay_refs = refs[10 : 10 + n]
    out_hbm, dq_hbm, dko_hbm, dvo_hbm, weights_ref = refs[10 + n : 15 + n]
    dq_ref, dko_ref, dvo_ref, sems = refs[15 + n :]
    heads, tokens, width = q_ref.shape
    part = pay_refs[0].shape[0] // 2

    def early_store(g):
        return pltpu.make_async_copy(att_ref.at[g], out_hbm.at[:, columns_of(g, width)], sems.at[0, g])

    def stores(g):
        slim = columns_of(g, HEAD_SIZE)
        return [
            pltpu.make_async_copy(dq_ref.at[g], dq_hbm.at[:, columns_of(g, width)], sems.at[1, g]),
            pltpu.make_async_copy(dko_ref.at[g], dko_hbm.at[:, slim], sems.at[2, g]),
            pltpu.make_async_copy(dvo_ref.at[g], dvo_hbm.at[:, slim], sems.at[3, g]),
        ]

    for g in range(heads):
        early_store(g).start()
    tile = sum_ref[...] + recv_ref[...]
    alive = alive_ref[...]
    mean = jnp.sum(tile * alive, 0, keepdims=True) / jnp.sum(alive, 0, keepdims=True)
    weights = (tile - mean) / row_of(tile, n)
    weights_ref[...] = weights
    weight = row_of(weights, lax.axis_index("resp"))
    weight_rows = jnp.concatenate([weight] * (group * tokens // HEAD_SIZE), 1)

    def step(g, carry):
        cols = columns_of(g, HEAD_SIZE)
        keys = jnp.concatenate([r[:part, cols] for r in pay_refs], 0)
        q = stacked(q_ref[g])
        u = stacked(u_ref[g])
        ko, vo = ko_ref[g], vo_ref[g]
        s = dot(ko, q, 1, 1)
        s = jnp.where(causal_mask(tokens, group), s, -1e30)
        p = jnp.exp2(s * POWER - line_ref[g, 0:1])
        dp = dot(vo, u, 1, 1)
        ds = (p * (dp - line_ref[g, 1:2])).astype(bf16)
        dq = dot(keys, ds_ref[g], 0, 0) + dot(ko, ds, 0, 0)
        dq_ref[g] = unstacked(dq * (weight_rows * SCALING), tokens)
        dko_ref[g] = (dot(ds, q, 1, 0) * (weight * SCALING)).astype(bf16)
        dvo_ref[g] = (dot(p.astype(bf16), u, 1, 0) * weight).astype(bf16)
        for copy in stores(g):
            copy.start()
        return carry

    lax.fori_loop(0, heads, step, 0)
    for g in range(heads):
        early_store(g).wait()
        for copy in stores(g):
            copy.wait()


def total_kernel(n, weights_ref, *refs):
    term_refs, (key_ref, value_ref) = refs[:n], refs[n:]
    part, width = key_ref.shape
    weights = weights_ref[...]
    member = lax.axis_index("resp")
    total = jnp.zeros((2 * part, width), f32)
    for k, ref in enumerate(term_refs):
        weight = row_of(weights, member ^ k)
        total += ref[...].astype(f32) * jnp.concatenate([weight] * (width // HEAD_SIZE), 1)
    key_ref[...] = total[:part].astype(bf16)
    value_ref[...] = total[part:].astype(bf16)


def local(q, ko, vo, u, kp, vp, kept, spaces, spans, payoffs):
    n = lax.axis_size("resp")
    n_prompt = lax.axis_size("prompt")
    tokens = q.shape[2]
    kv_width = ko.shape[3]
    heads = kv_width // HEAD_SIZE
    group = q.shape[3] // kv_width
    width = group * HEAD_SIZE
    rows = group * tokens
    part = kp.shape[1]
    prefix = n * part
    tile_shape = (-(-(n + 1) // 8) * 8, HEAD_SIZE)

    vmem = pl.BlockSpec(memory_space=pltpu.VMEM)
    hbm = pl.BlockSpec(memory_space=pl.ANY)

    def pinned(x):
        return pltpu.with_memory_space_constraint(x, pltpu.HBM)

    def call(kernel, units, ins, out, scratch):
        return pl.pallas_call(
            kernel,
            in_specs=[spec for spec, _ in ins],
            out_specs=[spec for spec, _ in out],
            out_shape=[shape for _, shape in out],
            scratch_shapes=scratch,
            compiler_params=pltpu.CompilerParams(vmem_limit_bytes=VMEM_LIMIT),
            cost_estimate=pl.CostEstimate(
                flops=units * 2 * heads * rows * tokens * HEAD_SIZE,
                bytes_accessed=1 << 20,
                transcendentals=0,
            ),
        )(*[x for _, x in ins])

    def kept_in(shape, kind):
        return (vmem, pltpu.VMEM(shape, kind))

    def given(shape, kind=bf16, spec=hbm):
        return (spec, jax.ShapeDtypeStruct(shape, kind))

    sems = pltpu.SemaphoreType.DMA((4, heads))
    stat = kept_in((heads, 8, rows), f32)
    tile_kind = kept_in(tile_shape, f32)
    wide, slim = (heads, tokens, width), (heads, tokens, HEAD_SIZE)
    q, ko, vo, u = q[0, 0], ko[0, 0], vo[0, 0], u[0, 0]

    (payload,) = call(
        pack_kernel,
        0,
        [(hbm, pinned(kp[0])), (hbm, pinned(vp[0]))],
        [kept_in((2 * part, kv_width), bf16)],
        [sems],
    )
    pays = [payload] + [swap(payload, n, k) for k in range(1, n)]

    share = -(-n_prompt // n)
    counts = []
    for a in range(share):
        perm = [
            (p * n + m, (p ^ (m * share + a)) * n + m)
            for p in range(n_prompt)
            for m in range(n)
            if m * share + a < n_prompt
        ]
        counts.append(lax.ppermute(kept, ("prompt", "resp"), perm))

    small = [kept, spaces, spans, payoffs] + counts
    q_in, u_in, ko_in, vo_in, own, own_stat, tile, alive = call(
        functools.partial(own_kernel, n, group, share),
        2,
        [(hbm, x) for x in small] + [(hbm, pinned(x)) for x in (q, u, ko, vo)],
        [kept_in(wide, bf16)] * 2
        + [kept_in(slim, bf16)] * 2
        + [kept_in((heads, HEAD_SIZE, rows), f32), stat, tile_kind, tile_kind],
        [pltpu.SMEM(x.shape, x.dtype) for x in small]
        + [sems, pltpu.SemaphoreType.DMA((len(small),))],
    )
    k = 1
    while 4 * k < n:
        tile = tile + swap(tile, n, k)
        k *= 2
    att, ds, line, tile_sum, *terms = call(
        functools.partial(prefix_kernel, n),
        5,
        [(vmem, x) for x in [q_in, u_in, own, own_stat, tile, swap(tile, n, k)] + pays],
        [kept_in(wide, bf16), kept_in((heads, prefix, rows), bf16), stat, tile_kind]
        + [kept_in((2 * part, kv_width), f32 if i == 0 else bf16) for i in range(n)],
        [],
    )
    other = swap(tile_sum, n, 2 * k)
    received = [swap(t, n, i) for i, t in enumerate(terms) if i > 0]
    attn_out, dq, dko, dvo, weights = call(
        functools.partial(rest_kernel, n, group),
        6,
        [(vmem, x) for x in [q_in, u_in, ko_in, vo_in, att, ds, line, tile_sum, other, alive] + pays],
        [given(q.shape), given(q.shape), given(ko.shape), given(ko.shape), tile_kind],
        [pltpu.VMEM(wide, bf16), pltpu.VMEM(slim, bf16), pltpu.VMEM(slim, bf16), sems],
    )
    key_total, value_total = call(
        functools.partial(total_kernel, n),
        0,
        [(vmem, x) for x in [weights, terms[0]] + received],
        [given((part, kv_width), spec=vmem)] * 2,
        [],
    )
    return (
        attn_out[None, None],
        dq[None, None],
        dko[None, None],
        dvo[None, None],
        key_total[None],
        value_total[None],
    )


def solution(mesh):
    wide = P("prompt", "resp", None, None)
    rows = P("prompt", "resp", None)
    pair = P("prompt", "resp")
    return jax.shard_map(
        local,
        mesh=mesh,
        in_specs=(wide, wide, wide, wide, rows, rows, P("prompt"), P("prompt", None), pair, pair),
        out_specs=(wide, wide, wide, wide, rows, rows),
        check_vma=False,
    )
```

time: 54.4 us -> 41.4 us (0.76)
  Pallas kernels: 10.2 us -> 16.2 us
  starting transfers between devices: 25.4 us -> 20.1 us
  waiting for transfers between devices: 6.68 us -> 1.64 us
  between operations: 7.24 us -> 2.65 us
  local copies, waits for them, and re-layouts: 2.98 us -> 0.65 us
  other arithmetic: 1.6 us -> 0 us
    pallas_call x1 -> x5, Pallas kernels: 10.2 us -> 16.2 us  [call(): pl.pallas_call(kernel, in_specs=[spec for spec, _ in ins], out_specs=[spe...]
    ppermute x14 -> x10, starting transfers between devices: 25.4 us -> 20.1 us  [the longest x8 18.2 us: swap(): return lax.ppermute(x, 'resp', [(i, i ^ k) for i in range(n)])]
    ppermute x14 -> x10, waiting for transfers between devices: 6.68 us -> 1.64 us  [the longest x8 1.63 us: swap(): return lax.ppermute(x, 'resp', [(i, i ^ k) for i in range(n)])]
    slice x2 -> x0, local copies, waits for them, and re-layouts: 1.73 us -> none  [the longest x1 1.07 us: local(): total += swap(terms[:, k * part:(k + 1) * part], 'resp', n, k).astype(f32)]
    convert_element_type x1 -> x0, other arithmetic: 0.97 us -> none  [local(): total = total.astype(bf16)]
    reduce_sum x1 -> x0, other arithmetic: 0.63 us -> none  [local(): jnp.sum(jnp.where((jnp.arange(n) < kept[0]) & (spaces[0] == member), 1, 0))]
    unnamed x14 -> x2, local copies, waits for them, and re-layouts: 1.25 us -> 0.65 us
  transfers between devices with their start and end apart: 14 -> 10, of which waited for: 7 -> 1; matrix products, arithmetic and copies ran while one was open for 1% -> 0% of each run, Pallas kernels for 0% -> 23%
where the time goes in v3:
time: 41.4 us; the launch traced here: 41.2 us
  starting transfers between devices  20.1 us (49%)
  Pallas kernels  16.2 us (39%)
  between operations  2.65 us (6%)
  waiting for transfers between devices  1.64 us (4%)
  local copies, waits for them, and re-layouts  0.65 us (2%)
    ppermute x8, starting transfers between devices, swap(): return lax.ppermute(x, 'resp', [(i, i ^ k) for i in range(n)])  18.2 us
    pallas_call x5, Pallas kernels, call(): pl.pallas_call(kernel, in_specs=[spec for spec, _ in ins], out_specs=[spe...  16.2 us
    ppermute x2, starting transfers between devices, local(): counts.append(lax.ppermute(kept, ('prompt', 'resp'), perm))  1.85 us
    ppermute x8, waiting for transfers between devices, swap(): return lax.ppermute(x, 'resp', [(i, i ^ k) for i in range(n)])  1.63 us
  transfers between devices with their start and end apart: 10, of which 1 were waited for; matrix products, arithmetic and copies ran while one was open for 0% of the time, Pallas kernels for 23%

profile of v3, /device:TPU:0, one launch (start us, length us, event | category | flops | bytes accessed | tf_op | source)
XLA Modules:
  0.0 41.2 jit_solution(9280069506154771392)
XLA Ops:
  0.6 1.0 %shard_map.146.refs_6_.refs_10_ = bf16[128,512]{1,0:T(8,128)(2,1)S(1)} custom-call(bf16[64,512]{1,0:T(8,128)(2,1)} %bitcast.16, bf16[64,512]{1,0:T(8,128)(2,1)} %bitcast.17), custom_call_target="tpu_custom_call" | custom-call | bytes 1048576 | tf_op jit(solution)/shard_map/pallas_call | solution.py:260
  1.7 4.0 %collective-permute-start.5 = (bf16[128,512]{1,0:T(8,128)(2,1)S(1)}, bf16[128,512]{1,0:T(8,128)(2,1)S(1)}, u32[]{:S(2)}, u32[]{:S(2)}) collective-permute-start(bf16[128,512]{1,0:T(8,128)(2,1)S(1)} %shard_map.146.refs_6_.refs_10_), channel_id=1, source_target_pairs={{0,3},{1,2},{2,1},{3,0},{4,7},{5,6},{6,5},{7,4},{8,11},{9,10},{10,... | collective-permute-start | bytes 393224 | tf_op jit(solution)/shard_map/ppermute | solution.py:24
  5.6 0.5 %collective-permute-start.4 = (bf16[128,512]{1,0:T(8,128)(2,1)S(1)}, bf16[128,512]{1,0:T(8,128)(2,1)S(1)}, u32[]{:S(2)}, u32[]{:S(2)}) collective-permute-start(bf16[128,512]{1,0:T(8,128)(2,1)S(1)} %shard_map.146.refs_6_.refs_10_), channel_id=1, source_target_pairs={{0,2},{1,3},{2,0},{3,1},{4,6},{5,7},{6,4},{7,5},{8,10},{9,11},{10,... | collective-permute-start | bytes 393224 | tf_op jit(solution)/shard_map/ppermute | solution.py:24
  6.1 0.1 collective-permute-start.3
  6.3 1.8 %collective-permute-start = (s32[1]{0:T(128)}, s32[1]{0:T(128)}, u32[]{:S(2)}, u32[]{:S(2)}) collective-permute-start(s32[1]{0:T(128)} %param.16), channel_id=1, source_target_pairs={{0,0},{1,9},{2,18},{3,27},{4,4},{5,13},{6,22},{7,31},{8,8},{9,1},{... | collective-permute-start | bytes 20 | tf_op jit(solution)/shard_map/ppermute | solution.py:304
  8.1 0.0 collective-permute-start.1
  10.1 0.0 collective-permute-done.refs_4_
  10.1 0.0 collective-permute-done.1.refs_5_
  10.1 0.0 copy-start
  10.1 0.6 %copy-done = s32[1,4]{1,0:T(1,128)S(1)} copy-done((s32[1,4]{1,0:T(1,128)S(1)}, s32[1,4]{1,0:T(1,128)}, u32[]{:S(2)}) %copy-start) | copy-done | bytes 40
  10.7 4.8 %shard_map.145 = (bf16[4,256,512]{2,1,0:T(8,128)(2,1)S(1)}, bf16[4,256,512]{2,1,0:T(8,128)(2,1)S(1)}, bf16[4,256,128]{2,1,0:T(8,128)(2,1)S(1)}, bf16[4,256,128]{...) custom-call(s32[1]{0:T(128)S(6)} %copy.16.refs_0_, ...), custom_call_target="tpu_custom_call" | custom-call | flops 536870912 | bytes 1048576 | tf_op jit(solution)/shard_map/pallas_call | solution.py:260
  15.6 4.7 %collective-permute-start.2 = (f32[8,128]{1,0:T(8,128)S(1)}, f32[8,128]{1,0:T(8,128)S(1)}, u32[]{:S(2)}, u32[]{:S(2)}) collective-permute-start(f32[8,128]{1,0:T(8,128)S(1)} %get-tuple-element.35.refs_4_), channel_id=1, source_target_pairs={{0,1},{1,0},{2,3},{3,2},{4,5},{5,4},{6,7},{7,6},{8,9},{9,8},{10,11... | collective-permute-start | bytes 12296 | tf_op jit(solution)/shard_map/ppermute | solution.py:24
  20.3 1.6 %collective-permute-done.2.refs_5_ = f32[8,128]{1,0:T(8,128)S(1)} collective-permute-done((f32[8,128]{1,0:T(8,128)S(1)}, f32[8,128]{1,0:T(8,128)S(1)}, u32[]{:S(2)}, u32[]{:S(2)}) %collective-permute-start.2) | collective-permute-done | bytes 4128 | tf_op jit(solution)/shard_map/ppermute | solution.py:24
  21.9 0.0 collective-permute-done.5.refs_9_.refs_13_
  21.9 0.0 collective-permute-done.4.refs_8_.refs_12_
  21.9 0.0 collective-permute-done.3.refs_7_.refs_11_
  21.9 4.7 %shard_map.147 = (bf16[4,256,512]{2,1,0:T(8,128)(2,1)S(1)}, bf16[4,256,1024]{2,1,0:T(8,128)(2,1)S(1)}, f32[4,8,1024]{2,1,0:T(8,128)S(1)}, f32[8,128]{1,0:T(8,128...) custom-call(bf16[4,256,512]{2,1,0:T(8,128)(2,1)S(1)} %get-tuple-elem, ...), custom_call_target="tpu_custom_call" | custom-call | flops 1342177280 | bytes 1048576 | tf_op jit(solution)/shard_map/pallas_call | solution.py:260
  26.6 5.4 %collective-permute-start.6 = (f32[8,128]{1,0:T(8,128)S(1)}, f32[8,128]{1,0:T(8,128)S(1)}, u32[]{:S(2)}, u32[]{:S(2)}) collective-permute-start(f32[8,128]{1,0:T(8,128)S(1)} %get-tuple-element.39.refs_7_), channel_id=1, source_target_pairs={{0,2},{1,3},{2,0},{3,1},{4,6},{5,7},{6,4},{7,5},{8,10},{9,11},{10,... | collective-permute-start | bytes 12296 | tf_op jit(solution)/shard_map/ppermute | solution.py:24
  32.1 2.0 %collective-permute-start.7 = (bf16[128,512]{1,0:T(8,128)(2,1)S(1)}, bf16[128,512]{1,0:T(8,128)(2,1)S(1)}, u32[]{:S(2)}, u32[]{:S(2)}) collective-permute-start(bf16[128,512]{1,0:T(8,128)(2,1)S(1)} %get-tuple-element.47), channel_id=1, source_target_pairs={{0,1},{1,0},{2,3},{3,2},{4,5},{5,4},{6,7},{7,6},{8,9},{9,8},{10,11... | collective-permute-start | bytes 393224 | tf_op jit(solution)/shard_map/ppermute | solution.py:24
  34.1 0.1 collective-permute-start.8
  34.2 1.4 %collective-permute-start.9 = (bf16[128,512]{1,0:T(8,128)(2,1)S(1)}, bf16[128,512]{1,0:T(8,128)(2,1)S(1)}, u32[]{:S(2)}, u32[]{:S(2)}) collective-permute-start(bf16[128,512]{1,0:T(8,128)(2,1)S(1)} %get-tuple-element.49), channel_id=1, source_target_pairs={{0,3},{1,2},{2,1},{3,0},{4,7},{5,6},{6,5},{7,4},{8,11},{9,10},{10,... | collective-permute-start | bytes 393224 | tf_op jit(solution)/shard_map/ppermute | solution.py:24
  35.5 4.9 %shard_map.148 = (bf16[256,2048]{1,0:T(8,128)(2,1)}, bf16[256,2048]{1,0:T(8,128)(2,1)}, bf16[256,512]{1,0:T(8,128)(2,1)}, bf16[256,512]{1,0:T(8,128)(2,1)}, f32[8,128]{1,0:T(8,128)S(1)}) custom-call(bf16[4,256,512]{2,1,0:T(8,128)(2,1)S(1)} %get-tuple-element.29.refs_0_, bf16[4,256,512]{2,1,0:T(8,128)(2,1)S(1)} %get-tuple-element.30.refs_1_, ...), custom_call_target="tpu_custom_call" | custom-call | flops 1610612736 | bytes 1048576 | tf_op jit(solution)/shard_map/pallas_call | solution.py:260
  40.4 0.0 collective-permute-done.8.refs_2_
  40.4 0.7 %shard_map.149 = (bf16[64,512]{1,0:T(8,128)(2,1)}, bf16[64,512]{1,0:T(8,128)(2,1)}) custom-call(f32[8,128]{1,0:T(8,128)S(1)} %get-tuple-element.45.weights_ref, f32[128,512]{1,0:T(8,128)S(1)} %get-tuple-element.46.refs_0_, bf16[128,512]{1,0:T(8,128)(2,1)S(1)} %collective-permute-done.7.refs_1_, bf16[128,512]{1,0:T(8,128)(2,1)S(1)} %collective-permute-done.8.refs_2_, ...), custom_call_target="tpu_custom_call" | custom-call | bytes 1048576 | tf_op jit(solution)/shard_map/pallas_call | solution.py:260
  (3 shorter events, 0.0 us)
Async XLA Ops:
  1.7 20.2 %collective-permute-start.5 = (bf16[128,512]{1,0:T(8,128)(2,1)S(1)}, bf16[128,512]{1,0:T(8,128)(2,1)S(1)}, u32[]{:S(2)}, u32[]{:S(2)}) collective-permute-start(bf16[128,512]{1,0:T(8,128)(2,1)S(1)} %shard_map.146.refs_6_.refs_10_), channel_id=1, source_target_pairs={{0,3},{1,2},{2,1},{3,0},{4,7},{5,6},{6,5},{7,4},{8,11},{9,10},{10,... | collective-permute-start | bytes 393224 | tf_op jit(solution)/shard_map/ppermute | solution.py:24
  5.6 16.3 %collective-permute-start.4 = (bf16[128,512]{1,0:T(8,128)(2,1)S(1)}, bf16[128,512]{1,0:T(8,128)(2,1)S(1)}, u32[]{:S(2)}, u32[]{:S(2)}) collective-permute-start(bf16[128,512]{1,0:T(8,128)(2,1)S(1)} %shard_map.146.refs_6_.refs_10_), channel_id=1, source_target_pairs={{0,2},{1,3},{2,0},{3,1},{4,6},{5,7},{6,4},{7,5},{8,10},{9,11},{10,... | collective-permute-start | bytes 393224 | tf_op jit(solution)/shard_map/ppermute | solution.py:24
  6.1 15.8 %collective-permute-start.3 = (bf16[128,512]{1,0:T(8,128)(2,1)S(1)}, bf16[128,512]{1,0:T(8,128)(2,1)S(1)}, u32[]{:S(2)}, u32[]{:S(2)}) collective-permute-start(bf16[128,512]{1,0:T(8,128)(2,1)S(1)} %shard_map.146.refs_6_.refs_10_), channel_id=1, source_target_pairs={{0,1},{1,0},{2,3},{3,2},{4,5},{5,4},{6,7},{7,6},{8,9},{9,8},{10,11... | collective-permute-start | bytes 393224 | tf_op jit(solution)/shard_map/ppermute | solution.py:24
  6.3 3.8 %collective-permute-start = (s32[1]{0:T(128)}, s32[1]{0:T(128)}, u32[]{:S(2)}, u32[]{:S(2)}) collective-permute-start(s32[1]{0:T(128)} %param.16), channel_id=1, source_target_pairs={{0,0},{1,9},{2,18},{3,27},{4,4},{5,13},{6,22},{7,31},{8,8},{9,1},{... | collective-permute-start | bytes 20 | tf_op jit(solution)/shard_map/ppermute | solution.py:304
  8.1 2.0 %collective-permute-start.1 = (s32[1]{0:T(128)}, s32[1]{0:T(128)}, u32[]{:S(2)}, u32[]{:S(2)}) collective-permute-start(s32[1]{0:T(128)} %param.16), channel_id=1, source_target_pairs={{0,4},{1,13},{2,22},{3,31},{4,0},{5,9},{6,18},{7,27},{8,12},{9,5},... | collective-permute-start | bytes 20 | tf_op jit(solution)/shard_map/ppermute | solution.py:304
  10.1 0.7 %copy-start = (s32[1,4]{1,0:T(1,128)S(1)}, s32[1,4]{1,0:T(1,128)}, u32[]{:S(2)}) copy-start(s32[1,4]{1,0:T(1,128)} %refs_1_.1) | copy-start | bytes 52
  15.6 6.3 %collective-permute-start.2 = (f32[8,128]{1,0:T(8,128)S(1)}, f32[8,128]{1,0:T(8,128)S(1)}, u32[]{:S(2)}, u32[]{:S(2)}) collective-permute-start(f32[8,128]{1,0:T(8,128)S(1)} %get-tuple-element.35.refs_4_), channel_id=1, source_target_pairs={{0,1},{1,0},{2,3},{3,2},{4,5},{5,4},{6,7},{7,6},{8,9},{9,8},{10,11... | collective-permute-start | bytes 12296 | tf_op jit(solution)/shard_map/ppermute | solution.py:24
  26.6 8.9 %collective-permute-start.6 = (f32[8,128]{1,0:T(8,128)S(1)}, f32[8,128]{1,0:T(8,128)S(1)}, u32[]{:S(2)}, u32[]{:S(2)}) collective-permute-start(f32[8,128]{1,0:T(8,128)S(1)} %get-tuple-element.39.refs_7_), channel_id=1, source_target_pairs={{0,2},{1,3},{2,0},{3,1},{4,6},{5,7},{6,4},{7,5},{8,10},{9,11},{10,... | collective-permute-start | bytes 12296 | tf_op jit(solution)/shard_map/ppermute | solution.py:24
  32.1 8.4 %collective-permute-start.7 = (bf16[128,512]{1,0:T(8,128)(2,1)S(1)}, bf16[128,512]{1,0:T(8,128)(2,1)S(1)}, u32[]{:S(2)}, u32[]{:S(2)}) collective-permute-start(bf16[128,512]{1,0:T(8,128)(2,1)S(1)} %get-tuple-element.47), channel_id=1, source_target_pairs={{0,1},{1,0},{2,3},{3,2},{4,5},{5,4},{6,7},{7,6},{8,9},{9,8},{10,11... | collective-permute-start | bytes 393224 | tf_op jit(solution)/shard_map/ppermute | solution.py:24
  34.1 6.4 %collective-permute-start.8 = (bf16[128,512]{1,0:T(8,128)(2,1)S(1)}, bf16[128,512]{1,0:T(8,128)(2,1)S(1)}, u32[]{:S(2)}, u32[]{:S(2)}) collective-permute-start(bf16[128,512]{1,0:T(8,128)(2,1)S(1)} %get-tuple-element.48), channel_id=1, source_target_pairs={{0,2},{1,3},{2,0},{3,1},{4,6},{5,7},{6,4},{7,5},{8,10},{9,11},{10,... | collective-permute-start | bytes 393224 | tf_op jit(solution)/shard_map/ppermute | solution.py:24
  34.2 6.3 %collective-permute-start.9 = (bf16[128,512]{1,0:T(8,128)(2,1)S(1)}, bf16[128,512]{1,0:T(8,128)(2,1)S(1)}, u32[]{:S(2)}, u32[]{:S(2)}) collective-permute-start(bf16[128,512]{1,0:T(8,128)(2,1)S(1)} %get-tuple-element.49), channel_id=1, source_target_pairs={{0,3},{1,2},{2,1},{3,0},{4,7},{5,6},{6,5},{7,4},{8,11},{9,10},{10,... | collective-permute-start | bytes 393224 | tf_op jit(solution)/shard_map/ppermute | solution.py:24

commit v4 on v3

--- a/solution.py
+++ b/solution.py
@@ -8,6 +8,7 @@
 
 HEAD_SIZE = 128
 BLOCK = 128
+EXTRA = 16
 SCALING = HEAD_SIZE**-0.5
 POWER = SCALING * 1.4426950408889634
 VMEM_LIMIT = 32 << 20
@@ -49,20 +50,27 @@
     return jnp.sum(jnp.where(row == index, tile, 0.0), 0, keepdims=True)
 
 
-def pack_kernel(kp_hbm, vp_hbm, payload_ref, sems):
-    part = kp_hbm.shape[0]
+def pack_kernel(payoff_ref, kp_hbm, vp_hbm, payload_ref, sems):
+    part, width = kp_hbm.shape
     copies = [
         pltpu.make_async_copy(kp_hbm, payload_ref.at[:part], sems.at[0, 0]),
-        pltpu.make_async_copy(vp_hbm, payload_ref.at[part:], sems.at[1, 0]),
+        pltpu.make_async_copy(vp_hbm, payload_ref.at[part : 2 * part], sems.at[1, 0]),
     ]
     for copy in copies:
         copy.start()
+    payoff = jnp.full((EXTRA, width), payoff_ref[0, 0], f32)
+    high = payoff.astype(bf16).astype(f32)
+    middle = (payoff - high).astype(bf16).astype(f32)
+    low = payoff - high - middle
+    row = lax.broadcasted_iota(i32, payoff.shape, 0)
+    pieces = jnp.where(row == 0, high, jnp.where(row == 1, middle, jnp.where(row == 2, low, 0.0)))
+    payload_ref[2 * part :] = pieces.astype(bf16)
     for copy in copies:
         copy.wait()
 
 
-def own_kernel(n, group, counts, *refs):
-    small_hbm, refs = refs[: 4 + counts], refs[4 + counts :]
+def own_kernel(group, counts, *refs):
+    small_hbm, refs = refs[: 3 + counts], refs[3 + counts :]
     q_hbm, u_hbm, ko_hbm, vo_hbm = refs[:4]
     q_ref, u_ref, ko_ref, vo_ref, att_ref, stat_ref, tile_ref, alive_ref = refs[4:12]
     small_refs, sems, small_sems = refs[12:-2], refs[-2], refs[-1]
@@ -92,18 +100,18 @@
 
     for copy in small:
         copy.wait()
-    kept_ref, spaces_ref, spans_ref, payoff_ref = small_refs[:4]
+    kept_ref, spaces_ref, spans_ref = small_refs[:3]
     member = lax.axis_index("resp")
     kept = kept_ref[0]
-    row = lax.broadcasted_iota(i32, tile_ref.shape, 0)
-    alive = jnp.zeros(tile_ref.shape, f32)
+    row = lax.broadcasted_iota(i32, alive_ref.shape, 0)
+    alive = jnp.zeros(alive_ref.shape, f32)
     own_alive = 0
     for i in range(spaces_ref.shape[1]):
         alive += jnp.where((row == spaces_ref[0, i]) & (i < kept), 1.0, 0.0)
         own_alive += jnp.where((spaces_ref[0, i] == member) & (i < kept), 1, 0)
     alive_ref[...] = alive
-    count = sum(r[0] for r in small_refs[4:]).astype(f32)
-    tile_ref[...] = jnp.where(row == member, payoff_ref[0, 0], 0.0) + jnp.where(row == n, count, 0.0)
+    count = kept + sum(r[0] for r in small_refs[3:])
+    tile_ref[...] = jnp.full(tile_ref.shape, count.astype(f32))
     token = lax.broadcasted_iota(i32, (1, tokens), 1)
     valid = jnp.where(token < own_alive * spans_ref[0, 0] * BLOCK, 1.0, 0.0)
     valid = jnp.concatenate([valid] * group, 1)
@@ -132,13 +140,13 @@
     out_ref, ds_ref, line_ref, sum_ref = refs[6 + n : 10 + n]
     term_refs = refs[10 + n :]
     heads, tokens, width = q_ref.shape
-    part = pay_refs[0].shape[0] // 2
+    part = (pay_refs[0].shape[0] - EXTRA) // 2
     sum_ref[...] = tile_ref[...] + recv_ref[...]
 
     def step(g, carry):
         cols = columns_of(g, HEAD_SIZE)
         keys = jnp.concatenate([r[:part, cols] for r in pay_refs], 0)
-        values = jnp.concatenate([r[part:, cols] for r in pay_refs], 0)
+        values = jnp.concatenate([r[part : 2 * part, cols] for r in pay_refs], 0)
         q = stacked(q_ref[g])
         u = stacked(u_ref[g])
         s = dot(keys, q, 1, 1)
@@ -175,7 +183,7 @@
     out_hbm, dq_hbm, dko_hbm, dvo_hbm, weights_ref = refs[10 + n : 15 + n]
     dq_ref, dko_ref, dvo_ref, sems = refs[15 + n :]
     heads, tokens, width = q_ref.shape
-    part = pay_refs[0].shape[0] // 2
+    part = (pay_refs[0].shape[0] - EXTRA) // 2
 
     def early_store(g):
         return pltpu.make_async_copy(att_ref.at[g], out_hbm.at[:, columns_of(g, width)], sems.at[0, g])
@@ -190,12 +198,18 @@
 
     for g in range(heads):
         early_store(g).start()
-    tile = sum_ref[...] + recv_ref[...]
+    batch = sum_ref[0:1] + recv_ref[0:1]
     alive = alive_ref[...]
-    mean = jnp.sum(tile * alive, 0, keepdims=True) / jnp.sum(alive, 0, keepdims=True)
-    weights = (tile - mean) / row_of(tile, n)
-    weights_ref[...] = weights
-    weight = row_of(weights, lax.axis_index("resp"))
+    member = lax.axis_index("resp")
+    rewards = [
+        jnp.sum(r[2 * part :, :HEAD_SIZE].astype(f32), 0, keepdims=True) for r in pay_refs
+    ]
+    total = sum(reward * row_of(alive, member ^ k) for k, reward in enumerate(rewards))
+    mean = total / jnp.sum(alive, 0, keepdims=True)
+    weights = [(reward - mean) / batch for reward in rewards]
+    for k in range(n):
+        weights_ref[k : k + 1] = weights[k]
+    weight = weights[0]
     weight_rows = jnp.concatenate([weight] * (group * tokens // HEAD_SIZE), 1)
 
     def step(g, carry):
@@ -227,11 +241,9 @@
 def total_kernel(n, weights_ref, *refs):
     term_refs, (key_ref, value_ref) = refs[:n], refs[n:]
     part, width = key_ref.shape
-    weights = weights_ref[...]
-    member = lax.axis_index("resp")
     total = jnp.zeros((2 * part, width), f32)
     for k, ref in enumerate(term_refs):
-        weight = row_of(weights, member ^ k)
+        weight = weights_ref[k : k + 1]
         total += ref[...].astype(f32) * jnp.concatenate([weight] * (width // HEAD_SIZE), 1)
     key_ref[...] = total[:part].astype(bf16)
     value_ref[...] = total[part:].astype(bf16)
@@ -248,10 +260,12 @@
     rows = group * tokens
     part = kp.shape[1]
     prefix = n * part
-    tile_shape = (-(-(n + 1) // 8) * 8, HEAD_SIZE)
+    tile_shape = (8, HEAD_SIZE)
+    slots_shape = (-(-n // 8) * 8, HEAD_SIZE)
 
     vmem = pl.BlockSpec(memory_space=pltpu.VMEM)
     hbm = pl.BlockSpec(memory_space=pl.ANY)
+    scalar = pl.BlockSpec(memory_space=pltpu.SMEM)
 
     def pinned(x):
         return pltpu.with_memory_space_constraint(x, pltpu.HBM)
@@ -280,59 +294,52 @@
     sems = pltpu.SemaphoreType.DMA((4, heads))
     stat = kept_in((heads, 8, rows), f32)
     tile_kind = kept_in(tile_shape, f32)
+    slots_kind = kept_in(slots_shape, f32)
     wide, slim = (heads, tokens, width), (heads, tokens, HEAD_SIZE)
     q, ko, vo, u = q[0, 0], ko[0, 0], vo[0, 0], u[0, 0]
 
     (payload,) = call(
         pack_kernel,
         0,
-        [(hbm, pinned(kp[0])), (hbm, pinned(vp[0]))],
-        [kept_in((2 * part, kv_width), bf16)],
+        [(scalar, payoffs), (hbm, pinned(kp[0])), (hbm, pinned(vp[0]))],
+        [kept_in((2 * part + EXTRA, kv_width), bf16)],
         [sems],
     )
     pays = [payload] + [swap(payload, n, k) for k in range(1, n)]
 
-    share = -(-n_prompt // n)
-    counts = []
-    for a in range(share):
-        perm = [
-            (p * n + m, (p ^ (m * share + a)) * n + m)
-            for p in range(n_prompt)
-            for m in range(n)
-            if m * share + a < n_prompt
-        ]
-        counts.append(lax.ppermute(kept, ("prompt", "resp"), perm))
-
-    small = [kept, spaces, spans, payoffs] + counts
+    def across(x, k):
+        return lax.ppermute(x, "prompt", [(i, i ^ k) for i in range(n_prompt)])
+
+    small = [kept, spaces, spans, across(kept, 1)]
     q_in, u_in, ko_in, vo_in, own, own_stat, tile, alive = call(
-        functools.partial(own_kernel, n, group, share),
+        functools.partial(own_kernel, group, 1),
         2,
         [(hbm, x) for x in small] + [(hbm, pinned(x)) for x in (q, u, ko, vo)],
         [kept_in(wide, bf16)] * 2
         + [kept_in(slim, bf16)] * 2
-        + [kept_in((heads, HEAD_SIZE, rows), f32), stat, tile_kind, tile_kind],
+        + [kept_in((heads, HEAD_SIZE, rows), f32), stat, tile_kind, slots_kind],
         [pltpu.SMEM(x.shape, x.dtype) for x in small]
         + [sems, pltpu.SemaphoreType.DMA((len(small),))],
     )
-    k = 1
-    while 4 * k < n:
-        tile = tile + swap(tile, n, k)
+    k = 2
+    while 4 * k < n_prompt:
+        tile = tile + across(tile, k)
         k *= 2
     att, ds, line, tile_sum, *terms = call(
         functools.partial(prefix_kernel, n),
         5,
-        [(vmem, x) for x in [q_in, u_in, own, own_stat, tile, swap(tile, n, k)] + pays],
+        [(vmem, x) for x in [q_in, u_in, own, own_stat, tile, across(tile, k)] + pays],
         [kept_in(wide, bf16), kept_in((heads, prefix, rows), bf16), stat, tile_kind]
         + [kept_in((2 * part, kv_width), f32 if i == 0 else bf16) for i in range(n)],
         [],
     )
-    other = swap(tile_sum, n, 2 * k)
+    other = across(tile_sum, 2 * k)
     received = [swap(t, n, i) for i, t in enumerate(terms) if i > 0]
     attn_out, dq, dko, dvo, weights = call(
         functools.partial(rest_kernel, n, group),
         6,
         [(vmem, x) for x in [q_in, u_in, ko_in, vo_in, att, ds, line, tile_sum, other, alive] + pays],
-        [given(q.shape), given(q.shape), given(ko.shape), given(ko.shape), tile_kind],
+        [given(q.shape), given(q.shape), given(ko.shape), given(ko.shape), slots_kind],
         [pltpu.VMEM(wide, bf16), pltpu.VMEM(slim, bf16), pltpu.VMEM(slim, bf16), sems],
     )
     key_total, value_total = call(

time: 41.4 us -> 34.7 us (0.84)
  starting transfers between devices: 20.1 us -> 13.2 us
  waiting for transfers between devices: 1.64 us -> 2.51 us
  Pallas kernels: 16.2 us -> 15.5 us
    ppermute x8 -> x6, starting transfers between devices: 18.2 us -> 8.09 us  [swap(): return lax.ppermute(x, 'resp', [(i, i ^ k) for i in range(n)])]
    ppermute x2 -> x3, starting transfers between devices: 1.85 us -> 5.11 us  [across(): return lax.ppermute(x, 'prompt', [(i, i ^ k) for i in range(n_prompt)])]
    ppermute x2 -> x3, waiting for transfers between devices: 0.01 us -> 1.71 us  [across(): return lax.ppermute(x, 'prompt', [(i, i ^ k) for i in range(n_prompt)])]
    ppermute x8 -> x6, waiting for transfers between devices: 1.63 us -> 0.8 us  [swap(): return lax.ppermute(x, 'resp', [(i, i ^ k) for i in range(n)])]
    pallas_call x5, Pallas kernels: 16.2 us -> 15.5 us  [call(): pl.pallas_call(kernel, in_specs=[spec for spec, _ in ins], out_specs=[spe...]
  transfers between devices with their start and end apart: 10 -> 9, of which waited for: 1 -> 3; matrix products, arithmetic and copies ran while one was open for 0% -> 0% of each run, Pallas kernels for 23% -> 26%
where the time goes in v4:
time: 34.7 us; the launch traced here: 34.5 us
  Pallas kernels  15.5 us (45%)
  starting transfers between devices  13.2 us (38%)
  between operations  2.63 us (8%)
  waiting for transfers between devices  2.51 us (7%)
  local copies, waits for them, and re-layouts  0.66 us (2%)
    pallas_call x5, Pallas kernels, call(): pl.pallas_call(kernel, in_specs=[spec for spec, _ in ins], out_specs=[spe...  15.5 us
    ppermute x6, starting transfers between devices, swap(): return lax.ppermute(x, 'resp', [(i, i ^ k) for i in range(n)])  8.09 us
    ppermute x3, starting transfers between devices, across(): return lax.ppermute(x, 'prompt', [(i, i ^ k) for i in range(n_prompt)])  5.11 us
    ppermute x3, waiting for transfers between devices, across(): return lax.ppermute(x, 'prompt', [(i, i ^ k) for i in range(n_prompt)])  1.71 us
    ppermute x6, waiting for transfers between devices, swap(): return lax.ppermute(x, 'resp', [(i, i ^ k) for i in range(n)])  0.8 us
  transfers between devices with their start and end apart: 9, of which 3 were waited for; matrix products, arithmetic and copies ran while one was open for 0% of the time, Pallas kernels for 26%

profile of v4, /device:TPU:0, one launch (start us, length us, event | category | flops | bytes accessed | tf_op | source)
XLA Modules:
  0.0 34.5 jit_solution(2079213829343121215)
XLA Ops:
  1.3 1.0 %shard_map.146.refs_6_.refs_10_ = bf16[144,512]{1,0:T(8,128)(2,1)S(1)} custom-call(f32[1,1]{1,0:T(1,128)S(6)} %copy.18.payoff_ref, bf16[64,512]{1,0:T(8,128)(2,1)} %bitcast.16, bf16[64,512]{1,0:T(8,128)(2,1)} %bitcast.17), custom_call_target="tpu_custom_call" | custom-call | bytes 1048576 | tf_op jit(solution)/shard_map/pallas_call | solution.py:274
  2.3 4.0 %collective-permute-start.4 = (bf16[144,512]{1,0:T(8,128)(2,1)S(1)}, bf16[144,512]{1,0:T(8,128)(2,1)S(1)}, u32[]{:S(2)}, u32[]{:S(2)}) collective-permute-start(bf16[144,512]{1,0:T(8,128)(2,1)S(1)} %shard_map.146.refs_6_.refs_10_), channel_id=1, source_target_pairs={{0,3},{1,2},{2,1},{3,0},{4,7},{5,6},{6,5},{7,4},{8,11},{9,10},{10,... | collective-permute-start | bytes 442376 | tf_op jit(solution)/shard_map/ppermute | solution.py:25
  6.3 0.5 %collective-permute-start.3 = (bf16[144,512]{1,0:T(8,128)(2,1)S(1)}, bf16[144,512]{1,0:T(8,128)(2,1)S(1)}, u32[]{:S(2)}, u32[]{:S(2)}) collective-permute-start(bf16[144,512]{1,0:T(8,128)(2,1)S(1)} %shard_map.146.refs_6_.refs_10_), channel_id=1, source_target_pairs={{0,2},{1,3},{2,0},{3,1},{4,6},{5,7},{6,4},{7,5},{8,10},{9,11},{10,... | collective-permute-start | bytes 442376 | tf_op jit(solution)/shard_map/ppermute | solution.py:25
  6.8 0.1 collective-permute-start.2
  6.9 0.0 collective-permute-start
  8.2 0.1 collective-permute-done.refs_3_
  8.3 0.7 %copy-done = s32[1,4]{1,0:T(1,128)S(1)} copy-done((s32[1,4]{1,0:T(1,128)S(1)}, s32[1,4]{1,0:T(1,128)}, u32[]{:S(2)}) %copy-start) | copy-done | bytes 40
  8.9 4.1 %shard_map.145 = (bf16[4,256,512]{2,1,0:T(8,128)(2,1)S(1)}, bf16[4,256,512]{2,1,0:T(8,128)(2,1)S(1)}, bf16[4,256,128]{2,1,0:T(8,128)(2,1)S(1)}, bf16[4,256,128]{...) custom-call(s32[1]{0:T(128)S(6)} %copy.16.refs_0_, ...), custom_call_target="tpu_custom_call" | custom-call | flops 536870912 | bytes 1048576 | tf_op jit(solution)/shard_map/pallas_call | solution.py:274
  13.1 2.0 %collective-permute-start.1 = (f32[8,128]{1,0:T(8,128)S(1)}, f32[8,128]{1,0:T(8,128)S(1)}, u32[]{:S(2)}, u32[]{:S(2)}) collective-permute-start(f32[8,128]{1,0:T(8,128)S(1)} %get-tuple-element.35.refs_4_), channel_id=1, source_target_pairs={{0,8},{4,12},{8,0},{12,4},{16,24},{20,28},{24,16},{28,20},{1,9},{5... | collective-permute-start | bytes 12296 | tf_op jit(solution)/shard_map/ppermute | solution.py:311
  15.1 1.6 %collective-permute-done.1.refs_5_ = f32[8,128]{1,0:T(8,128)S(1)} collective-permute-done((f32[8,128]{1,0:T(8,128)S(1)}, f32[8,128]{1,0:T(8,128)S(1)}, u32[]{:S(2)}, u32[]{:S(2)}) %collective-permute-start.1) | collective-permute-done | bytes 4128 | tf_op jit(solution)/shard_map/ppermute | solution.py:311
  16.8 0.0 collective-permute-done.4.refs_9_.refs_13_
  16.8 0.0 collective-permute-done.3.refs_8_.refs_12_
  16.8 0.0 collective-permute-done.2.refs_7_.refs_11_
  16.8 4.7 %shard_map.147 = (bf16[4,256,512]{2,1,0:T(8,128)(2,1)S(1)}, bf16[4,256,1024]{2,1,0:T(8,128)(2,1)S(1)}, f32[4,8,1024]{2,1,0:T(8,128)S(1)}, f32[8,128]{1,0:T(8,128...) custom-call(bf16[4,256,512]{2,1,0:T(8,128)(2,1)S(1)} %get-tuple-elem, ...), custom_call_target="tpu_custom_call" | custom-call | flops 1342177280 | bytes 1048576 | tf_op jit(solution)/shard_map/pallas_call | solution.py:274
  21.5 3.1 %collective-permute-start.5 = (f32[8,128]{1,0:T(8,128)S(1)}, f32[8,128]{1,0:T(8,128)S(1)}, u32[]{:S(2)}, u32[]{:S(2)}) collective-permute-start(f32[8,128]{1,0:T(8,128)S(1)} %get-tuple-element.39.refs_7_), channel_id=1, source_target_pairs={{0,16},{4,20},{8,24},{12,28},{16,0},{20,4},{24,8},{28,12},{1,17},{... | collective-permute-start | bytes 12296 | tf_op jit(solution)/shard_map/ppermute | solution.py:311
  24.5 1.5 %collective-permute-start.6 = (bf16[128,512]{1,0:T(8,128)(2,1)S(1)}, bf16[128,512]{1,0:T(8,128)(2,1)S(1)}, u32[]{:S(2)}, u32[]{:S(2)}) collective-permute-start(bf16[128,512]{1,0:T(8,128)(2,1)S(1)} %get-tuple-element.47), channel_id=1, source_target_pairs={{0,1},{1,0},{2,3},{3,2},{4,5},{5,4},{6,7},{7,6},{8,9},{9,8},{10,11... | collective-permute-start | bytes 393224 | tf_op jit(solution)/shard_map/ppermute | solution.py:25
  26.0 1.5 %collective-permute-start.7 = (bf16[128,512]{1,0:T(8,128)(2,1)S(1)}, bf16[128,512]{1,0:T(8,128)(2,1)S(1)}, u32[]{:S(2)}, u32[]{:S(2)}) collective-permute-start(bf16[128,512]{1,0:T(8,128)(2,1)S(1)} %get-tuple-element.48), channel_id=1, source_target_pairs={{0,2},{1,3},{2,0},{3,1},{4,6},{5,7},{6,4},{7,5},{8,10},{9,11},{10,... | collective-permute-start | bytes 393224 | tf_op jit(solution)/shard_map/ppermute | solution.py:25
  27.6 0.5 %collective-permute-start.8 = (bf16[128,512]{1,0:T(8,128)(2,1)S(1)}, bf16[128,512]{1,0:T(8,128)(2,1)S(1)}, u32[]{:S(2)}, u32[]{:S(2)}) collective-permute-start(bf16[128,512]{1,0:T(8,128)(2,1)S(1)} %get-tuple-element.49), channel_id=1, source_target_pairs={{0,3},{1,2},{2,1},{3,0},{4,7},{5,6},{6,5},{7,4},{8,11},{9,10},{10,... | collective-permute-start | bytes 393224 | tf_op jit(solution)/shard_map/ppermute | solution.py:25
  28.0 0.0 collective-permute-done.5.refs_8_
  28.0 4.9 %shard_map.148 = (bf16[256,2048]{1,0:T(8,128)(2,1)}, bf16[256,2048]{1,0:T(8,128)(2,1)}, bf16[256,512]{1,0:T(8,128)(2,1)}, bf16[256,512]{1,0:T(8,128)(2,1)}, f32[8,128]{1,0:T(8,128)S(1)}) custom-call(bf16[4,256,512]{2,1,0:T(8,128)(2,1)S(1)} %get-tuple-element.29.refs_0_, bf16[4,256,512]{2,1,0:T(8,128)(2,1)S(1)} %get-tuple-element.30.refs_1_, ...), custom_call_target="tpu_custom_call" | custom-call | flops 1610612736 | bytes 1048576 | tf_op jit(solution)/shard_map/pallas_call | solution.py:274
  32.9 0.0 collective-permute-done.6.refs_1_
  32.9 0.8 %collective-permute-done.7.refs_2_ = bf16[128,512]{1,0:T(8,128)(2,1)S(1)} collective-permute-done((bf16[128,512]{1,0:T(8,128)(2,1)S(1)}, bf16[128,512]{1,0:T(8,128)(2,1)S(1)}, u32[]{:S(2)}, u32[]{:S(2)}) %collective-permute-start.7) | collective-permute-done | bytes 131104 | tf_op jit(solution)/shard_map/ppermute | solution.py:25
  33.7 0.0 collective-permute-done.8.refs_3_
  33.7 0.7 %shard_map.149 = (bf16[64,512]{1,0:T(8,128)(2,1)}, bf16[64,512]{1,0:T(8,128)(2,1)}) custom-call(f32[8,128]{1,0:T(8,128)S(1)} %get-tuple-element.45.weights_ref, f32[128,512]{1,0:T(8,128)S(1)} %get-tuple-element.46.refs_0_, bf16[128,512]{1,0:T(8,128)(2,1)S(1)} %collective-permute-done.6.refs_1_, bf16[128,512]{1,0:T(8,128)(2,1)S(1)} %collective-permute-done.7.refs_2_, ...), custom_call_target="tpu_custom_call" | custom-call | bytes 1048576 | tf_op jit(solution)/shard_map/pallas_call | solution.py:274
  (1 shorter events, 0.0 us)
Async XLA Ops:
  2.3 14.5 %collective-permute-start.4 = (bf16[144,512]{1,0:T(8,128)(2,1)S(1)}, bf16[144,512]{1,0:T(8,128)(2,1)S(1)}, u32[]{:S(2)}, u32[]{:S(2)}) collective-permute-start(bf16[144,512]{1,0:T(8,128)(2,1)S(1)} %shard_map.146.refs_6_.refs_10_), channel_id=1, source_target_pairs={{0,3},{1,2},{2,1},{3,0},{4,7},{5,6},{6,5},{7,4},{8,11},{9,10},{10,... | collective-permute-start | bytes 442376 | tf_op jit(solution)/shard_map/ppermute | solution.py:25
  6.3 10.5 %collective-permute-start.3 = (bf16[144,512]{1,0:T(8,128)(2,1)S(1)}, bf16[144,512]{1,0:T(8,128)(2,1)S(1)}, u32[]{:S(2)}, u32[]{:S(2)}) collective-permute-start(bf16[144,512]{1,0:T(8,128)(2,1)S(1)} %shard_map.146.refs_6_.refs_10_), channel_id=1, source_target_pairs={{0,2},{1,3},{2,0},{3,1},{4,6},{5,7},{6,4},{7,5},{8,10},{9,11},{10,... | collective-permute-start | bytes 442376 | tf_op jit(solution)/shard_map/ppermute | solution.py:25
  6.8 10.0 %collective-permute-start.2 = (bf16[144,512]{1,0:T(8,128)(2,1)S(1)}, bf16[144,512]{1,0:T(8,128)(2,1)S(1)}, u32[]{:S(2)}, u32[]{:S(2)}) collective-permute-start(bf16[144,512]{1,0:T(8,128)(2,1)S(1)} %shard_map.146.refs_6_.refs_10_), channel_id=1, source_target_pairs={{0,1},{1,0},{2,3},{3,2},{4,5},{5,4},{6,7},{7,6},{8,9},{9,8},{10,11... | collective-permute-start | bytes 442376 | tf_op jit(solution)/shard_map/ppermute | solution.py:25
  6.9 1.4 %collective-permute-start = (s32[1]{0:T(128)}, s32[1]{0:T(128)}, u32[]{:S(2)}, u32[]{:S(2)}) collective-permute-start(s32[1]{0:T(128)} %param.16), channel_id=1, source_target_pairs={{0,4},{4,0},{8,12},{12,8},{16,20},{20,16},{24,28},{28,24},{1,5},{5... | collective-permute-start | bytes 20 | tf_op jit(solution)/shard_map/ppermute | solution.py:311
  8.3 0.7 %copy-start = (s32[1,4]{1,0:T(1,128)S(1)}, s32[1,4]{1,0:T(1,128)}, u32[]{:S(2)}) copy-start(s32[1,4]{1,0:T(1,128)} %refs_1_.1) | copy-start | bytes 52
  13.1 3.7 %collective-permute-start.1 = (f32[8,128]{1,0:T(8,128)S(1)}, f32[8,128]{1,0:T(8,128)S(1)}, u32[]{:S(2)}, u32[]{:S(2)}) collective-permute-start(f32[8,128]{1,0:T(8,128)S(1)} %get-tuple-element.35.refs_4_), channel_id=1, source_target_pairs={{0,8},{4,12},{8,0},{12,4},{16,24},{20,28},{24,16},{28,20},{1,9},{5... | collective-permute-start | bytes 12296 | tf_op jit(solution)/shard_map/ppermute | solution.py:311
  21.5 6.6 %collective-permute-start.5 = (f32[8,128]{1,0:T(8,128)S(1)}, f32[8,128]{1,0:T(8,128)S(1)}, u32[]{:S(2)}, u32[]{:S(2)}) collective-permute-start(f32[8,128]{1,0:T(8,128)S(1)} %get-tuple-element.39.refs_7_), channel_id=1, source_target_pairs={{0,16},{4,20},{8,24},{12,28},{16,0},{20,4},{24,8},{28,12},{1,17},{... | collective-permute-start | bytes 12296 | tf_op jit(solution)/shard_map/ppermute | solution.py:311
  24.5 8.4 %collective-permute-start.6 = (bf16[128,512]{1,0:T(8,128)(2,1)S(1)}, bf16[128,512]{1,0:T(8,128)(2,1)S(1)}, u32[]{:S(2)}, u32[]{:S(2)}) collective-permute-start(bf16[128,512]{1,0:T(8,128)(2,1)S(1)} %get-tuple-element.47), channel_id=1, source_target_pairs={{0,1},{1,0},{2,3},{3,2},{4,5},{5,4},{6,7},{7,6},{8,9},{9,8},{10,11... | collective-permute-start | bytes 393224 | tf_op jit(solution)/shard_map/ppermute | solution.py:25
  26.0 7.7 %collective-permute-start.7 = (bf16[128,512]{1,0:T(8,128)(2,1)S(1)}, bf16[128,512]{1,0:T(8,128)(2,1)S(1)}, u32[]{:S(2)}, u32[]{:S(2)}) collective-permute-start(bf16[128,512]{1,0:T(8,128)(2,1)S(1)} %get-tuple-element.48), channel_id=1, source_target_pairs={{0,2},{1,3},{2,0},{3,1},{4,6},{5,7},{6,4},{7,5},{8,10},{9,11},{10,... | collective-permute-start | bytes 393224 | tf_op jit(solution)/shard_map/ppermute | solution.py:25
  27.6 6.2 %collective-permute-start.8 = (bf16[128,512]{1,0:T(8,128)(2,1)S(1)}, bf16[128,512]{1,0:T(8,128)(2,1)S(1)}, u32[]{:S(2)}, u32[]{:S(2)}) collective-permute-start(bf16[128,512]{1,0:T(8,128)(2,1)S(1)} %get-tuple-element.49), channel_id=1, source_target_pairs={{0,3},{1,2},{2,1},{3,0},{4,7},{5,6},{6,5},{7,4},{8,11},{9,10},{10,... | collective-permute-start | bytes 393224 | tf_op jit(solution)/shard_map/ppermute | solution.py:25

commit v5 on v4

--- a/solution.py
+++ b/solution.py
@@ -135,13 +135,12 @@
 
 
 def prefix_kernel(n, *refs):
-    q_ref, u_ref, own_ref, stat_ref, tile_ref, recv_ref = refs[:6]
-    pay_refs = refs[6 : 6 + n]
-    out_ref, ds_ref, line_ref, sum_ref = refs[6 + n : 10 + n]
-    term_refs = refs[10 + n :]
+    q_ref, u_ref, own_ref, stat_ref = refs[:4]
+    pay_refs = refs[4 : 4 + n]
+    out_ref, ds_ref, line_ref = refs[4 + n : 7 + n]
+    term_refs = refs[7 + n :]
     heads, tokens, width = q_ref.shape
     part = (pay_refs[0].shape[0] - EXTRA) // 2
-    sum_ref[...] = tile_ref[...] + recv_ref[...]
 
     def step(g, carry):
         cols = columns_of(g, HEAD_SIZE)
@@ -177,6 +176,10 @@
     lax.fori_loop(0, heads, step, 0)
 
 
+def add_kernel(tile_ref, recv_ref, after_ref, sum_ref):
+    sum_ref[...] = tile_ref[...] + recv_ref[...]
+
+
 def rest_kernel(n, group, *refs):
     q_ref, u_ref, ko_ref, vo_ref, att_ref, ds_ref, line_ref, sum_ref, recv_ref, alive_ref = refs[:10]
     pay_refs = refs[10 : 10 + n]
@@ -310,7 +313,7 @@
     def across(x, k):
         return lax.ppermute(x, "prompt", [(i, i ^ k) for i in range(n_prompt)])
 
-    small = [kept, spaces, spans, across(kept, 1)]
+    small = [kept, pinned(spaces), spans, across(kept, 1)]
     q_in, u_in, ko_in, vo_in, own, own_stat, tile, alive = call(
         functools.partial(own_kernel, group, 1),
         2,
@@ -325,13 +328,17 @@
     while 4 * k < n_prompt:
         tile = tile + across(tile, k)
         k *= 2
-    att, ds, line, tile_sum, *terms = call(
+    arriving = across(tile, k)
+    att, ds, line, *terms = call(
         functools.partial(prefix_kernel, n),
         5,
-        [(vmem, x) for x in [q_in, u_in, own, own_stat, tile, across(tile, k)] + pays],
-        [kept_in(wide, bf16), kept_in((heads, prefix, rows), bf16), stat, tile_kind]
+        [(vmem, x) for x in [q_in, u_in, own, own_stat] + pays],
+        [kept_in(wide, bf16), kept_in((heads, prefix, rows), bf16), stat]
         + [kept_in((2 * part, kv_width), f32 if i == 0 else bf16) for i in range(n)],
         [],
+    )
+    (tile_sum,) = call(
+        add_kernel, 0, [(vmem, tile), (vmem, arriving), (hbm, line)], [tile_kind], []
     )
     other = across(tile_sum, 2 * k)
     received = [swap(t, n, i) for i, t in enumerate(terms) if i > 0]

time: 34.7 us -> 32.2 us (0.928)
  waiting for transfers between devices: 2.51 us -> 1.07 us
  local copies, waits for them, and re-layouts: 0.66 us -> 0 us
  starting transfers between devices: 13.2 us -> 12.8 us
    ppermute x3, waiting for transfers between devices: 1.71 us -> 0.09 us  [across(): return lax.ppermute(x, 'prompt', [(i, i ^ k) for i in range(n_prompt)])]
    unnamed x2 -> x0, local copies, waits for them, and re-layouts: 0.66 us -> none
    ppermute x3, starting transfers between devices: 5.11 us -> 4.7 us  [across(): return lax.ppermute(x, 'prompt', [(i, i ^ k) for i in range(n_prompt)])]
    pallas_call x5 -> x6, Pallas kernels: 15.5 us -> 15.5 us  [call(): pl.pallas_call(kernel, in_specs=[spec for spec, _ in ins], out_specs=[spe...]
  transfers between devices with their start and end apart: 9 -> 9, of which waited for: 3 -> 2; matrix products, arithmetic and copies ran while one was open for 0% -> 0% of each run, Pallas kernels for 26% -> 43%
where the time goes in v5:
time: 32.2 us; the launch traced here: 32 us
  Pallas kernels  15.5 us (48%)
  starting transfers between devices  12.8 us (40%)
  between operations  2.64 us (8%)
  waiting for transfers between devices  1.07 us (3%)
    pallas_call x6, Pallas kernels, call(): pl.pallas_call(kernel, in_specs=[spec for spec, _ in ins], out_specs=[spe...  15.5 us
    ppermute x6, starting transfers between devices, swap(): return lax.ppermute(x, 'resp', [(i, i ^ k) for i in range(n)])  8.09 us
    ppermute x3, starting transfers between devices, across(): return lax.ppermute(x, 'prompt', [(i, i ^ k) for i in range(n_prompt)])  4.7 us
    ppermute x6, waiting for transfers between devices, swap(): return lax.ppermute(x, 'resp', [(i, i ^ k) for i in range(n)])  0.98 us
  transfers between devices with their start and end apart: 9, of which 2 were waited for; matrix products, arithmetic and copies ran while one was open for 0% of the time, Pallas kernels for 43%

profile of v5, /device:TPU:0, one launch (start us, length us, event | category | flops | bytes accessed | tf_op | source)
XLA Modules:
  0.0 32.0 jit_solution(3013787509301076219)
XLA Ops:
  1.3 1.0 %shard_map.146.refs_4_.refs_10_ = bf16[144,512]{1,0:T(8,128)(2,1)S(1)} custom-call(f32[1,1]{1,0:T(1,128)S(6)} %copy.18.payoff_ref, bf16[64,512]{1,0:T(8,128)(2,1)} %bitcast.16, bf16[64,512]{1,0:T(8,128)(2,1)} %bitcast.17), custom_call_target="tpu_custom_call" | custom-call | bytes 1048576 | tf_op jit(solution)/shard_map/pallas_call | solution.py:277
  2.3 4.0 %collective-permute-start.3 = (bf16[144,512]{1,0:T(8,128)(2,1)S(1)}, bf16[144,512]{1,0:T(8,128)(2,1)S(1)}, u32[]{:S(2)}, u32[]{:S(2)}) collective-permute-start(bf16[144,512]{1,0:T(8,128)(2,1)S(1)} %shard_map.146.refs_4_.refs_10_), channel_id=1, source_target_pairs={{0,3},{1,2},{2,1},{3,0},{4,7},{5,6},{6,5},{7,4},{8,11},{9,10},{10,... | collective-permute-start | bytes 442376 | tf_op jit(solution)/shard_map/ppermute | solution.py:25
  6.3 0.5 %collective-permute-start.2 = (bf16[144,512]{1,0:T(8,128)(2,1)S(1)}, bf16[144,512]{1,0:T(8,128)(2,1)S(1)}, u32[]{:S(2)}, u32[]{:S(2)}) collective-permute-start(bf16[144,512]{1,0:T(8,128)(2,1)S(1)} %shard_map.146.refs_4_.refs_10_), channel_id=1, source_target_pairs={{0,2},{1,3},{2,0},{3,1},{4,6},{5,7},{6,4},{7,5},{8,10},{9,11},{10,... | collective-permute-start | bytes 442376 | tf_op jit(solution)/shard_map/ppermute | solution.py:25
  6.8 0.1 collective-permute-start.1
  6.9 0.0 collective-permute-start
  8.2 0.1 collective-permute-done.refs_3_
  8.3 4.2 %shard_map.145 = (bf16[4,256,512]{2,1,0:T(8,128)(2,1)S(1)}, bf16[4,256,512]{2,1,0:T(8,128)(2,1)S(1)}, bf16[4,256,128]{2,1,0:T(8,128)(2,1)S(1)}, bf16[4,256,128]{...) custom-call(s32[1]{0:T(128)S(6)} %copy.16.refs_0_, ...), custom_call_target="tpu_custom_call" | custom-call | flops 536870912 | bytes 1048576 | tf_op jit(solution)/shard_map/pallas_call | solution.py:277
  12.5 2.0 %collective-permute-start.4 = (f32[8,128]{1,0:T(8,128)S(1)}, f32[8,128]{1,0:T(8,128)S(1)}, u32[]{:S(2)}, u32[]{:S(2)}) collective-permute-start(f32[8,128]{1,0:T(8,128)S(1)} %get-tuple-element.37.tile_ref), channel_id=1, source_target_pairs={{0,8},{4,12},{8,0},{12,4},{16,24},{20,28},{24,16},{28,20},{1,9},{5... | collective-permute-start | bytes 12296 | tf_op jit(solution)/shard_map/ppermute | solution.py:314
  14.5 0.0 collective-permute-done.3.refs_7_.refs_13_
  14.5 0.0 collective-permute-done.2.refs_6_.refs_12_
  14.6 0.0 collective-permute-done.1.refs_5_.refs_11_
  14.6 4.7 %shard_map.147 = (bf16[4,256,512]{2,1,0:T(8,128)(2,1)S(1)}, bf16[4,256,1024]{2,1,0:T(8,128)(2,1)S(1)}, f32[4,8,1024]{2,1,0:T(8,128)S(1)}, f32[128,512]{1,0:T(8,1...) custom-call(bf16[4,256,512]{2,1,0:T(8,128)(2,1)S(1)} %get-tuple-element.28.refs_0_, ...), custom_call_target="tpu_custom_call" | custom-call | flops 1342177280 | bytes 1048576 | tf_op jit(solution)/shard_map/pallas_call | solution.py:277
  19.2 0.0 collective-permute-done.4.recv_ref
  19.3 2.6 %collective-permute-start.5 = (f32[8,128]{1,0:T(8,128)S(1)}, f32[8,128]{1,0:T(8,128)S(1)}, u32[]{:S(2)}, u32[]{:S(2)}) collective-permute-start(f32[8,128]{1,0:T(8,128)S(1)} %shard_map.148.refs_7_), channel_id=1, source_target_pairs={{0,16},{4,20},{8,24},{12,28},{16,0},{20,4},{24,8},{28,12},{1,17},{... | collective-permute-start | bytes 12296 | tf_op jit(solution)/shard_map/ppermute | solution.py:314
  21.9 1.5 %collective-permute-start.6 = (bf16[128,512]{1,0:T(8,128)(2,1)S(1)}, bf16[128,512]{1,0:T(8,128)(2,1)S(1)}, u32[]{:S(2)}, u32[]{:S(2)}) collective-permute-start(bf16[128,512]{1,0:T(8,128)(2,1)S(1)} %get-tuple-element.45), channel_id=1, source_target_pairs={{0,1},{1,0},{2,3},{3,2},{4,5},{5,4},{6,7},{7,6},{8,9},{9,8},{10,11... | collective-permute-start | bytes 393224 | tf_op jit(solution)/shard_map/ppermute | solution.py:25
  23.4 1.5 %collective-permute-start.7 = (bf16[128,512]{1,0:T(8,128)(2,1)S(1)}, bf16[128,512]{1,0:T(8,128)(2,1)S(1)}, u32[]{:S(2)}, u32[]{:S(2)}) collective-permute-start(bf16[128,512]{1,0:T(8,128)(2,1)S(1)} %get-tuple-element.46), channel_id=1, source_target_pairs={{0,2},{1,3},{2,0},{3,1},{4,6},{5,7},{6,4},{7,5},{8,10},{9,11},{10,... | collective-permute-start | bytes 393224 | tf_op jit(solution)/shard_map/ppermute | solution.py:25
  24.9 0.5 %collective-permute-start.8 = (bf16[128,512]{1,0:T(8,128)(2,1)S(1)}, bf16[128,512]{1,0:T(8,128)(2,1)S(1)}, u32[]{:S(2)}, u32[]{:S(2)}) collective-permute-start(bf16[128,512]{1,0:T(8,128)(2,1)S(1)} %get-tuple-element.47), channel_id=1, source_target_pairs={{0,3},{1,2},{2,1},{3,0},{4,7},{5,6},{6,5},{7,4},{8,11},{9,10},{10,... | collective-permute-start | bytes 393224 | tf_op jit(solution)/shard_map/ppermute | solution.py:25
  25.4 0.0 collective-permute-done.5.refs_8_
  25.4 4.9 %shard_map.149 = (bf16[256,2048]{1,0:T(8,128)(2,1)}, bf16[256,2048]{1,0:T(8,128)(2,1)}, bf16[256,512]{1,0:T(8,128)(2,1)}, bf16[256,512]{1,0:T(8,128)(2,1)}, f32[8,128]{1,0:T(8,128)S(1)}) custom-call(bf16[4,256,512]{2,1,0:T(8,128)(2,1)S(1)} %get-tuple-element.28.refs_0_, bf16[4,256,512]{2,1,0:T(8,128)(2,1)S(1)} %get-tuple-element.29.refs_1_, ...), custom_call_target="tpu_custom_call" | custom-call | flops 1610612736 | bytes 1048576 | tf_op jit(solution)/shard_map/pallas_call | solution.py:277
  30.3 0.0 collective-permute-done.6.refs_1_
  30.3 1.0 %collective-permute-done.7.refs_2_ = bf16[128,512]{1,0:T(8,128)(2,1)S(1)} collective-permute-done((bf16[128,512]{1,0:T(8,128)(2,1)S(1)}, bf16[128,512]{1,0:T(8,128)(2,1)S(1)}, u32[]{:S(2)}, u32[]{:S(2)}) %collective-permute-start.7) | collective-permute-done | bytes 131104 | tf_op jit(solution)/shard_map/ppermute | solution.py:25
  31.2 0.0 collective-permute-done.8.refs_3_
  31.2 0.7 %shard_map.150 = (bf16[64,512]{1,0:T(8,128)(2,1)}, bf16[64,512]{1,0:T(8,128)(2,1)}) custom-call(f32[8,128]{1,0:T(8,128)S(1)} %get-tuple-element.43.weights_ref, f32[128,512]{1,0:T(8,128)S(1)} %get-tuple-element.44.refs_0_, bf16[128,512]{1,0:T(8,128)(2,1)S(1)} %collective-permute-done.6.refs_1_, bf16[128,512]{1,0:T(8,128)(2,1)S(1)} %collective-permute-done.7.refs_2_, ...), custom_call_target="tpu_custom_call" | custom-call | bytes 1048576 | tf_op jit(solution)/shard_map/pallas_call | solution.py:277
  (1 shorter events, 0.0 us)
Async XLA Ops:
  2.3 12.2 %collective-permute-start.3 = (bf16[144,512]{1,0:T(8,128)(2,1)S(1)}, bf16[144,512]{1,0:T(8,128)(2,1)S(1)}, u32[]{:S(2)}, u32[]{:S(2)}) collective-permute-start(bf16[144,512]{1,0:T(8,128)(2,1)S(1)} %shard_map.146.refs_4_.refs_10_), channel_id=1, source_target_pairs={{0,3},{1,2},{2,1},{3,0},{4,7},{5,6},{6,5},{7,4},{8,11},{9,10},{10,... | collective-permute-start | bytes 442376 | tf_op jit(solution)/shard_map/ppermute | solution.py:25
  6.3 8.3 %collective-permute-start.2 = (bf16[144,512]{1,0:T(8,128)(2,1)S(1)}, bf16[144,512]{1,0:T(8,128)(2,1)S(1)}, u32[]{:S(2)}, u32[]{:S(2)}) collective-permute-start(bf16[144,512]{1,0:T(8,128)(2,1)S(1)} %shard_map.146.refs_4_.refs_10_), channel_id=1, source_target_pairs={{0,2},{1,3},{2,0},{3,1},{4,6},{5,7},{6,4},{7,5},{8,10},{9,11},{10,... | collective-permute-start | bytes 442376 | tf_op jit(solution)/shard_map/ppermute | solution.py:25
  6.8 7.8 %collective-permute-start.1 = (bf16[144,512]{1,0:T(8,128)(2,1)S(1)}, bf16[144,512]{1,0:T(8,128)(2,1)S(1)}, u32[]{:S(2)}, u32[]{:S(2)}) collective-permute-start(bf16[144,512]{1,0:T(8,128)(2,1)S(1)} %shard_map.146.refs_4_.refs_10_), channel_id=1, source_target_pairs={{0,1},{1,0},{2,3},{3,2},{4,5},{5,4},{6,7},{7,6},{8,9},{9,8},{10,11... | collective-permute-start | bytes 442376 | tf_op jit(solution)/shard_map/ppermute | solution.py:25
  6.9 1.4 %collective-permute-start = (s32[1]{0:T(128)}, s32[1]{0:T(128)}, u32[]{:S(2)}, u32[]{:S(2)}) collective-permute-start(s32[1]{0:T(128)} %param.16), channel_id=1, source_target_pairs={{0,4},{4,0},{8,12},{12,8},{16,20},{20,16},{24,28},{28,24},{1,5},{5... | collective-permute-start | bytes 20 | tf_op jit(solution)/shard_map/ppermute | solution.py:314
  12.5 6.7 %collective-permute-start.4 = (f32[8,128]{1,0:T(8,128)S(1)}, f32[8,128]{1,0:T(8,128)S(1)}, u32[]{:S(2)}, u32[]{:S(2)}) collective-permute-start(f32[8,128]{1,0:T(8,128)S(1)} %get-tuple-element.37.tile_ref), channel_id=1, source_target_pairs={{0,8},{4,12},{8,0},{12,4},{16,24},{20,28},{24,16},{28,20},{1,9},{5... | collective-permute-start | bytes 12296 | tf_op jit(solution)/shard_map/ppermute | solution.py:314
  19.3 6.1 %collective-permute-start.5 = (f32[8,128]{1,0:T(8,128)S(1)}, f32[8,128]{1,0:T(8,128)S(1)}, u32[]{:S(2)}, u32[]{:S(2)}) collective-permute-start(f32[8,128]{1,0:T(8,128)S(1)} %shard_map.148.refs_7_), channel_id=1, source_target_pairs={{0,16},{4,20},{8,24},{12,28},{16,0},{20,4},{24,8},{28,12},{1,17},{... | collective-permute-start | bytes 12296 | tf_op jit(solution)/shard_map/ppermute | solution.py:314
  21.9 8.4 %collective-permute-start.6 = (bf16[128,512]{1,0:T(8,128)(2,1)S(1)}, bf16[128,512]{1,0:T(8,128)(2,1)S(1)}, u32[]{:S(2)}, u32[]{:S(2)}) collective-permute-start(bf16[128,512]{1,0:T(8,128)(2,1)S(1)} %get-tuple-element.45), channel_id=1, source_target_pairs={{0,1},{1,0},{2,3},{3,2},{4,5},{5,4},{6,7},{7,6},{8,9},{9,8},{10,11... | collective-permute-start | bytes 393224 | tf_op jit(solution)/shard_map/ppermute | solution.py:25
  23.4 7.8 %collective-permute-start.7 = (bf16[128,512]{1,0:T(8,128)(2,1)S(1)}, bf16[128,512]{1,0:T(8,128)(2,1)S(1)}, u32[]{:S(2)}, u32[]{:S(2)}) collective-permute-start(bf16[128,512]{1,0:T(8,128)(2,1)S(1)} %get-tuple-element.46), channel_id=1, source_target_pairs={{0,2},{1,3},{2,0},{3,1},{4,6},{5,7},{6,4},{7,5},{8,10},{9,11},{10,... | collective-permute-start | bytes 393224 | tf_op jit(solution)/shard_map/ppermute | solution.py:25
  24.9 6.3 %collective-permute-start.8 = (bf16[128,512]{1,0:T(8,128)(2,1)S(1)}, bf16[128,512]{1,0:T(8,128)(2,1)S(1)}, u32[]{:S(2)}, u32[]{:S(2)}) collective-permute-start(bf16[128,512]{1,0:T(8,128)(2,1)S(1)} %get-tuple-element.47), channel_id=1, source_target_pairs={{0,3},{1,2},{2,1},{3,0},{4,7},{5,6},{6,5},{7,4},{8,11},{9,10},{10,... | collective-permute-start | bytes 393224 | tf_op jit(solution)/shard_map/ppermute | solution.py:25

commit v6 on v5

--- a/solution.py
+++ b/solution.py
@@ -36,13 +36,21 @@
 
 def unstacked(x, tokens):
     x = x.astype(bf16)
-    return jnp.concatenate([x[:, i : i + tokens].T for i in range(0, x.shape[1], tokens)], 1)
+    return jnp.concatenate([x[i : i + tokens] for i in range(0, x.shape[0], tokens)], 1)
+
+
+def spread(x, width):
+    return jnp.concatenate([x] * (width // HEAD_SIZE), 1)
+
+
+def with_ones(values):
+    return jnp.concatenate([values, jnp.ones(values.shape, bf16)], 1)
 
 
 def causal_mask(tokens, group):
-    key = lax.broadcasted_iota(i32, (tokens, tokens), 0)
-    row = lax.broadcasted_iota(i32, (tokens, tokens), 1)
-    return jnp.concatenate([key <= row] * group, 1)
+    row = lax.broadcasted_iota(i32, (tokens, tokens), 0)
+    key = lax.broadcasted_iota(i32, (tokens, tokens), 1)
+    return jnp.concatenate([key <= row] * group, 0)
 
 
 def row_of(tile, index):
@@ -72,8 +80,8 @@
 def own_kernel(group, counts, *refs):
     small_hbm, refs = refs[: 3 + counts], refs[3 + counts :]
     q_hbm, u_hbm, ko_hbm, vo_hbm = refs[:4]
-    q_ref, u_ref, ko_ref, vo_ref, att_ref, stat_ref, tile_ref, alive_ref = refs[4:12]
-    small_refs, sems, small_sems = refs[12:-2], refs[-2], refs[-1]
+    q_ref, u_ref, ko_ref, vo_ref, att_ref, lse_ref, tile_ref, alive_ref, length_ref = refs[4:13]
+    small_refs, sems, small_sems = refs[13:-2], refs[-2], refs[-1]
     heads, tokens, width = q_ref.shape
 
     def loads(g):
@@ -112,68 +120,71 @@
     alive_ref[...] = alive
     count = kept + sum(r[0] for r in small_refs[3:])
     tile_ref[...] = jnp.full(tile_ref.shape, count.astype(f32))
-    token = lax.broadcasted_iota(i32, (1, tokens), 1)
-    valid = jnp.where(token < own_alive * spans_ref[0, 0] * BLOCK, 1.0, 0.0)
-    valid = jnp.concatenate([valid] * group, 1)
-
-    def step(g, carry):
+    length = own_alive * spans_ref[0, 0] * BLOCK
+    length_ref[...] = jnp.full(length_ref.shape, length.astype(f32))
+
+    for g in range(heads):
         for copy in loads(g):
             copy.wait()
-        s = dot(ko_ref[g], stacked(q_ref[g]), 1, 1)
+
+    def step(g, carry):
+        s = dot(stacked(q_ref[g]), ko_ref[g], 1, 1)
         s = jnp.where(causal_mask(tokens, group), s, -1e30)
-        top = jnp.max(s, 0, keepdims=True)
-        e = jnp.exp2((s - top) * POWER)
-        stat_ref[g, 0:1] = top
-        stat_ref[g, 1:2] = jnp.sum(e, 0, keepdims=True)
-        stat_ref[g, 2:3] = valid
-        att_ref[g] = dot(vo_ref[g], e.astype(bf16), 0, 0)
+        top = jnp.max(s, 1, keepdims=True) * POWER
+        e = jnp.exp2(s * POWER - top)
+        both = dot(e.astype(bf16), with_ones(vo_ref[g]), 1, 0)
+        mass = both[:, HEAD_SIZE:]
+        att_ref[g] = both[:, :HEAD_SIZE] / mass
+        lse_ref[g] = jnp.log2(mass) + top
         return carry
 
-    lax.fori_loop(0, heads, step, 0)
+    lax.fori_loop(0, heads, step, 0, unroll=True)
     for g in range(heads):
         late_load(g).wait()
 
 
 def prefix_kernel(n, *refs):
-    q_ref, u_ref, own_ref, stat_ref = refs[:4]
-    pay_refs = refs[4 : 4 + n]
-    out_ref, ds_ref, line_ref = refs[4 + n : 7 + n]
-    term_refs = refs[7 + n :]
+    q_ref, u_ref, own_ref, lse_ref, length_ref = refs[:5]
+    pay_refs = refs[5 : 5 + n]
+    out_ref, grad_ref, ds_ref, top_ref, delta_ref = refs[5 + n : 10 + n]
+    term_refs = refs[10 + n :]
     heads, tokens, width = q_ref.shape
+    group = width // HEAD_SIZE
     part = (pay_refs[0].shape[0] - EXTRA) // 2
+    token = lax.broadcasted_iota(i32, (tokens, HEAD_SIZE), 0).astype(f32)
+    valid = jnp.concatenate([token < length_ref[0:1]] * group, 0)
 
     def step(g, carry):
         cols = columns_of(g, HEAD_SIZE)
         keys = jnp.concatenate([r[:part, cols] for r in pay_refs], 0)
         values = jnp.concatenate([r[part : 2 * part, cols] for r in pay_refs], 0)
         q = stacked(q_ref[g])
-        u = stacked(u_ref[g])
-        s = dot(keys, q, 1, 1)
-        own_top = stat_ref[g, 0:1]
-        valid = stat_ref[g, 2:3] > 0.0
-        top = jnp.maximum(jnp.max(s, 0, keepdims=True), own_top)
-        e = jnp.exp2((s - top) * POWER)
-        shrink = jnp.exp2((own_top - top) * POWER)
-        mass = jnp.sum(e, 0, keepdims=True) + shrink * stat_ref[g, 1:2]
-        inverse = jnp.where(valid, 1.0 / mass, 0.0)
-        p = e * inverse
-        p_low = p.astype(bf16)
-        attended = dot(values, p_low, 0, 0) + own_ref[g] * (shrink * inverse)
+        s = dot(q, keys, 1, 1)
+        own_lse = lse_ref[g]
+        top = jnp.maximum(jnp.max(s, 1, keepdims=True) * POWER, own_lse)
+        e = jnp.exp2(s * POWER - spread(top, s.shape[1]))
+        e_low = e.astype(bf16)
+        both = dot(e_low, with_ones(values), 1, 0)
+        own_mass = jnp.exp2(own_lse - top)
+        inverse = jnp.where(valid, 1.0 / (both[:, HEAD_SIZE:] + own_mass), 0.0)
+        attended = (both[:, :HEAD_SIZE] + own_ref[g] * own_mass) * inverse
         out_ref[g] = unstacked(attended, tokens)
-        dp = dot(values, u, 1, 1)
-        delta = jnp.sum(u.T.astype(f32) * attended, 0, keepdims=True)
-        ds = (p * (dp - delta)).astype(bf16)
+        grad = (stacked(u_ref[g]).astype(f32) * inverse).astype(bf16)
+        grad_ref[g] = grad
+        dp = dot(grad, values, 1, 1)
+        delta = jnp.sum(grad.astype(f32) * attended, 1, keepdims=True)
+        ds = (e * (dp - delta)).astype(bf16)
         ds_ref[g] = ds
-        line_ref[g, 0:1] = jnp.where(valid, top * POWER + jnp.log2(mass), 1e30)
-        line_ref[g, 1:2] = delta
-        dk = dot(ds, q, 1, 0) * SCALING
-        dv = dot(p_low, u, 1, 0)
+        top_ref[g] = top
+        delta_ref[g] = jnp.broadcast_to(delta, top.shape)
+        dk = dot(q, ds, 0, 0).T * SCALING
+        dv = dot(grad, e_low, 0, 0).T
         for k, ref in enumerate(term_refs):
             ref[:part, cols] = dk[k * part : (k + 1) * part].astype(ref.dtype)
-            ref[part:, cols] = dv[k * part : (k + 1) * part].astype(ref.dtype)
+            ref[part : 2 * part, cols] = dv[k * part : (k + 1) * part].astype(ref.dtype)
         return carry
 
-    lax.fori_loop(0, heads, step, 0)
+    lax.fori_loop(0, heads, step, 0, unroll=True)
 
 
 def add_kernel(tile_ref, recv_ref, after_ref, sum_ref):
@@ -181,10 +192,11 @@
 
 
 def rest_kernel(n, group, *refs):
-    q_ref, u_ref, ko_ref, vo_ref, att_ref, ds_ref, line_ref, sum_ref, recv_ref, alive_ref = refs[:10]
-    pay_refs = refs[10 : 10 + n]
-    out_hbm, dq_hbm, dko_hbm, dvo_hbm, weights_ref = refs[10 + n : 15 + n]
-    dq_ref, dko_ref, dvo_ref, sems = refs[15 + n :]
+    q_ref, grad_ref, ko_ref, vo_ref, att_ref, ds_ref, top_ref, delta_ref = refs[:8]
+    sum_ref, recv_ref, alive_ref = refs[8:11]
+    pay_refs = refs[11 : 11 + n]
+    out_hbm, dq_hbm, dko_hbm, dvo_hbm, weights_ref = refs[11 + n : 16 + n]
+    dq_ref, dko_ref, dvo_ref, sems = refs[16 + n :]
     heads, tokens, width = q_ref.shape
     part = (pay_refs[0].shape[0] - EXTRA) // 2
 
@@ -213,28 +225,27 @@
     for k in range(n):
         weights_ref[k : k + 1] = weights[k]
     weight = weights[0]
-    weight_rows = jnp.concatenate([weight] * (group * tokens // HEAD_SIZE), 1)
 
     def step(g, carry):
         cols = columns_of(g, HEAD_SIZE)
         keys = jnp.concatenate([r[:part, cols] for r in pay_refs], 0)
         q = stacked(q_ref[g])
-        u = stacked(u_ref[g])
         ko, vo = ko_ref[g], vo_ref[g]
-        s = dot(ko, q, 1, 1)
-        s = jnp.where(causal_mask(tokens, group), s, -1e30)
-        p = jnp.exp2(s * POWER - line_ref[g, 0:1])
-        dp = dot(vo, u, 1, 1)
-        ds = (p * (dp - line_ref[g, 1:2])).astype(bf16)
-        dq = dot(keys, ds_ref[g], 0, 0) + dot(ko, ds, 0, 0)
-        dq_ref[g] = unstacked(dq * (weight_rows * SCALING), tokens)
-        dko_ref[g] = (dot(ds, q, 1, 0) * (weight * SCALING)).astype(bf16)
-        dvo_ref[g] = (dot(p.astype(bf16), u, 1, 0) * weight).astype(bf16)
+        grad = grad_ref[g]
+        s = dot(q, ko, 1, 1) * POWER - spread(top_ref[g], tokens)
+        e = jnp.exp2(jnp.where(causal_mask(tokens, group), s, -1e30))
+        dp = dot(grad, vo, 1, 1)
+        ds = (e * (dp - spread(delta_ref[g], tokens))).astype(bf16)
+        all_ds = jnp.concatenate([ds_ref[g], ds], 1)
+        dq = dot(all_ds, jnp.concatenate([keys, ko], 0), 1, 0)
+        dq_ref[g] = unstacked(dq * (weight * SCALING), tokens)
+        dko_ref[g] = (dot(q, ds, 0, 0).T * (weight * SCALING)).astype(bf16)
+        dvo_ref[g] = (dot(grad, e.astype(bf16), 0, 0).T * weight).astype(bf16)
         for copy in stores(g):
             copy.start()
         return carry
 
-    lax.fori_loop(0, heads, step, 0)
+    lax.fori_loop(0, heads, step, 0, unroll=True)
     for g in range(heads):
         early_store(g).wait()
         for copy in stores(g):
@@ -295,7 +306,7 @@
         return (spec, jax.ShapeDtypeStruct(shape, kind))
 
     sems = pltpu.SemaphoreType.DMA((4, heads))
-    stat = kept_in((heads, 8, rows), f32)
+    stat = kept_in((heads, rows, HEAD_SIZE), f32)
     tile_kind = kept_in(tile_shape, f32)
     slots_kind = kept_in(slots_shape, f32)
     wide, slim = (heads, tokens, width), (heads, tokens, HEAD_SIZE)
@@ -314,13 +325,13 @@
         return lax.ppermute(x, "prompt", [(i, i ^ k) for i in range(n_prompt)])
 
     small = [kept, pinned(spaces), spans, across(kept, 1)]
-    q_in, u_in, ko_in, vo_in, own, own_stat, tile, alive = call(
+    q_in, u_in, ko_in, vo_in, own, own_lse, tile, alive, length = call(
         functools.partial(own_kernel, group, 1),
         2,
         [(hbm, x) for x in small] + [(hbm, pinned(x)) for x in (q, u, ko, vo)],
         [kept_in(wide, bf16)] * 2
         + [kept_in(slim, bf16)] * 2
-        + [kept_in((heads, HEAD_SIZE, rows), f32), stat, tile_kind, slots_kind],
+        + [stat, stat, tile_kind, slots_kind, tile_kind],
         [pltpu.SMEM(x.shape, x.dtype) for x in small]
         + [sems, pltpu.SemaphoreType.DMA((len(small),))],
     )
@@ -329,23 +340,24 @@
         tile = tile + across(tile, k)
         k *= 2
     arriving = across(tile, k)
-    att, ds, line, *terms = call(
+    att, grad, ds, top, delta, *terms = call(
         functools.partial(prefix_kernel, n),
         5,
-        [(vmem, x) for x in [q_in, u_in, own, own_stat] + pays],
-        [kept_in(wide, bf16), kept_in((heads, prefix, rows), bf16), stat]
+        [(vmem, x) for x in [q_in, u_in, own, own_lse, length] + pays],
+        [kept_in(wide, bf16), kept_in((heads, rows, HEAD_SIZE), bf16)]
+        + [kept_in((heads, rows, prefix), bf16), stat, stat]
         + [kept_in((2 * part, kv_width), f32 if i == 0 else bf16) for i in range(n)],
         [],
     )
     (tile_sum,) = call(
-        add_kernel, 0, [(vmem, tile), (vmem, arriving), (hbm, line)], [tile_kind], []
+        add_kernel, 0, [(vmem, tile), (vmem, arriving), (hbm, top)], [tile_kind], []
     )
     other = across(tile_sum, 2 * k)
     received = [swap(t, n, i) for i, t in enumerate(terms) if i > 0]
     attn_out, dq, dko, dvo, weights = call(
         functools.partial(rest_kernel, n, group),
         6,
-        [(vmem, x) for x in [q_in, u_in, ko_in, vo_in, att, ds, line, tile_sum, other, alive] + pays],
+        [(vmem, x) for x in [q_in, grad, ko_in, vo_in, att, ds, top, delta, tile_sum, other, alive] + pays],
         [given(q.shape), given(q.shape), given(ko.shape), given(ko.shape), slots_kind],
         [pltpu.VMEM(wide, bf16), pltpu.VMEM(slim, bf16), pltpu.VMEM(slim, bf16), sems],
     )

time: 32.2 us -> 31.1 us (0.966)
  Pallas kernels: 15.5 us -> 13.4 us
  waiting for transfers between devices: 1.07 us -> 1.96 us
    pallas_call x6, Pallas kernels: 15.5 us -> 13.4 us  [call(): pl.pallas_call(kernel, in_specs=[spec for spec, _ in ins], out_specs=[spe...]
    ppermute x6, waiting for transfers between devices: 0.98 us -> 1.87 us  [swap(): return lax.ppermute(x, 'resp', [(i, i ^ k) for i in range(n)])]
  transfers between devices with their start and end apart: 9 -> 9, of which waited for: 2 -> 2; matrix products, arithmetic and copies ran while one was open for 0% -> 0% of each run, Pallas kernels for 43% -> 38%
where the time goes in v6:
time: 31.1 us; the launch traced here: 30.8 us
  Pallas kernels  13.4 us (43%)
  starting transfers between devices  12.8 us (41%)
  between operations  2.64 us (8%)
  waiting for transfers between devices  1.96 us (6%)
    pallas_call x6, Pallas kernels, call(): pl.pallas_call(kernel, in_specs=[spec for spec, _ in ins], out_specs=[spe...  13.4 us
    ppermute x6, starting transfers between devices, swap(): return lax.ppermute(x, 'resp', [(i, i ^ k) for i in range(n)])  8.03 us
    ppermute x3, starting transfers between devices, across(): return lax.ppermute(x, 'prompt', [(i, i ^ k) for i in range(n_prompt)])  4.76 us
    ppermute x6, waiting for transfers between devices, swap(): return lax.ppermute(x, 'resp', [(i, i ^ k) for i in range(n)])  1.87 us
  transfers between devices with their start and end apart: 9, of which 2 were waited for; matrix products, arithmetic and copies ran while one was open for 0% of the time, Pallas kernels for 38%

profile of v6, /device:TPU:0, one launch (start us, length us, event | category | flops | bytes accessed | tf_op | source)
XLA Modules:
  0.0 30.8 jit_solution(17079418996124551687)
XLA Ops:
  1.3 1.0 %shard_map.146.refs_5_.refs_11_ = bf16[144,512]{1,0:T(8,128)(2,1)S(1)} custom-call(f32[1,1]{1,0:T(1,128)S(6)} %copy.18.payoff_ref, bf16[64,512]{1,0:T(8,128)(2,1)} %bitcast.16, bf16[64,512]{1,0:T(8,128)(2,1)} %bitcast.17), custom_call_target="tpu_custom_call" | custom-call | bytes 1048576 | tf_op jit(solution)/shard_map/pallas_call | solution.py:288
  2.3 3.0 %collective-permute-start.1 = (bf16[144,512]{1,0:T(8,128)(2,1)S(1)}, bf16[144,512]{1,0:T(8,128)(2,1)S(1)}, u32[]{:S(2)}, u32[]{:S(2)}) collective-permute-start(bf16[144,512]{1,0:T(8,128)(2,1)S(1)} %shard_map.146.refs_5_.refs_11_), channel_id=1, source_target_pairs={{0,1},{1,0},{2,3},{3,2},{4,5},{5,4},{6,7},{7,6},{8,9},{9,8},{10,11... | collective-permute-start | bytes 442376 | tf_op jit(solution)/shard_map/ppermute | solution.py:25
  5.3 1.5 %collective-permute-start.2 = (bf16[144,512]{1,0:T(8,128)(2,1)S(1)}, bf16[144,512]{1,0:T(8,128)(2,1)S(1)}, u32[]{:S(2)}, u32[]{:S(2)}) collective-permute-start(bf16[144,512]{1,0:T(8,128)(2,1)S(1)} %shard_map.146.refs_5_.refs_11_), channel_id=1, source_target_pairs={{0,2},{1,3},{2,0},{3,1},{4,6},{5,7},{6,4},{7,5},{8,10},{9,11},{10,... | collective-permute-start | bytes 442376 | tf_op jit(solution)/shard_map/ppermute | solution.py:25
  6.8 0.0 collective-permute-start.3
  6.8 0.0 collective-permute-start
  8.1 0.1 collective-permute-done.refs_3_
  8.2 3.8 %shard_map.145 = (bf16[4,256,512]{2,1,0:T(8,128)(2,1)S(1)}, bf16[4,256,512]{2,1,0:T(8,128)(2,1)S(1)}, bf16[4,256,128]{2,1,0:T(8,128)(2,1)S(1)}, bf16[4,256,128]{...) custom-call(s32[1]{0:T(128)S(6)} %copy.16.refs_0_, ...), custom_call_target="tpu_custom_call" | custom-call | flops 536870912 | bytes 1048576 | tf_op jit(solution)/shard_map/pallas_call | solution.py:288
  12.0 2.1 %collective-permute-start.4 = (f32[8,128]{1,0:T(8,128)S(1)}, f32[8,128]{1,0:T(8,128)S(1)}, u32[]{:S(2)}, u32[]{:S(2)}) collective-permute-start(f32[8,128]{1,0:T(8,128)S(1)} %get-tuple-element.43.tile_ref), channel_id=1, source_target_pairs={{0,8},{4,12},{8,0},{12,4},{16,24},{20,28},{24,16},{28,20},{1,9},{5... | collective-permute-start | bytes 12296 | tf_op jit(solution)/shard_map/ppermute | solution.py:325
  14.1 0.0 collective-permute-done.1.refs_6_.refs_12_
  14.1 0.0 collective-permute-done.2.refs_7_.refs_13_
  14.1 0.0 collective-permute-done.3.refs_8_.refs_14_
  14.1 4.0 %shard_map.147 = (bf16[4,256,512]{2,1,0:T(8,128)(2,1)S(1)}, bf16[4,1024,128]{2,1,0:T(8,128)(2,1)S(1)}, bf16[4,1024,256]{2,1,0:T(8,128)(2,1)S(1)}, f32[4,1024,128...) custom-call(bf16[4,256,512]{2,1,0:T(8,128)(2,1)S(1)} %get-tuple-elem, ...), custom_call_target="tpu_custom_call" | custom-call | flops 1342177280 | bytes 1048576 | tf_op jit(solution)/shard_map/pallas_call | solution.py:288
  18.1 0.0 collective-permute-done.4.recv_ref
  18.1 2.7 %collective-permute-start.5 = (f32[8,128]{1,0:T(8,128)S(1)}, f32[8,128]{1,0:T(8,128)S(1)}, u32[]{:S(2)}, u32[]{:S(2)}) collective-permute-start(f32[8,128]{1,0:T(8,128)S(1)} %shard_map.148.refs_8_), channel_id=1, source_target_pairs={{0,16},{4,20},{8,24},{12,28},{16,0},{20,4},{24,8},{28,12},{1,17},{... | collective-permute-start | bytes 12296 | tf_op jit(solution)/shard_map/ppermute | solution.py:325
  20.8 1.5 %collective-permute-start.6 = (bf16[128,512]{1,0:T(8,128)(2,1)S(1)}, bf16[128,512]{1,0:T(8,128)(2,1)S(1)}, u32[]{:S(2)}, u32[]{:S(2)}) collective-permute-start(bf16[128,512]{1,0:T(8,128)(2,1)S(1)} %get-tuple-element.51), channel_id=1, source_target_pairs={{0,1},{1,0},{2,3},{3,2},{4,5},{5,4},{6,7},{7,6},{8,9},{9,8},{10,11... | collective-permute-start | bytes 393224 | tf_op jit(solution)/shard_map/ppermute | solution.py:25
  22.3 1.5 %collective-permute-start.7 = (bf16[128,512]{1,0:T(8,128)(2,1)S(1)}, bf16[128,512]{1,0:T(8,128)(2,1)S(1)}, u32[]{:S(2)}, u32[]{:S(2)}) collective-permute-start(bf16[128,512]{1,0:T(8,128)(2,1)S(1)} %get-tuple-element.52), channel_id=1, source_target_pairs={{0,2},{1,3},{2,0},{3,1},{4,6},{5,7},{6,4},{7,5},{8,10},{9,11},{10,... | collective-permute-start | bytes 393224 | tf_op jit(solution)/shard_map/ppermute | solution.py:25
  23.8 0.5 %collective-permute-start.8 = (bf16[128,512]{1,0:T(8,128)(2,1)S(1)}, bf16[128,512]{1,0:T(8,128)(2,1)S(1)}, u32[]{:S(2)}, u32[]{:S(2)}) collective-permute-start(bf16[128,512]{1,0:T(8,128)(2,1)S(1)} %get-tuple-element.53), channel_id=1, source_target_pairs={{0,3},{1,2},{2,1},{3,0},{4,7},{5,6},{6,5},{7,4},{8,11},{9,10},{10,... | collective-permute-start | bytes 393224 | tf_op jit(solution)/shard_map/ppermute | solution.py:25
  24.3 0.0 collective-permute-done.5.refs_9_
  24.3 3.9 %shard_map.149 = (bf16[256,2048]{1,0:T(8,128)(2,1)}, bf16[256,2048]{1,0:T(8,128)(2,1)}, bf16[256,512]{1,0:T(8,128)(2,1)}, bf16[256,512]{1,0:T(8,128)(2,1)}, f32[8,128]{1,0:T(8,128)S(1)}) custom-call(bf16[4,256,512]{2,1,0:T(8,128)(2,1)S(1)} %get-tuple-element.31.refs_0_, bf16[4,1024,128]{2,1,0:T(8,128)(2,1)S(1)} %get-tuple-element.36.refs_1_, ...), custom_call_target="tpu_custom_call" | custom-call | flops 1610612736 | bytes 1048576 | tf_op jit(solution)/shard_map/pallas_call | solution.py:288
  28.2 0.0 collective-permute-done.6.refs_1_
  28.2 1.9 %collective-permute-done.7.refs_2_ = bf16[128,512]{1,0:T(8,128)(2,1)S(1)} collective-permute-done((bf16[128,512]{1,0:T(8,128)(2,1)S(1)}, bf16[128,512]{1,0:T(8,128)(2,1)S(1)}, u32[]{:S(2)}, u32[]{:S(2)}) %collective-permute-start.7) | collective-permute-done | bytes 131104 | tf_op jit(solution)/shard_map/ppermute | solution.py:25
  30.1 0.0 collective-permute-done.8.refs_3_
  30.1 0.7 %shard_map.150 = (bf16[64,512]{1,0:T(8,128)(2,1)}, bf16[64,512]{1,0:T(8,128)(2,1)}) custom-call(f32[8,128]{1,0:T(8,128)S(1)} %get-tuple-element.49.weights_ref, f32[128,512]{1,0:T(8,128)S(1)} %get-tuple-element.50.refs_0_, bf16[128,512]{1,0:T(8,128)(2,1)S(1)} %collective-permute-done.6.refs_1_, bf16[128,512]{1,0:T(8,128)(2,1)S(1)} %collective-permute-done.7.refs_2_, ...), custom_call_target="tpu_custom_call" | custom-call | bytes 1048576 | tf_op jit(solution)/shard_map/pallas_call | solution.py:288
  (1 shorter events, 0.0 us)
Async XLA Ops:
  2.3 11.8 %collective-permute-start.1 = (bf16[144,512]{1,0:T(8,128)(2,1)S(1)}, bf16[144,512]{1,0:T(8,128)(2,1)S(1)}, u32[]{:S(2)}, u32[]{:S(2)}) collective-permute-start(bf16[144,512]{1,0:T(8,128)(2,1)S(1)} %shard_map.146.refs_5_.refs_11_), channel_id=1, source_target_pairs={{0,1},{1,0},{2,3},{3,2},{4,5},{5,4},{6,7},{7,6},{8,9},{9,8},{10,11... | collective-permute-start | bytes 442376 | tf_op jit(solution)/shard_map/ppermute | solution.py:25
  5.3 8.8 %collective-permute-start.2 = (bf16[144,512]{1,0:T(8,128)(2,1)S(1)}, bf16[144,512]{1,0:T(8,128)(2,1)S(1)}, u32[]{:S(2)}, u32[]{:S(2)}) collective-permute-start(bf16[144,512]{1,0:T(8,128)(2,1)S(1)} %shard_map.146.refs_5_.refs_11_), channel_id=1, source_target_pairs={{0,2},{1,3},{2,0},{3,1},{4,6},{5,7},{6,4},{7,5},{8,10},{9,11},{10,... | collective-permute-start | bytes 442376 | tf_op jit(solution)/shard_map/ppermute | solution.py:25
  6.8 7.3 %collective-permute-start.3 = (bf16[144,512]{1,0:T(8,128)(2,1)S(1)}, bf16[144,512]{1,0:T(8,128)(2,1)S(1)}, u32[]{:S(2)}, u32[]{:S(2)}) collective-permute-start(bf16[144,512]{1,0:T(8,128)(2,1)S(1)} %shard_map.146.refs_5_.refs_11_), channel_id=1, source_target_pairs={{0,3},{1,2},{2,1},{3,0},{4,7},{5,6},{6,5},{7,4},{8,11},{9,10},{10,... | collective-permute-start | bytes 442376 | tf_op jit(solution)/shard_map/ppermute | solution.py:25
  6.8 1.4 %collective-permute-start = (s32[1]{0:T(128)}, s32[1]{0:T(128)}, u32[]{:S(2)}, u32[]{:S(2)}) collective-permute-start(s32[1]{0:T(128)} %param.16), channel_id=1, source_target_pairs={{0,4},{4,0},{8,12},{12,8},{16,20},{20,16},{24,28},{28,24},{1,5},{5... | collective-permute-start | bytes 20 | tf_op jit(solution)/shard_map/ppermute | solution.py:325
  12.0 6.1 %collective-permute-start.4 = (f32[8,128]{1,0:T(8,128)S(1)}, f32[8,128]{1,0:T(8,128)S(1)}, u32[]{:S(2)}, u32[]{:S(2)}) collective-permute-start(f32[8,128]{1,0:T(8,128)S(1)} %get-tuple-element.43.tile_ref), channel_id=1, source_target_pairs={{0,8},{4,12},{8,0},{12,4},{16,24},{20,28},{24,16},{28,20},{1,9},{5... | collective-permute-start | bytes 12296 | tf_op jit(solution)/shard_map/ppermute | solution.py:325
  18.1 6.1 %collective-permute-start.5 = (f32[8,128]{1,0:T(8,128)S(1)}, f32[8,128]{1,0:T(8,128)S(1)}, u32[]{:S(2)}, u32[]{:S(2)}) collective-permute-start(f32[8,128]{1,0:T(8,128)S(1)} %shard_map.148.refs_8_), channel_id=1, source_target_pairs={{0,16},{4,20},{8,24},{12,28},{16,0},{20,4},{24,8},{28,12},{1,17},{... | collective-permute-start | bytes 12296 | tf_op jit(solution)/shard_map/ppermute | solution.py:325
  20.8 7.4 %collective-permute-start.6 = (bf16[128,512]{1,0:T(8,128)(2,1)S(1)}, bf16[128,512]{1,0:T(8,128)(2,1)S(1)}, u32[]{:S(2)}, u32[]{:S(2)}) collective-permute-start(bf16[128,512]{1,0:T(8,128)(2,1)S(1)} %get-tuple-element.51), channel_id=1, source_target_pairs={{0,1},{1,0},{2,3},{3,2},{4,5},{5,4},{6,7},{7,6},{8,9},{9,8},{10,11... | collective-permute-start | bytes 393224 | tf_op jit(solution)/shard_map/ppermute | solution.py:25
  22.3 7.8 %collective-permute-start.7 = (bf16[128,512]{1,0:T(8,128)(2,1)S(1)}, bf16[128,512]{1,0:T(8,128)(2,1)S(1)}, u32[]{:S(2)}, u32[]{:S(2)}) collective-permute-start(bf16[128,512]{1,0:T(8,128)(2,1)S(1)} %get-tuple-element.52), channel_id=1, source_target_pairs={{0,2},{1,3},{2,0},{3,1},{4,6},{5,7},{6,4},{7,5},{8,10},{9,11},{10,... | collective-permute-start | bytes 393224 | tf_op jit(solution)/shard_map/ppermute | solution.py:25
  23.8 6.3 %collective-permute-start.8 = (bf16[128,512]{1,0:T(8,128)(2,1)S(1)}, bf16[128,512]{1,0:T(8,128)(2,1)S(1)}, u32[]{:S(2)}, u32[]{:S(2)}) collective-permute-start(bf16[128,512]{1,0:T(8,128)(2,1)S(1)} %get-tuple-element.53), channel_id=1, source_target_pairs={{0,3},{1,2},{2,1},{3,0},{4,7},{5,6},{6,5},{7,4},{8,11},{9,10},{10,... | collective-permute-start | bytes 393224 | tf_op jit(solution)/shard_map/ppermute | solution.py:25

commit v7 on v6

v7 whole, which is shorter than its diff:
```python
import functools
import jax
import jax.numpy as jnp
from jax import lax
from jax.experimental import pallas as pl
from jax.experimental.pallas import tpu as pltpu
from jax.sharding import PartitionSpec as P

HEAD_SIZE = 128
BLOCK = 128
EXTRA = 16
SCALING = HEAD_SIZE**-0.5
POWER = SCALING * 1.4426950408889634
VMEM_LIMIT = 32 << 20
f32 = jnp.float32
bf16 = jnp.bfloat16
i32 = jnp.int32


def dot(a, b, ca, cb):
    return lax.dot_general(a, b, (((ca,), (cb,)), ((), ())), preferred_element_type=f32)


def swap(x, n, k):
    return lax.ppermute(x, "resp", [(i, i ^ k) for i in range(n)])


def columns_of(g, width):
    return pl.ds(pl.multiple_of(g * width, width), width)


def stacked(block):
    tokens, width = block.shape
    return jnp.concatenate(
        [
            block[t : t + BLOCK, i : i + HEAD_SIZE]
            for t in range(0, tokens, BLOCK)
            for i in range(0, width, HEAD_SIZE)
        ],
        0,
    )


def unstacked(x, group):
    x = x.astype(bf16)
    lines = [
        jnp.concatenate([x[t + i * BLOCK : t + (i + 1) * BLOCK] for i in range(group)], 1)
        for t in range(0, x.shape[0], group * BLOCK)
    ]
    return jnp.concatenate(lines, 0)


def row_blocks(rows, group):
    return [(slice(t, t + group * BLOCK), t // group + BLOCK) for t in range(0, rows, group * BLOCK)]


def spread(x, width):
    return jnp.concatenate([x] * (width // HEAD_SIZE), 1)


def with_ones(values):
    return jnp.concatenate([values, jnp.ones(values.shape, bf16)], 1)


def causal_mask(group):
    row = lax.broadcasted_iota(i32, (BLOCK, BLOCK), 0)
    key = lax.broadcasted_iota(i32, (BLOCK, BLOCK), 1)
    return jnp.concatenate([key <= row] * group, 0)


def row_of(tile, index):
    row = lax.broadcasted_iota(i32, tile.shape, 0)
    return jnp.sum(jnp.where(row == index, tile, 0.0), 0, keepdims=True)


def pack_kernel(kp_hbm, vp_hbm, ko_hbm, vo_hbm, q_hbm, payload_ref, ko_ref, vo_ref, q_ref, sems):
    part = kp_hbm.shape[0]
    heads, width = ko_ref.shape[0], q_ref.shape[1]
    copies = [
        pltpu.make_async_copy(kp_hbm, payload_ref.at[:part], sems.at[0, 0]),
        pltpu.make_async_copy(vp_hbm, payload_ref.at[part:], sems.at[1, 0]),
        pltpu.make_async_copy(q_hbm.at[:, :width], q_ref, sems.at[2, 0]),
    ]
    for g in range(heads):
        cols = columns_of(g, HEAD_SIZE)
        copies.append(pltpu.make_async_copy(ko_hbm.at[:, cols], ko_ref.at[g], sems.at[3, g]))
        copies.append(pltpu.make_async_copy(vo_hbm.at[:, cols], vo_ref.at[g], sems.at[4, g]))
    for copy in copies:
        copy.start()
    for copy in copies:
        copy.wait()


def reward_rows(payoff):
    whole = jnp.full((EXTRA, HEAD_SIZE), payoff, f32)
    high = whole.astype(bf16).astype(f32)
    middle = (whole - high).astype(bf16).astype(f32)
    low = whole - high - middle
    row = lax.broadcasted_iota(i32, whole.shape, 0)
    return jnp.where(row == 0, high, jnp.where(row == 1, middle, jnp.where(row == 2, low, 0.0)))


def own_kernel(group, counts, *refs):
    small_hbm, refs = refs[: 4 + counts], refs[4 + counts :]
    q_hbm, u_hbm, q_first, ko_ref, vo_ref = refs[:5]
    q_ref, u_ref, att_ref, lse_ref, tile_ref, alive_ref, length_ref = refs[5:12]
    qt_ref, ut_ref, s_ref, reward_ref = refs[12:16]
    small_refs, sems, small_sems = refs[16:-2], refs[-2], refs[-1]
    heads, tokens, width = q_ref.shape

    def load(g):
        return pltpu.make_async_copy(q_hbm.at[:, columns_of(g, width)], q_ref.at[g], sems.at[0, g])

    def late_load(g):
        return pltpu.make_async_copy(u_hbm.at[:, columns_of(g, width)], u_ref.at[g], sems.at[1, g])

    small = [
        pltpu.make_async_copy(a, b, small_sems.at[i])
        for i, (a, b) in enumerate(zip(small_hbm, small_refs))
    ]
    for copy in small:
        copy.start()
    for g in range(1, heads):
        load(g).start()
    for g in range(heads):
        late_load(g).start()

    mask = causal_mask(group)

    def step(g, carry):
        q, ko, vo = stacked(q_ref[g]), ko_ref[g], vo_ref[g]
        for at, span in row_blocks(q.shape[0], group):
            s = dot(q[at], ko[:span], 1, 1) * POWER
            open_part = [s[:, : span - BLOCK]] if span > BLOCK else []
            s = jnp.concatenate(open_part + [jnp.where(mask, s[:, span - BLOCK :], -1e30)], 1)
            s_ref[g, at, :span] = s
            top = jnp.max(s, 1, keepdims=True)
            e = jnp.exp2(s - top)
            both = dot(e.astype(bf16), with_ones(vo[:span]), 1, 0)
            mass = both[:, HEAD_SIZE:]
            att_ref[g, at] = both[:, :HEAD_SIZE] / mass
            lse_ref[g, at] = jnp.log2(mass) + top
        qt_ref[g] = q.T
        return carry

    q_ref[0] = q_first[...]
    step(0, 0)
    for copy in small:
        copy.wait()
    kept_ref, spaces_ref, spans_ref, payoff_ref = small_refs[:4]
    reward_ref[...] = reward_rows(payoff_ref[0, 0])
    member = lax.axis_index("resp")
    kept = kept_ref[0]
    row = lax.broadcasted_iota(i32, alive_ref.shape, 0)
    alive = jnp.zeros(alive_ref.shape, f32)
    own_alive = 0
    for i in range(spaces_ref.shape[1]):
        alive += jnp.where((row == spaces_ref[0, i]) & (i < kept), 1.0, 0.0)
        own_alive += jnp.where((spaces_ref[0, i] == member) & (i < kept), 1, 0)
    alive_ref[...] = alive
    count = kept + sum(r[0] for r in small_refs[4:])
    tile_ref[...] = jnp.full(tile_ref.shape, count.astype(f32))
    length = own_alive * spans_ref[0, 0] * BLOCK
    length_ref[...] = jnp.full(length_ref.shape, length.astype(f32))

    for g in range(1, heads):
        load(g).wait()
    lax.fori_loop(1, heads, step, 0, unroll=True)
    for g in range(heads):
        late_load(g).wait()
    for g in range(heads):
        ut_ref[g] = stacked(u_ref[g]).T


def prefix_kernel(n, *refs):
    q_ref, u_ref, own_ref, lse_ref, length_ref, qt_ref, ut_ref, reward_ref = refs[:8]
    pay_refs = refs[8 : 8 + n]
    out_ref, ds_ref, line_ref, delta_ref = refs[8 + n : 12 + n]
    term_refs = refs[12 + n :]
    for ref in term_refs:
        ref[-EXTRA:] = reward_ref[...].astype(ref.dtype)
    heads, tokens, width = q_ref.shape
    group = width // HEAD_SIZE
    part = pay_refs[0].shape[0] // 2
    token = lax.broadcasted_iota(i32, (tokens, HEAD_SIZE), 0).astype(f32)
    fits = token < length_ref[0:1]
    valid = jnp.concatenate(
        [fits[t : t + BLOCK] for t in range(0, tokens, BLOCK) for _ in range(group)], 0
    )

    def step(g, carry):
        cols = columns_of(g, HEAD_SIZE)
        keys = jnp.concatenate([r[:part, cols] for r in pay_refs], 0)
        values = jnp.concatenate([r[part : 2 * part, cols] for r in pay_refs], 0)
        q = stacked(q_ref[g])
        s = dot(q, keys, 1, 1)
        own_lse = lse_ref[g]
        top = jnp.maximum(jnp.max(s, 1, keepdims=True) * POWER, own_lse)
        e = jnp.exp2(s * POWER - spread(top, s.shape[1]))
        both = dot(e.astype(bf16), with_ones(values), 1, 0)
        own_mass = jnp.exp2(own_lse - top)
        mass = both[:, HEAD_SIZE:] + own_mass
        inverse = jnp.where(valid, 1.0 / mass, 0.0)
        attended = (both[:, :HEAD_SIZE] + own_ref[g] * own_mass) * inverse
        out_ref[g] = unstacked(attended, group)
        p = e * spread(inverse, s.shape[1])
        u = stacked(u_ref[g])
        dp = dot(u, values, 1, 1)
        delta = jnp.sum(u.astype(f32) * attended, 1, keepdims=True)
        ds = (p * (dp - delta)).astype(bf16)
        ds_ref[g] = ds
        line_ref[g] = jnp.where(valid, top + jnp.log2(mass), 1e30)
        delta_ref[g] = jnp.broadcast_to(delta, top.shape)
        dk = dot(qt_ref[g], ds, 1, 0).T * SCALING
        dv = dot(ut_ref[g], p.astype(bf16), 1, 0).T
        for k, ref in enumerate(term_refs):
            at = 2 * g * part
            ref[pl.ds(at, part)] = dk[k * part : (k + 1) * part].astype(ref.dtype)
            ref[pl.ds(at + part, part)] = dv[k * part : (k + 1) * part].astype(ref.dtype)
        return carry

    lax.fori_loop(0, heads, step, 0, unroll=True)


def add_kernel(tile_ref, recv_ref, after_ref, sum_ref):
    sum_ref[...] = tile_ref[...] + recv_ref[...]


def rest_kernel(n, group, begin, end, *refs):
    u_ref, ko_ref, vo_ref, att_ref, ds_ref, line_ref, delta_ref = refs[:7]
    qt_ref, ut_ref, s_ref = refs[7:10]
    pay_refs = refs[10 : 10 + n]
    dq_ref, dko_ref, dvo_ref = refs[10 + n : 13 + n]
    out_hbm, sems = refs[13 + n :] if len(refs) > 13 + n else (None, None)
    _, tokens, width = u_ref.shape
    part = pay_refs[0].shape[0] // 2

    def store(g):
        return pltpu.make_async_copy(att_ref.at[g], out_hbm.at[:, columns_of(g, width)], sems.at[0, g])

    stored = range(u_ref.shape[0]) if out_hbm is not None else ()
    for g in stored:
        store(g).start()

    def step(g, carry):
        cols = columns_of(g, HEAD_SIZE)
        keys = jnp.concatenate([r[:part, cols] for r in pay_refs], 0)
        u, ko, vo = stacked(u_ref[g]), ko_ref[g], vo_ref[g]
        dk, dv = 0.0, 0.0
        for at, span in row_blocks(u.shape[0], group):
            p = jnp.exp2(s_ref[g, at, :span] - spread(line_ref[g, at], span))
            dp = dot(u[at], vo[:span], 1, 1)
            ds = (p * (dp - spread(delta_ref[g, at], span))).astype(bf16)
            all_ds = jnp.concatenate([ds_ref[g, at], ds], 1)
            dq_ref[g - begin, at] = dot(all_ds, jnp.concatenate([keys, ko[:span]], 0), 1, 0)
            missing = [jnp.zeros((HEAD_SIZE, tokens - span), f32)] if span < tokens else []
            dk += jnp.concatenate([dot(qt_ref[g, :, at], ds, 1, 0)] + missing, 1)
            dv += jnp.concatenate([dot(ut_ref[g, :, at], p.astype(bf16), 1, 0)] + missing, 1)
        dko_ref[g - begin] = dk.T
        dvo_ref[g - begin] = dv.T
        return carry

    lax.fori_loop(begin, end, step, 0, unroll=True)
    for g in stored:
        store(g).wait()


def total_kernel(order, alive_ref, *refs):
    term_refs, (total_ref, weight_ref) = refs[:-2], refs[-2:]
    alive = alive_ref[...]
    member = lax.axis_index("resp")
    rewards = [jnp.sum(r[-EXTRA:].astype(f32), 0, keepdims=True) for r in term_refs]
    total = sum(reward * row_of(alive, member ^ k) for k, reward in zip(order, rewards))
    mean = total / jnp.sum(alive, 0, keepdims=True)
    weights = [reward - mean for reward in rewards]
    rows = total_ref.shape[0]
    total_ref[...] = sum(r[:rows].astype(f32) * w for r, w in zip(term_refs, weights))
    weight_ref[...] = jnp.broadcast_to(weights[0], weight_ref.shape)


def last_kernel(group, *refs):
    dq_ref, dko_ref, dvo_ref, sum_ref, total_ref, weight_ref, recv_ref = refs[:7]
    dq_hbm, dko_hbm, dvo_hbm, key_hbm, value_hbm = refs[7:12]
    dq_low, dko_low, dvo_low, key_ref, value_ref, sems = refs[12:]
    heads = dko_low.shape[0]
    part = key_ref.shape[0]
    width = group * HEAD_SIZE

    def stores(g):
        wide, slim = columns_of(g, width), columns_of(g, HEAD_SIZE)
        return [
            pltpu.make_async_copy(dq_low.at[g], dq_hbm.at[:, wide], sems.at[0, g]),
            pltpu.make_async_copy(dko_low.at[g], dko_hbm.at[:, slim], sems.at[1, g]),
            pltpu.make_async_copy(dvo_low.at[g], dvo_hbm.at[:, slim], sems.at[2, g]),
        ]

    totals = [
        pltpu.make_async_copy(key_ref, key_hbm, sems.at[3, 0]),
        pltpu.make_async_copy(value_ref, value_hbm, sems.at[3, 1]),
    ]
    share = 1.0 / (sum_ref[0:1] + recv_ref[0:1])
    weight = weight_ref[0:1] * share
    for g in range(heads):
        dq_low[g] = unstacked(dq_ref[g] * (weight * SCALING), group)
        dko_low[g] = (dko_ref[g] * (weight * SCALING)).astype(bf16)
        dvo_low[g] = (dvo_ref[g] * weight).astype(bf16)
        for copy in stores(g):
            copy.start()
    for g in range(heads):
        for at, ref in ((2 * g * part, key_ref), ((2 * g + 1) * part, value_ref)):
            whole = (total_ref[at : at + part] * share).astype(bf16)
            ref[:, g * HEAD_SIZE : (g + 1) * HEAD_SIZE] = whole
    for copy in totals:
        copy.start()
    for g in range(heads):
        for copy in stores(g):
            copy.wait()
    for copy in totals:
        copy.wait()


def local(q, ko, vo, u, kp, vp, kept, spaces, spans, payoffs):
    n = lax.axis_size("resp")
    n_prompt = lax.axis_size("prompt")
    tokens = q.shape[2]
    kv_width = ko.shape[3]
    heads = kv_width // HEAD_SIZE
    group = q.shape[3] // kv_width
    width = group * HEAD_SIZE
    rows = group * tokens
    part = kp.shape[1]
    prefix = n * part
    tile_shape = (8, HEAD_SIZE)
    slots_shape = (-(-n // 8) * 8, HEAD_SIZE)

    vmem = pl.BlockSpec(memory_space=pltpu.VMEM)
    hbm = pl.BlockSpec(memory_space=pl.ANY)

    def pinned(x):
        return pltpu.with_memory_space_constraint(x, pltpu.HBM)

    def call(kernel, units, ins, out, scratch):
        return pl.pallas_call(
            kernel,
            in_specs=[spec for spec, _ in ins],
            out_specs=[spec for spec, _ in out],
            out_shape=[shape for _, shape in out],
            scratch_shapes=scratch,
            compiler_params=pltpu.CompilerParams(vmem_limit_bytes=VMEM_LIMIT),
            cost_estimate=pl.CostEstimate(
                flops=units * 2 * heads * rows * tokens * HEAD_SIZE,
                bytes_accessed=1 << 20,
                transcendentals=0,
            ),
        )(*[x for _, x in ins])

    def kept_in(shape, kind):
        return (vmem, pltpu.VMEM(shape, kind))

    def given(shape, kind=bf16, spec=hbm):
        return (spec, jax.ShapeDtypeStruct(shape, kind))

    sems = pltpu.SemaphoreType.DMA((5, heads))
    stat = kept_in((heads, rows, HEAD_SIZE), f32)
    tile_kind = kept_in(tile_shape, f32)
    slots_kind = kept_in(slots_shape, f32)
    wide, slim = (heads, tokens, width), (heads, tokens, HEAD_SIZE)
    q, ko, vo, u = q[0, 0], ko[0, 0], vo[0, 0], u[0, 0]

    payload, ko_in, vo_in, q_first = call(
        pack_kernel,
        0,
        [(hbm, pinned(x)) for x in (kp[0], vp[0], ko, vo, q)],
        [kept_in((2 * part, kv_width), bf16)]
        + [kept_in(slim, bf16)] * 2
        + [kept_in((tokens, width), bf16)],
        [sems],
    )
    order = [0] + sorted(range(1, n), key=lambda k: -bin(k).count("1"))
    pays = [payload] + [swap(payload, n, k) for k in order[1:]]

    def across(x, k):
        return lax.ppermute(x, "prompt", [(i, i ^ k) for i in range(n_prompt)])

    small = [kept, pinned(spaces), spans, payoffs, across(kept, 1)]
    q_in, u_in, own, own_lse, tile, alive, length, qt, ut, scores, reward = call(
        functools.partial(own_kernel, group, 1),
        2,
        [(hbm, x) for x in small]
        + [(hbm, pinned(x)) for x in (q, u)]
        + [(vmem, x) for x in (q_first, ko_in, vo_in)],
        [kept_in(wide, bf16)] * 2
        + [stat, stat, tile_kind, slots_kind, tile_kind] + [kept_in((heads, HEAD_SIZE, rows), bf16)] * 2
        + [kept_in((heads, rows, tokens), f32), kept_in((EXTRA, HEAD_SIZE), f32)],
        [pltpu.SMEM(x.shape, x.dtype) for x in small]
        + [sems, pltpu.SemaphoreType.DMA((len(small),))],
    )
    k = 2
    while 4 * k < n_prompt:
        tile = tile + across(tile, k)
        k *= 2
    arriving = across(tile, k)
    att, ds, line, delta, *terms = call(
        functools.partial(prefix_kernel, n),
        5,
        [(vmem, x) for x in [q_in, u_in, own, own_lse, length, qt, ut, reward] + pays],
        [kept_in(wide, bf16), kept_in((heads, rows, prefix), bf16), stat, stat]
        + [kept_in((2 * heads * part + EXTRA, HEAD_SIZE), f32 if i == 0 else bf16) for i in range(n)],
        [],
    )
    def rest(begin, end, out, scratch):
        done = end - begin
        return call(
            functools.partial(rest_kernel, n, group, begin, end),
            6,
            [(vmem, x) for x in [u_in, ko_in, vo_in, att, ds, line, delta, qt, ut, scores] + pays],
            [kept_in((done, rows, HEAD_SIZE), f32)]
            + [kept_in((done, tokens, HEAD_SIZE), f32)] * 2
            + out,
            scratch,
        )

    received = [swap(t, n, k) for k, t in zip(order[1:], terms[1:])]
    (tile_sum,) = call(
        add_kernel, 0, [(vmem, tile), (vmem, arriving), (hbm, line)], [tile_kind], []
    )
    other = across(tile_sum, 2 * k)
    dq_sum, dko_sum, dvo_sum, attn_out = rest(0, heads, [given(q.shape)], [sems])
    total, weight = call(
        functools.partial(total_kernel, order),
        0,
        [(vmem, x) for x in [alive, terms[0]] + received],
        [kept_in((2 * heads * part, HEAD_SIZE), f32), tile_kind],
        [],
    )
    dq, dko, dvo, key_total, value_total = call(
        functools.partial(last_kernel, group),
        0,
        [(vmem, x) for x in [dq_sum, dko_sum, dvo_sum, tile_sum, total, weight, other]],
        [given(q.shape)] + [given(ko.shape)] * 2 + [given((part, kv_width))] * 2,
        [pltpu.VMEM(wide, bf16), pltpu.VMEM(slim, bf16), pltpu.VMEM(slim, bf16)]
        + [pltpu.VMEM((part, kv_width), bf16)] * 2
        + [sems],
    )
    return (
        attn_out[None, None],
        dq[None, None],
        dko[None, None],
        dvo[None, None],
        key_total[None],
        value_total[None],
    )


def solution(mesh):
    wide = P("prompt", "resp", None, None)
    rows = P("prompt", "resp", None)
    pair = P("prompt", "resp")
    return jax.shard_map(
        local,
        mesh=mesh,
        in_specs=(wide, wide, wide, wide, rows, rows, P("prompt"), P("prompt", None), pair, pair),
        out_specs=(wide, wide, wide, wide, rows, rows),
        check_vma=False,
    )
```

time: 31.1 us -> 30.2 us (0.971)
  waiting for transfers between devices: 1.96 us -> 0.02 us
  Pallas kernels: 13.4 us -> 14.6 us
    ppermute x6, waiting for transfers between devices: 1.87 us -> 0.02 us  [swap(): return lax.ppermute(x, 'resp', [(i, i ^ k) for i in range(n)])]
    pallas_call x6 -> x7, Pallas kernels: 13.4 us -> 14.6 us  [call(): pl.pallas_call(kernel, in_specs=[spec for spec, _ in ins], out_specs=[spe...]
  transfers between devices with their start and end apart: 9 -> 9, of which waited for: 2 -> 0; matrix products, arithmetic and copies ran while one was open for 0% -> 0% of each run, Pallas kernels for 38% -> 39%
where the time goes in v7:
time: 30.2 us; the launch traced here: 30 us
  Pallas kernels  14.6 us (48%)
  starting transfers between devices  12.8 us (42%)
  between operations  2.66 us (9%)
    pallas_call x7, Pallas kernels, call(): pl.pallas_call(kernel, in_specs=[spec for spec, _ in ins], out_specs=[spe...  14.6 us
    ppermute x6, starting transfers between devices, swap(): return lax.ppermute(x, 'resp', [(i, i ^ k) for i in range(n)])  8.16 us
    ppermute x3, starting transfers between devices, across(): return lax.ppermute(x, 'prompt', [(i, i ^ k) for i in range(n_prompt)])  4.63 us
  transfers between devices with their start and end apart: 9, of which 0 were waited for; matrix products, arithmetic and copies ran while one was open for 0% of the time, Pallas kernels for 39%

profile of v7, /device:TPU:0, one launch (start us, length us, event | category | flops | bytes accessed | tf_op | source)
XLA Modules:
  0.0 30.0 jit_solution(6929813300878244365)
XLA Ops:
  0.6 1.3 %shard_map.145 = (bf16[128,512]{1,0:T(8,128)(2,1)S(1)}, bf16[4,256,128]{2,1,0:T(8,128)(2,1)S(1)}, bf16[4,256,128]{2,1,0:T(8,128)(2,1)S(1)}, bf16[256,512]{1,0:T(8,128)(2,1)S(1)}) custom-call(bf16[64,512]{1,0:T(8,128)(2,1)} %bitcast.17, bf16[64,512]{1,0:T(8,128)(2,1)} %bitcast.18, bf16[256,512]{1,0:T(8,128)(2,1)} %bitcast.15, bf16[256,512]{1,0:T(8,128)(2,1)} %bitcast.16, ...), custom_call_target="tpu_custom_call" | custom-call | bytes 1048576 | tf_op jit(solution)/shard_map/pallas_call | solution.py:343
  2.0 4.0 %collective-permute-start.1 = (bf16[128,512]{1,0:T(8,128)(2,1)S(1)}, bf16[128,512]{1,0:T(8,128)(2,1)S(1)}, u32[]{:S(2)}, u32[]{:S(2)}) collective-permute-start(bf16[128,512]{1,0:T(8,128)(2,1)S(1)} %get-tuple-element.51.refs_8_.refs_10_), channel_id=1, source_target_pairs={{0,3},{1,2},{2,1},{3,0},{4,7},{5,6},{6,5},{7,4},{8,11},{9,10},{10,... | collective-permute-start | bytes 393224 | tf_op jit(solution)/shard_map/ppermute | solution.py:25
  5.9 0.5 %collective-permute-start.2 = (bf16[128,512]{1,0:T(8,128)(2,1)S(1)}, bf16[128,512]{1,0:T(8,128)(2,1)S(1)}, u32[]{:S(2)}, u32[]{:S(2)}) collective-permute-start(bf16[128,512]{1,0:T(8,128)(2,1)S(1)} %get-tuple-element.51.refs_8_.refs_10_), channel_id=1, source_target_pairs={{0,1},{1,0},{2,3},{3,2},{4,5},{5,4},{6,7},{7,6},{8,9},{9,8},{10,11... | collective-permute-start | bytes 393224 | tf_op jit(solution)/shard_map/ppermute | solution.py:25
  6.5 0.1 collective-permute-start.3
  6.6 0.0 collective-permute-start
  8.5 0.0 collective-permute-done.refs_4_
  8.5 4.0 %shard_map.146 = (bf16[4,256,512]{2,1,0:T(8,128)(2,1)S(1)}, bf16[4,256,512]{2,1,0:T(8,128)(2,1)S(1)}, f32[4,1024,128]{2,1,0:T(8,128)S(1)}, f32[4,1024,128]{2,1,0...) custom-call(s32[1]{0:T(128)S(6)} %copy.16.refs_0_, ...), custom_call_target="tpu_custom_call" | custom-call | flops 536870912 | bytes 1048576 | tf_op jit(solution)/shard_map/pallas_call | solution.py:343
  12.6 2.0 %collective-permute-start.4 = (f32[8,128]{1,0:T(8,128)S(1)}, f32[8,128]{1,0:T(8,128)S(1)}, u32[]{:S(2)}, u32[]{:S(2)}) collective-permute-start(f32[8,128]{1,0:T(8,128)S(1)} %get-tuple-element.61.tile_ref), channel_id=1, source_target_pairs={{0,8},{4,12},{8,0},{12,4},{16,24},{20,28},{24,16},{28,20},{1,9},{5... | collective-permute-start | bytes 12296 | tf_op jit(solution)/shard_map/ppermute | solution.py:383
  14.6 0.0 collective-permute-done.1.refs_9_.refs_11_
  14.6 0.0 collective-permute-done.2.refs_10_.refs_12_
  14.6 0.0 collective-permute-done.3.refs_11_.refs_13_
  14.6 4.0 %shard_map.147 = (bf16[4,256,512]{2,1,0:T(8,128)(2,1)S(1)}, bf16[4,1024,256]{2,1,0:T(8,128)(2,1)S(1)}, f32[4,1024,128]{2,1,0:T(8,128)S(1)}, f32[4,1024,128]{2,1,...) custom-call(bf16[4,256,512]{2,1,0:T(8,128)(2,1)S(1)} %get-tuple-elem, ...), custom_call_target="tpu_custom_call" | custom-call | flops 1342177280 | bytes 1048576 | tf_op jit(solution)/shard_map/pallas_call | solution.py:343
  18.7 2.5 %collective-permute-start.5 = (bf16[528,128]{1,0:T(8,128)(2,1)S(1)}, bf16[528,128]{1,0:T(8,128)(2,1)S(1)}, u32[]{:S(2)}, u32[]{:S(2)}) collective-permute-start(bf16[528,128]{1,0:T(8,128)(2,1)S(1)} %get-tuple-element.64), channel_id=1, source_target_pairs={{0,3},{1,2},{2,1},{3,0},{4,7},{5,6},{6,5},{7,4},{8,11},{9,10},{10,... | collective-permute-start | bytes 405512 | tf_op jit(solution)/shard_map/ppermute | solution.py:25
  21.2 0.5 %collective-permute-start.6 = (bf16[528,128]{1,0:T(8,128)(2,1)S(1)}, bf16[528,128]{1,0:T(8,128)(2,1)S(1)}, u32[]{:S(2)}, u32[]{:S(2)}) collective-permute-start(bf16[528,128]{1,0:T(8,128)(2,1)S(1)} %get-tuple-element.65), channel_id=1, source_target_pairs={{0,1},{1,0},{2,3},{3,2},{4,5},{5,4},{6,7},{7,6},{8,9},{9,8},{10,11... | collective-permute-start | bytes 405512 | tf_op jit(solution)/shard_map/ppermute | solution.py:25
  21.7 0.5 %collective-permute-start.7 = (bf16[528,128]{1,0:T(8,128)(2,1)S(1)}, bf16[528,128]{1,0:T(8,128)(2,1)S(1)}, u32[]{:S(2)}, u32[]{:S(2)}) collective-permute-start(bf16[528,128]{1,0:T(8,128)(2,1)S(1)} %get-tuple-element.66), channel_id=1, source_target_pairs={{0,2},{1,3},{2,0},{3,1},{4,6},{5,7},{6,4},{7,5},{8,10},{9,11},{10,... | collective-permute-start | bytes 405512 | tf_op jit(solution)/shard_map/ppermute | solution.py:25
  22.2 0.0 collective-permute-done.4.recv_ref
  22.2 2.6 %collective-permute-start.8 = (f32[8,128]{1,0:T(8,128)S(1)}, f32[8,128]{1,0:T(8,128)S(1)}, u32[]{:S(2)}, u32[]{:S(2)}) collective-permute-start(f32[8,128]{1,0:T(8,128)S(1)} %shard_map.149.refs_3_), channel_id=1, source_target_pairs={{0,16},{4,20},{8,24},{12,28},{16,0},{20,4},{24,8},{28,12},{1,17},{... | collective-permute-start | bytes 12296 | tf_op jit(solution)/shard_map/ppermute | solution.py:383
  24.8 3.7 %shard_map.148 = (f32[4,1024,128]{2,1,0:T(8,128)S(1)}, f32[4,256,128]{2,1,0:T(8,128)S(1)}, f32[4,256,128]{2,1,0:T(8,128)S(1)}, bf16[256,2048]{1,0:T(8,128)(2,1)}) custom-call(bf16[4,256,512]{2,1,0:T(8,128)(2,1)S(1)} %get-tuple-element.43.refs_1_.refs_0_, bf16[4,256,128]{2,1,0:T(8,128)(2,1)S(1)} %get-tuple-element.41.refs_8_.refs_1_, ...), custom_call_target="tpu_custom_call" | custom-call | flops 1610612736 | bytes 1048576 | tf_op jit(solution)/shard_map/pallas_call | solution.py:343
  28.5 0.0 collective-permute-done.5.refs_1_
  28.5 0.0 collective-permute-done.6.refs_2_
  28.5 0.0 collective-permute-done.7.refs_3_
  28.5 0.1 shard_map.150
  28.6 0.0 collective-permute-done.8.refs_6_
  28.6 1.4 %shard_map.151 = (bf16[256,2048]{1,0:T(8,128)(2,1)}, bf16[256,512]{1,0:T(8,128)(2,1)}, bf16[256,512]{1,0:T(8,128)(2,1)}, bf16[64,512]{1,0:T(8,128)(2,1)}, bf16[64,512]{1,0:T(8,128)(2,1)}) custom-call(f32[4,1024,128]{2,1,0:T(8,128)S(1)} %get-tuple-element.58.refs_0_, f32[4,256,128]{2,1,0:T(8,128)S(1)} %get-tuple-element.59.refs_1_, ...), custom_call_target="tpu_custom_call" | custom-call | bytes 1048576 | tf_op jit(solution)/shard_map/pallas_call | solution.py:343
  (1 shorter events, 0.0 us)
Async XLA Ops:
  2.0 12.6 %collective-permute-start.1 = (bf16[128,512]{1,0:T(8,128)(2,1)S(1)}, bf16[128,512]{1,0:T(8,128)(2,1)S(1)}, u32[]{:S(2)}, u32[]{:S(2)}) collective-permute-start(bf16[128,512]{1,0:T(8,128)(2,1)S(1)} %get-tuple-element.51.refs_8_.refs_10_), channel_id=1, source_target_pairs={{0,3},{1,2},{2,1},{3,0},{4,7},{5,6},{6,5},{7,4},{8,11},{9,10},{10,... | collective-permute-start | bytes 393224 | tf_op jit(solution)/shard_map/ppermute | solution.py:25
  5.9 8.7 %collective-permute-start.2 = (bf16[128,512]{1,0:T(8,128)(2,1)S(1)}, bf16[128,512]{1,0:T(8,128)(2,1)S(1)}, u32[]{:S(2)}, u32[]{:S(2)}) collective-permute-start(bf16[128,512]{1,0:T(8,128)(2,1)S(1)} %get-tuple-element.51.refs_8_.refs_10_), channel_id=1, source_target_pairs={{0,1},{1,0},{2,3},{3,2},{4,5},{5,4},{6,7},{7,6},{8,9},{9,8},{10,11... | collective-permute-start | bytes 393224 | tf_op jit(solution)/shard_map/ppermute | solution.py:25
  6.5 8.1 %collective-permute-start.3 = (bf16[128,512]{1,0:T(8,128)(2,1)S(1)}, bf16[128,512]{1,0:T(8,128)(2,1)S(1)}, u32[]{:S(2)}, u32[]{:S(2)}) collective-permute-start(bf16[128,512]{1,0:T(8,128)(2,1)S(1)} %get-tuple-element.51.refs_8_.refs_10_), channel_id=1, source_target_pairs={{0,2},{1,3},{2,0},{3,1},{4,6},{5,7},{6,4},{7,5},{8,10},{9,11},{10,... | collective-permute-start | bytes 393224 | tf_op jit(solution)/shard_map/ppermute | solution.py:25
  6.6 2.0 %collective-permute-start = (s32[1]{0:T(128)}, s32[1]{0:T(128)}, u32[]{:S(2)}, u32[]{:S(2)}) collective-permute-start(s32[1]{0:T(128)} %param.16), channel_id=1, source_target_pairs={{0,4},{4,0},{8,12},{12,8},{16,20},{20,16},{24,28},{28,24},{1,5},{5... | collective-permute-start | bytes 20 | tf_op jit(solution)/shard_map/ppermute | solution.py:383
  12.6 9.6 %collective-permute-start.4 = (f32[8,128]{1,0:T(8,128)S(1)}, f32[8,128]{1,0:T(8,128)S(1)}, u32[]{:S(2)}, u32[]{:S(2)}) collective-permute-start(f32[8,128]{1,0:T(8,128)S(1)} %get-tuple-element.61.tile_ref), channel_id=1, source_target_pairs={{0,8},{4,12},{8,0},{12,4},{16,24},{20,28},{24,16},{28,20},{1,9},{5... | collective-permute-start | bytes 12296 | tf_op jit(solution)/shard_map/ppermute | solution.py:383
  18.7 9.8 %collective-permute-start.5 = (bf16[528,128]{1,0:T(8,128)(2,1)S(1)}, bf16[528,128]{1,0:T(8,128)(2,1)S(1)}, u32[]{:S(2)}, u32[]{:S(2)}) collective-permute-start(bf16[528,128]{1,0:T(8,128)(2,1)S(1)} %get-tuple-element.64), channel_id=1, source_target_pairs={{0,3},{1,2},{2,1},{3,0},{4,7},{5,6},{6,5},{7,4},{8,11},{9,10},{10,... | collective-permute-start | bytes 405512 | tf_op jit(solution)/shard_map/ppermute | solution.py:25
  21.2 7.3 %collective-permute-start.6 = (bf16[528,128]{1,0:T(8,128)(2,1)S(1)}, bf16[528,128]{1,0:T(8,128)(2,1)S(1)}, u32[]{:S(2)}, u32[]{:S(2)}) collective-permute-start(bf16[528,128]{1,0:T(8,128)(2,1)S(1)} %get-tuple-element.65), channel_id=1, source_target_pairs={{0,1},{1,0},{2,3},{3,2},{4,5},{5,4},{6,7},{7,6},{8,9},{9,8},{10,11... | collective-permute-start | bytes 405512 | tf_op jit(solution)/shard_map/ppermute | solution.py:25
  21.7 6.8 %collective-permute-start.7 = (bf16[528,128]{1,0:T(8,128)(2,1)S(1)}, bf16[528,128]{1,0:T(8,128)(2,1)S(1)}, u32[]{:S(2)}, u32[]{:S(2)}) collective-permute-start(bf16[528,128]{1,0:T(8,128)(2,1)S(1)} %get-tuple-element.66), channel_id=1, source_target_pairs={{0,2},{1,3},{2,0},{3,1},{4,6},{5,7},{6,4},{7,5},{8,10},{9,11},{10,... | collective-permute-start | bytes 405512 | tf_op jit(solution)/shard_map/ppermute | solution.py:25
  22.2 6.4 %collective-permute-start.8 = (f32[8,128]{1,0:T(8,128)S(1)}, f32[8,128]{1,0:T(8,128)S(1)}, u32[]{:S(2)}, u32[]{:S(2)}) collective-permute-start(f32[8,128]{1,0:T(8,128)S(1)} %shard_map.149.refs_3_), channel_id=1, source_target_pairs={{0,16},{4,20},{8,24},{12,28},{16,0},{20,4},{24,8},{28,12},{1,17},{... | collective-permute-start | bytes 12296 | tf_op jit(solution)/shard_map/ppermute | solution.py:383

commit v8 on v7

--- a/solution.py
+++ b/solution.py
@@ -62,10 +62,12 @@
     return jnp.concatenate([values, jnp.ones(values.shape, bf16)], 1)
 
 
-def causal_mask(group):
-    row = lax.broadcasted_iota(i32, (BLOCK, BLOCK), 0)
-    key = lax.broadcasted_iota(i32, (BLOCK, BLOCK), 1)
-    return jnp.concatenate([key <= row] * group, 0)
+def causal_mask(tokens, group):
+    row = lax.broadcasted_iota(i32, (BLOCK, tokens), 0)
+    key = lax.broadcasted_iota(i32, (BLOCK, tokens), 1)
+    return jnp.concatenate(
+        [key <= row + t for t in range(0, tokens, BLOCK) for _ in range(group)], 0
+    )
 
 
 def row_of(tile, index):
@@ -125,21 +127,18 @@
     for g in range(heads):
         late_load(g).start()
 
-    mask = causal_mask(group)
+    mask = causal_mask(tokens, group)
 
     def step(g, carry):
         q, ko, vo = stacked(q_ref[g]), ko_ref[g], vo_ref[g]
-        for at, span in row_blocks(q.shape[0], group):
-            s = dot(q[at], ko[:span], 1, 1) * POWER
-            open_part = [s[:, : span - BLOCK]] if span > BLOCK else []
-            s = jnp.concatenate(open_part + [jnp.where(mask, s[:, span - BLOCK :], -1e30)], 1)
-            s_ref[g, at, :span] = s
-            top = jnp.max(s, 1, keepdims=True)
-            e = jnp.exp2(s - top)
-            both = dot(e.astype(bf16), with_ones(vo[:span]), 1, 0)
-            mass = both[:, HEAD_SIZE:]
-            att_ref[g, at] = both[:, :HEAD_SIZE] / mass
-            lse_ref[g, at] = jnp.log2(mass) + top
+        s = jnp.where(mask, dot(q, ko, 1, 1) * POWER, -1e30)
+        s_ref[g] = s
+        top = jnp.max(s, 1, keepdims=True)
+        e = jnp.exp2(s - top)
+        both = dot(e.astype(bf16), with_ones(vo), 1, 0)
+        mass = both[:, HEAD_SIZE:]
+        att_ref[g] = both[:, :HEAD_SIZE] / mass
+        lse_ref[g] = jnp.log2(mass) + top
         qt_ref[g] = q.T
         return carry
 
@@ -194,6 +193,8 @@
         values = jnp.concatenate([r[part : 2 * part, cols] for r in pay_refs], 0)
         q = stacked(q_ref[g])
         s = dot(q, keys, 1, 1)
+        u = stacked(u_ref[g])
+        dp = dot(u, values, 1, 1)
         own_lse = lse_ref[g]
         top = jnp.maximum(jnp.max(s, 1, keepdims=True) * POWER, own_lse)
         e = jnp.exp2(s * POWER - spread(top, s.shape[1]))
@@ -204,8 +205,6 @@
         attended = (both[:, :HEAD_SIZE] + own_ref[g] * own_mass) * inverse
         out_ref[g] = unstacked(attended, group)
         p = e * spread(inverse, s.shape[1])
-        u = stacked(u_ref[g])
-        dp = dot(u, values, 1, 1)
         delta = jnp.sum(u.astype(f32) * attended, 1, keepdims=True)
         ds = (p * (dp - delta)).astype(bf16)
         ds_ref[g] = ds
@@ -246,16 +245,13 @@
         cols = columns_of(g, HEAD_SIZE)
         keys = jnp.concatenate([r[:part, cols] for r in pay_refs], 0)
         u, ko, vo = stacked(u_ref[g]), ko_ref[g], vo_ref[g]
-        dk, dv = 0.0, 0.0
-        for at, span in row_blocks(u.shape[0], group):
-            p = jnp.exp2(s_ref[g, at, :span] - spread(line_ref[g, at], span))
-            dp = dot(u[at], vo[:span], 1, 1)
-            ds = (p * (dp - spread(delta_ref[g, at], span))).astype(bf16)
-            all_ds = jnp.concatenate([ds_ref[g, at], ds], 1)
-            dq_ref[g - begin, at] = dot(all_ds, jnp.concatenate([keys, ko[:span]], 0), 1, 0)
-            missing = [jnp.zeros((HEAD_SIZE, tokens - span), f32)] if span < tokens else []
-            dk += jnp.concatenate([dot(qt_ref[g, :, at], ds, 1, 0)] + missing, 1)
-            dv += jnp.concatenate([dot(ut_ref[g, :, at], p.astype(bf16), 1, 0)] + missing, 1)
+        p = jnp.exp2(s_ref[g] - spread(line_ref[g], tokens))
+        dp = dot(u, vo, 1, 1)
+        ds = (p * (dp - spread(delta_ref[g], tokens))).astype(bf16)
+        all_ds = jnp.concatenate([ds_ref[g], ds], 1)
+        dq_ref[g - begin] = dot(all_ds, jnp.concatenate([keys, ko], 0), 1, 0)
+        dk = dot(qt_ref[g], ds, 1, 0)
+        dv = dot(ut_ref[g], p.astype(bf16), 1, 0)
         dko_ref[g - begin] = dk.T
         dvo_ref[g - begin] = dv.T
         return carry
@@ -282,40 +278,35 @@
     dq_ref, dko_ref, dvo_ref, sum_ref, total_ref, weight_ref, recv_ref = refs[:7]
     dq_hbm, dko_hbm, dvo_hbm, key_hbm, value_hbm = refs[7:12]
     dq_low, dko_low, dvo_low, key_ref, value_ref, sems = refs[12:]
-    heads = dko_low.shape[0]
+    heads = dko_ref.shape[0]
     part = key_ref.shape[0]
     width = group * HEAD_SIZE
 
-    def stores(g):
-        wide, slim = columns_of(g, width), columns_of(g, HEAD_SIZE)
-        return [
-            pltpu.make_async_copy(dq_low.at[g], dq_hbm.at[:, wide], sems.at[0, g]),
-            pltpu.make_async_copy(dko_low.at[g], dko_hbm.at[:, slim], sems.at[1, g]),
-            pltpu.make_async_copy(dvo_low.at[g], dvo_hbm.at[:, slim], sems.at[2, g]),
-        ]
-
-    totals = [
-        pltpu.make_async_copy(key_ref, key_hbm, sems.at[3, 0]),
-        pltpu.make_async_copy(value_ref, value_hbm, sems.at[3, 1]),
+    def store(g):
+        return pltpu.make_async_copy(dq_low.at[g], dq_hbm.at[:, columns_of(g, width)], sems.at[0, g])
+
+    whole = [
+        pltpu.make_async_copy(a, b, sems.at[1, i])
+        for i, (a, b) in enumerate(
+            ((dko_low, dko_hbm), (dvo_low, dvo_hbm), (key_ref, key_hbm), (value_ref, value_hbm))
+        )
     ]
     share = 1.0 / (sum_ref[0:1] + recv_ref[0:1])
     weight = weight_ref[0:1] * share
     for g in range(heads):
         dq_low[g] = unstacked(dq_ref[g] * (weight * SCALING), group)
-        dko_low[g] = (dko_ref[g] * (weight * SCALING)).astype(bf16)
-        dvo_low[g] = (dvo_ref[g] * weight).astype(bf16)
-        for copy in stores(g):
-            copy.start()
-    for g in range(heads):
+        store(g).start()
+    for g in range(heads):
+        cols = slice(g * HEAD_SIZE, (g + 1) * HEAD_SIZE)
+        dko_low[:, cols] = (dko_ref[g] * (weight * SCALING)).astype(bf16)
+        dvo_low[:, cols] = (dvo_ref[g] * weight).astype(bf16)
         for at, ref in ((2 * g * part, key_ref), ((2 * g + 1) * part, value_ref)):
-            whole = (total_ref[at : at + part] * share).astype(bf16)
-            ref[:, g * HEAD_SIZE : (g + 1) * HEAD_SIZE] = whole
-    for copy in totals:
+            ref[:, cols] = (total_ref[at : at + part] * share).astype(bf16)
+    for copy in whole:
         copy.start()
     for g in range(heads):
-        for copy in stores(g):
-            copy.wait()
-    for copy in totals:
+        store(g).wait()
+    for copy in whole:
         copy.wait()
 
 
@@ -438,7 +429,8 @@
         0,
         [(vmem, x) for x in [dq_sum, dko_sum, dvo_sum, tile_sum, total, weight, other]],
         [given(q.shape)] + [given(ko.shape)] * 2 + [given((part, kv_width))] * 2,
-        [pltpu.VMEM(wide, bf16), pltpu.VMEM(slim, bf16), pltpu.VMEM(slim, bf16)]
+        [pltpu.VMEM(wide, bf16)]
+        + [pltpu.VMEM((tokens, kv_width), bf16)] * 2
         + [pltpu.VMEM((part, kv_width), bf16)] * 2
         + [sems],
     )

time: 30.2 us -> 29.7 us (0.983)
  Pallas kernels: 14.6 us -> 13.9 us
    pallas_call x7, Pallas kernels: 14.6 us -> 13.9 us  [call(): pl.pallas_call(kernel, in_specs=[spec for spec, _ in ins], out_specs=[spe...]
  transfers between devices with their start and end apart: 9 -> 9, of which waited for: 0 -> 1; matrix products, arithmetic and copies ran while one was open for 0% -> 0% of each run, Pallas kernels for 39% -> 38%
where the time goes in v8:
time: 29.7 us; the launch traced here: 29.5 us
  Pallas kernels  13.9 us (47%)
  starting transfers between devices  12.8 us (43%)
  between operations  2.64 us (9%)
    pallas_call x7, Pallas kernels, call(): pl.pallas_call(kernel, in_specs=[spec for spec, _ in ins], out_specs=[spe...  13.9 us
    ppermute x6, starting transfers between devices, swap(): return lax.ppermute(x, 'resp', [(i, i ^ k) for i in range(n)])  8.16 us
    ppermute x3, starting transfers between devices, across(): return lax.ppermute(x, 'prompt', [(i, i ^ k) for i in range(n_prompt)])  4.63 us
  transfers between devices with their start and end apart: 9, of which 1 were waited for; matrix products, arithmetic and copies ran while one was open for 0% of the time, Pallas kernels for 38%

profile of v8, /device:TPU:0, one launch (start us, length us, event | category | flops | bytes accessed | tf_op | source)
XLA Modules:
  0.0 29.5 jit_solution(2145541688635932650)
XLA Ops:
  0.6 1.3 %shard_map.145 = (bf16[128,512]{1,0:T(8,128)(2,1)S(1)}, bf16[4,256,128]{2,1,0:T(8,128)(2,1)S(1)}, bf16[4,256,128]{2,1,0:T(8,128)(2,1)S(1)}, bf16[256,512]{1,0:T(8,128)(2,1)S(1)}) custom-call(bf16[64,512]{1,0:T(8,128)(2,1)} %bitcast.17, bf16[64,512]{1,0:T(8,128)(2,1)} %bitcast.18, bf16[256,512]{1,0:T(8,128)(2,1)} %bitcast.15, bf16[256,512]{1,0:T(8,128)(2,1)} %bitcast.16, ...), custom_call_target="tpu_custom_call" | custom-call | bytes 1048576 | tf_op jit(solution)/shard_map/pallas_call | solution.py:334
  2.0 4.0 %collective-permute-start.1 = (bf16[128,512]{1,0:T(8,128)(2,1)S(1)}, bf16[128,512]{1,0:T(8,128)(2,1)S(1)}, u32[]{:S(2)}, u32[]{:S(2)}) collective-permute-start(bf16[128,512]{1,0:T(8,128)(2,1)S(1)} %get-tuple-element.51.refs_8_.refs_10_), channel_id=1, source_target_pairs={{0,3},{1,2},{2,1},{3,0},{4,7},{5,6},{6,5},{7,4},{8,11},{9,10},{10,... | collective-permute-start | bytes 393224 | tf_op jit(solution)/shard_map/ppermute | solution.py:25
  5.9 0.5 %collective-permute-start.2 = (bf16[128,512]{1,0:T(8,128)(2,1)S(1)}, bf16[128,512]{1,0:T(8,128)(2,1)S(1)}, u32[]{:S(2)}, u32[]{:S(2)}) collective-permute-start(bf16[128,512]{1,0:T(8,128)(2,1)S(1)} %get-tuple-element.51.refs_8_.refs_10_), channel_id=1, source_target_pairs={{0,1},{1,0},{2,3},{3,2},{4,5},{5,4},{6,7},{7,6},{8,9},{9,8},{10,11... | collective-permute-start | bytes 393224 | tf_op jit(solution)/shard_map/ppermute | solution.py:25
  6.5 0.1 collective-permute-start.3
  6.6 0.0 collective-permute-start
  8.5 0.0 collective-permute-done.refs_4_
  8.5 3.8 %shard_map.146 = (bf16[4,256,512]{2,1,0:T(8,128)(2,1)S(1)}, bf16[4,256,512]{2,1,0:T(8,128)(2,1)S(1)}, f32[4,1024,128]{2,1,0:T(8,128)S(1)}, f32[4,1024,128]{2,1,0...) custom-call(s32[1]{0:T(128)S(6)} %copy.16.refs_0_, ...), custom_call_target="tpu_custom_call" | custom-call | flops 536870912 | bytes 1048576 | tf_op jit(solution)/shard_map/pallas_call | solution.py:334
  12.4 2.0 %collective-permute-start.4 = (f32[8,128]{1,0:T(8,128)S(1)}, f32[8,128]{1,0:T(8,128)S(1)}, u32[]{:S(2)}, u32[]{:S(2)}) collective-permute-start(f32[8,128]{1,0:T(8,128)S(1)} %get-tuple-element.61.tile_ref), channel_id=1, source_target_pairs={{0,8},{4,12},{8,0},{12,4},{16,24},{20,28},{24,16},{28,20},{1,9},{5... | collective-permute-start | bytes 12296 | tf_op jit(solution)/shard_map/ppermute | solution.py:374
  14.4 0.0 collective-permute-done.1.refs_9_.refs_11_
  14.4 0.0 collective-permute-done.2.refs_10_.refs_12_
  14.4 0.0 collective-permute-done.3.refs_11_.refs_13_
  14.4 3.9 %shard_map.147 = (bf16[4,256,512]{2,1,0:T(8,128)(2,1)S(1)}, bf16[4,1024,256]{2,1,0:T(8,128)(2,1)S(1)}, f32[4,1024,128]{2,1,0:T(8,128)S(1)}, f32[4,1024,128]{2,1,...) custom-call(bf16[4,256,512]{2,1,0:T(8,128)(2,1)S(1)} %get-tuple-elem, ...), custom_call_target="tpu_custom_call" | custom-call | flops 1342177280 | bytes 1048576 | tf_op jit(solution)/shard_map/pallas_call | solution.py:334
  18.3 2.5 %collective-permute-start.5 = (bf16[528,128]{1,0:T(8,128)(2,1)S(1)}, bf16[528,128]{1,0:T(8,128)(2,1)S(1)}, u32[]{:S(2)}, u32[]{:S(2)}) collective-permute-start(bf16[528,128]{1,0:T(8,128)(2,1)S(1)} %get-tuple-element.64), channel_id=1, source_target_pairs={{0,3},{1,2},{2,1},{3,0},{4,7},{5,6},{6,5},{7,4},{8,11},{9,10},{10,... | collective-permute-start | bytes 405512 | tf_op jit(solution)/shard_map/ppermute | solution.py:25
  20.8 0.5 %collective-permute-start.6 = (bf16[528,128]{1,0:T(8,128)(2,1)S(1)}, bf16[528,128]{1,0:T(8,128)(2,1)S(1)}, u32[]{:S(2)}, u32[]{:S(2)}) collective-permute-start(bf16[528,128]{1,0:T(8,128)(2,1)S(1)} %get-tuple-element.65), channel_id=1, source_target_pairs={{0,1},{1,0},{2,3},{3,2},{4,5},{5,4},{6,7},{7,6},{8,9},{9,8},{10,11... | collective-permute-start | bytes 405512 | tf_op jit(solution)/shard_map/ppermute | solution.py:25
  21.3 0.5 %collective-permute-start.7 = (bf16[528,128]{1,0:T(8,128)(2,1)S(1)}, bf16[528,128]{1,0:T(8,128)(2,1)S(1)}, u32[]{:S(2)}, u32[]{:S(2)}) collective-permute-start(bf16[528,128]{1,0:T(8,128)(2,1)S(1)} %get-tuple-element.66), channel_id=1, source_target_pairs={{0,2},{1,3},{2,0},{3,1},{4,6},{5,7},{6,4},{7,5},{8,10},{9,11},{10,... | collective-permute-start | bytes 405512 | tf_op jit(solution)/shard_map/ppermute | solution.py:25
  21.8 0.0 collective-permute-done.4.recv_ref
  21.9 2.6 %collective-permute-start.8 = (f32[8,128]{1,0:T(8,128)S(1)}, f32[8,128]{1,0:T(8,128)S(1)}, u32[]{:S(2)}, u32[]{:S(2)}) collective-permute-start(f32[8,128]{1,0:T(8,128)S(1)} %shard_map.149.refs_3_), channel_id=1, source_target_pairs={{0,16},{4,20},{8,24},{12,28},{16,0},{20,4},{24,8},{28,12},{1,17},{... | collective-permute-start | bytes 12296 | tf_op jit(solution)/shard_map/ppermute | solution.py:374
  24.4 3.4 %shard_map.148 = (f32[4,1024,128]{2,1,0:T(8,128)S(1)}, f32[4,256,128]{2,1,0:T(8,128)S(1)}, f32[4,256,128]{2,1,0:T(8,128)S(1)}, bf16[256,2048]{1,0:T(8,128)(2,1)}) custom-call(bf16[4,256,512]{2,1,0:T(8,128)(2,1)S(1)} %get-tuple-element.43.refs_1_.refs_0_, bf16[4,256,128]{2,1,0:T(8,128)(2,1)S(1)} %get-tuple-element.41.refs_8_.refs_1_, ...), custom_call_target="tpu_custom_call" | custom-call | flops 1610612736 | bytes 1048576 | tf_op jit(solution)/shard_map/pallas_call | solution.py:334
  27.8 0.0 collective-permute-done.5.refs_1_
  27.9 0.1 collective-permute-done.6.refs_2_
  27.9 0.0 collective-permute-done.7.refs_3_
  27.9 0.1 shard_map.150
  28.1 0.0 collective-permute-done.8.refs_6_
  28.1 1.4 %shard_map.151 = (bf16[256,2048]{1,0:T(8,128)(2,1)}, bf16[256,512]{1,0:T(8,128)(2,1)}, bf16[256,512]{1,0:T(8,128)(2,1)}, bf16[64,512]{1,0:T(8,128)(2,1)}, bf16[64,512]{1,0:T(8,128)(2,1)}) custom-call(f32[4,1024,128]{2,1,0:T(8,128)S(1)} %get-tuple-element.58.refs_0_, f32[4,256,128]{2,1,0:T(8,128)S(1)} %get-tuple-element.59.refs_1_, ...), custom_call_target="tpu_custom_call" | custom-call | bytes 1048576 | tf_op jit(solution)/shard_map/pallas_call | solution.py:334
  (1 shorter events, 0.0 us)
Async XLA Ops:
  2.0 12.4 %collective-permute-start.1 = (bf16[128,512]{1,0:T(8,128)(2,1)S(1)}, bf16[128,512]{1,0:T(8,128)(2,1)S(1)}, u32[]{:S(2)}, u32[]{:S(2)}) collective-permute-start(bf16[128,512]{1,0:T(8,128)(2,1)S(1)} %get-tuple-element.51.refs_8_.refs_10_), channel_id=1, source_target_pairs={{0,3},{1,2},{2,1},{3,0},{4,7},{5,6},{6,5},{7,4},{8,11},{9,10},{10,... | collective-permute-start | bytes 393224 | tf_op jit(solution)/shard_map/ppermute | solution.py:25
  5.9 8.5 %collective-permute-start.2 = (bf16[128,512]{1,0:T(8,128)(2,1)S(1)}, bf16[128,512]{1,0:T(8,128)(2,1)S(1)}, u32[]{:S(2)}, u32[]{:S(2)}) collective-permute-start(bf16[128,512]{1,0:T(8,128)(2,1)S(1)} %get-tuple-element.51.refs_8_.refs_10_), channel_id=1, source_target_pairs={{0,1},{1,0},{2,3},{3,2},{4,5},{5,4},{6,7},{7,6},{8,9},{9,8},{10,11... | collective-permute-start | bytes 393224 | tf_op jit(solution)/shard_map/ppermute | solution.py:25
  6.5 7.9 %collective-permute-start.3 = (bf16[128,512]{1,0:T(8,128)(2,1)S(1)}, bf16[128,512]{1,0:T(8,128)(2,1)S(1)}, u32[]{:S(2)}, u32[]{:S(2)}) collective-permute-start(bf16[128,512]{1,0:T(8,128)(2,1)S(1)} %get-tuple-element.51.refs_8_.refs_10_), channel_id=1, source_target_pairs={{0,2},{1,3},{2,0},{3,1},{4,6},{5,7},{6,4},{7,5},{8,10},{9,11},{10,... | collective-permute-start | bytes 393224 | tf_op jit(solution)/shard_map/ppermute | solution.py:25
  6.6 2.0 %collective-permute-start = (s32[1]{0:T(128)}, s32[1]{0:T(128)}, u32[]{:S(2)}, u32[]{:S(2)}) collective-permute-start(s32[1]{0:T(128)} %param.16), channel_id=1, source_target_pairs={{0,4},{4,0},{8,12},{12,8},{16,20},{20,16},{24,28},{28,24},{1,5},{5... | collective-permute-start | bytes 20 | tf_op jit(solution)/shard_map/ppermute | solution.py:374
  12.4 9.5 %collective-permute-start.4 = (f32[8,128]{1,0:T(8,128)S(1)}, f32[8,128]{1,0:T(8,128)S(1)}, u32[]{:S(2)}, u32[]{:S(2)}) collective-permute-start(f32[8,128]{1,0:T(8,128)S(1)} %get-tuple-element.61.tile_ref), channel_id=1, source_target_pairs={{0,8},{4,12},{8,0},{12,4},{16,24},{20,28},{24,16},{28,20},{1,9},{5... | collective-permute-start | bytes 12296 | tf_op jit(solution)/shard_map/ppermute | solution.py:374
  18.3 9.6 %collective-permute-start.5 = (bf16[528,128]{1,0:T(8,128)(2,1)S(1)}, bf16[528,128]{1,0:T(8,128)(2,1)S(1)}, u32[]{:S(2)}, u32[]{:S(2)}) collective-permute-start(bf16[528,128]{1,0:T(8,128)(2,1)S(1)} %get-tuple-element.64), channel_id=1, source_target_pairs={{0,3},{1,2},{2,1},{3,0},{4,7},{5,6},{6,5},{7,4},{8,11},{9,10},{10,... | collective-permute-start | bytes 405512 | tf_op jit(solution)/shard_map/ppermute | solution.py:25
  20.8 7.1 %collective-permute-start.6 = (bf16[528,128]{1,0:T(8,128)(2,1)S(1)}, bf16[528,128]{1,0:T(8,128)(2,1)S(1)}, u32[]{:S(2)}, u32[]{:S(2)}) collective-permute-start(bf16[528,128]{1,0:T(8,128)(2,1)S(1)} %get-tuple-element.65), channel_id=1, source_target_pairs={{0,1},{1,0},{2,3},{3,2},{4,5},{5,4},{6,7},{7,6},{8,9},{9,8},{10,11... | collective-permute-start | bytes 405512 | tf_op jit(solution)/shard_map/ppermute | solution.py:25
  21.3 6.6 %collective-permute-start.7 = (bf16[528,128]{1,0:T(8,128)(2,1)S(1)}, bf16[528,128]{1,0:T(8,128)(2,1)S(1)}, u32[]{:S(2)}, u32[]{:S(2)}) collective-permute-start(bf16[528,128]{1,0:T(8,128)(2,1)S(1)} %get-tuple-element.66), channel_id=1, source_target_pairs={{0,2},{1,3},{2,0},{3,1},{4,6},{5,7},{6,4},{7,5},{8,10},{9,11},{10,... | collective-permute-start | bytes 405512 | tf_op jit(solution)/shard_map/ppermute | solution.py:25
  21.9 6.2 %collective-permute-start.8 = (f32[8,128]{1,0:T(8,128)S(1)}, f32[8,128]{1,0:T(8,128)S(1)}, u32[]{:S(2)}, u32[]{:S(2)}) collective-permute-start(f32[8,128]{1,0:T(8,128)S(1)} %shard_map.149.refs_3_), channel_id=1, source_target_pairs={{0,16},{4,20},{8,24},{12,28},{16,0},{20,4},{24,8},{28,12},{1,17},{... | collective-permute-start | bytes 12296 | tf_op jit(solution)/shard_map/ppermute | solution.py:374

commit v9 on v8

--- a/solution.py
+++ b/solution.py
@@ -75,18 +75,19 @@
     return jnp.sum(jnp.where(row == index, tile, 0.0), 0, keepdims=True)
 
 
-def pack_kernel(kp_hbm, vp_hbm, ko_hbm, vo_hbm, q_hbm, payload_ref, ko_ref, vo_ref, q_ref, sems):
+def pack_kernel(kp_hbm, vp_hbm, ko_hbm, vo_hbm, q_hbm, u_hbm, payload_ref, ko_ref, vo_ref, q_ref, u_ref, sems):
     part = kp_hbm.shape[0]
-    heads, width = ko_ref.shape[0], q_ref.shape[1]
+    width = q_ref.shape[2]
     copies = [
         pltpu.make_async_copy(kp_hbm, payload_ref.at[:part], sems.at[0, 0]),
-        pltpu.make_async_copy(vp_hbm, payload_ref.at[part:], sems.at[1, 0]),
-        pltpu.make_async_copy(q_hbm.at[:, :width], q_ref, sems.at[2, 0]),
+        pltpu.make_async_copy(vp_hbm, payload_ref.at[part:], sems.at[0, 1]),
     ]
-    for g in range(heads):
-        cols = columns_of(g, HEAD_SIZE)
-        copies.append(pltpu.make_async_copy(ko_hbm.at[:, cols], ko_ref.at[g], sems.at[3, g]))
-        copies.append(pltpu.make_async_copy(vo_hbm.at[:, cols], vo_ref.at[g], sems.at[4, g]))
+    for g in range(q_ref.shape[0]):
+        cols = columns_of(g, width)
+        copies.append(pltpu.make_async_copy(q_hbm.at[:, cols], q_ref.at[g], sems.at[2, g]))
+        copies.append(pltpu.make_async_copy(u_hbm.at[:, cols], u_ref.at[g], sems.at[1, g]))
+    copies.append(pltpu.make_async_copy(ko_hbm, ko_ref, sems.at[3, 0]))
+    copies.append(pltpu.make_async_copy(vo_hbm, vo_ref, sems.at[4, 0]))
     for copy in copies:
         copy.start()
     for copy in copies:
@@ -103,18 +104,13 @@
 
 
 def own_kernel(group, counts, *refs):
-    small_hbm, refs = refs[: 4 + counts], refs[4 + counts :]
-    q_hbm, u_hbm, q_first, ko_ref, vo_ref = refs[:5]
-    q_ref, u_ref, att_ref, lse_ref, tile_ref, alive_ref, length_ref = refs[5:12]
-    qt_ref, ut_ref, s_ref, reward_ref = refs[12:16]
-    small_refs, sems, small_sems = refs[16:-2], refs[-2], refs[-1]
+    kept_ref, spans_ref, payoff_ref = refs[:3]
+    small_hbm, refs = refs[3 : 4 + counts], refs[4 + counts :]
+    u_ref, q_ref, ko_ref, vo_ref = refs[:4]
+    att_ref, lse_ref, tile_ref, alive_ref, length_ref = refs[4:9]
+    qt_ref, ut_ref, s_ref, reward_ref = refs[9:13]
+    small_refs, small_sems = refs[13:-1], refs[-1]
     heads, tokens, width = q_ref.shape
-
-    def load(g):
-        return pltpu.make_async_copy(q_hbm.at[:, columns_of(g, width)], q_ref.at[g], sems.at[0, g])
-
-    def late_load(g):
-        return pltpu.make_async_copy(u_hbm.at[:, columns_of(g, width)], u_ref.at[g], sems.at[1, g])
 
     small = [
         pltpu.make_async_copy(a, b, small_sems.at[i])
@@ -122,15 +118,12 @@
     ]
     for copy in small:
         copy.start()
-    for g in range(1, heads):
-        load(g).start()
-    for g in range(heads):
-        late_load(g).start()
 
     mask = causal_mask(tokens, group)
 
     def step(g, carry):
-        q, ko, vo = stacked(q_ref[g]), ko_ref[g], vo_ref[g]
+        cols = columns_of(g, HEAD_SIZE)
+        q, ko, vo = stacked(q_ref[g]), ko_ref[:, cols], vo_ref[:, cols]
         s = jnp.where(mask, dot(q, ko, 1, 1) * POWER, -1e30)
         s_ref[g] = s
         top = jnp.max(s, 1, keepdims=True)
@@ -140,13 +133,13 @@
         att_ref[g] = both[:, :HEAD_SIZE] / mass
         lse_ref[g] = jnp.log2(mass) + top
         qt_ref[g] = q.T
+        ut_ref[g] = stacked(u_ref[g]).T
         return carry
 
-    q_ref[0] = q_first[...]
-    step(0, 0)
+    lax.fori_loop(0, heads, step, 0, unroll=True)
     for copy in small:
         copy.wait()
-    kept_ref, spaces_ref, spans_ref, payoff_ref = small_refs[:4]
+    spaces_ref = small_refs[0]
     reward_ref[...] = reward_rows(payoff_ref[0, 0])
     member = lax.axis_index("resp")
     kept = kept_ref[0]
@@ -157,18 +150,10 @@
         alive += jnp.where((row == spaces_ref[0, i]) & (i < kept), 1.0, 0.0)
         own_alive += jnp.where((spaces_ref[0, i] == member) & (i < kept), 1, 0)
     alive_ref[...] = alive
-    count = kept + sum(r[0] for r in small_refs[4:])
+    count = kept + sum(r[0] for r in small_refs[1:])
     tile_ref[...] = jnp.full(tile_ref.shape, count.astype(f32))
     length = own_alive * spans_ref[0, 0] * BLOCK
     length_ref[...] = jnp.full(length_ref.shape, length.astype(f32))
-
-    for g in range(1, heads):
-        load(g).wait()
-    lax.fori_loop(1, heads, step, 0, unroll=True)
-    for g in range(heads):
-        late_load(g).wait()
-    for g in range(heads):
-        ut_ref[g] = stacked(u_ref[g]).T
 
 
 def prefix_kernel(n, *refs):
@@ -244,7 +229,7 @@
     def step(g, carry):
         cols = columns_of(g, HEAD_SIZE)
         keys = jnp.concatenate([r[:part, cols] for r in pay_refs], 0)
-        u, ko, vo = stacked(u_ref[g]), ko_ref[g], vo_ref[g]
+        u, ko, vo = stacked(u_ref[g]), ko_ref[:, cols], vo_ref[:, cols]
         p = jnp.exp2(s_ref[g] - spread(line_ref[g], tokens))
         dp = dot(u, vo, 1, 1)
         ds = (p * (dp - spread(delta_ref[g], tokens))).astype(bf16)
@@ -326,6 +311,7 @@
 
     vmem = pl.BlockSpec(memory_space=pltpu.VMEM)
     hbm = pl.BlockSpec(memory_space=pl.ANY)
+    scalar = pl.BlockSpec(memory_space=pltpu.SMEM)
 
     def pinned(x):
         return pltpu.with_memory_space_constraint(x, pltpu.HBM)
@@ -358,13 +344,13 @@
     wide, slim = (heads, tokens, width), (heads, tokens, HEAD_SIZE)
     q, ko, vo, u = q[0, 0], ko[0, 0], vo[0, 0], u[0, 0]
 
-    payload, ko_in, vo_in, q_first = call(
+    payload, ko_in, vo_in, q_in, u_in = call(
         pack_kernel,
         0,
-        [(hbm, pinned(x)) for x in (kp[0], vp[0], ko, vo, q)],
+        [(hbm, pinned(x)) for x in (kp[0], vp[0], ko, vo, q, u)],
         [kept_in((2 * part, kv_width), bf16)]
-        + [kept_in(slim, bf16)] * 2
-        + [kept_in((tokens, width), bf16)],
+        + [kept_in((tokens, kv_width), bf16)] * 2
+        + [kept_in(wide, bf16)] * 2,
         [sems],
     )
     order = [0] + sorted(range(1, n), key=lambda k: -bin(k).count("1"))
@@ -373,18 +359,17 @@
     def across(x, k):
         return lax.ppermute(x, "prompt", [(i, i ^ k) for i in range(n_prompt)])
 
-    small = [kept, pinned(spaces), spans, payoffs, across(kept, 1)]
-    q_in, u_in, own, own_lse, tile, alive, length, qt, ut, scores, reward = call(
+    small = [pinned(spaces), across(kept, 1)]
+    own, own_lse, tile, alive, length, qt, ut, scores, reward = call(
         functools.partial(own_kernel, group, 1),
         2,
-        [(hbm, x) for x in small]
-        + [(hbm, pinned(x)) for x in (q, u)]
-        + [(vmem, x) for x in (q_first, ko_in, vo_in)],
-        [kept_in(wide, bf16)] * 2
-        + [stat, stat, tile_kind, slots_kind, tile_kind] + [kept_in((heads, HEAD_SIZE, rows), bf16)] * 2
+        [(scalar, x) for x in (kept, spans, payoffs)]
+        + [(hbm, x) for x in small]
+        + [(vmem, x) for x in (u_in, q_in, ko_in, vo_in)],
+        [stat, stat, tile_kind, slots_kind, tile_kind] + [kept_in((heads, HEAD_SIZE, rows), bf16)] * 2
         + [kept_in((heads, rows, tokens), f32), kept_in((EXTRA, HEAD_SIZE), f32)],
         [pltpu.SMEM(x.shape, x.dtype) for x in small]
-        + [sems, pltpu.SemaphoreType.DMA((len(small),))],
+        + [pltpu.SemaphoreType.DMA((len(small),))],
     )
     k = 2
     while 4 * k < n_prompt:

time: 29.7 us -> 29.2 us (0.983)
  Pallas kernels: 13.9 us -> 13.4 us
    pallas_call x7, Pallas kernels: 13.9 us -> 13.4 us  [call(): pl.pallas_call(kernel, in_specs=[spec for spec, _ in ins], out_specs=[spe...]
  transfers between devices with their start and end apart: 9 -> 9, of which waited for: 1 -> 1; matrix products, arithmetic and copies ran while one was open for 0% -> 0% of each run, Pallas kernels for 38% -> 35%
where the time goes in v9:
time: 29.2 us; the launch traced here: 29 us
  Pallas kernels  13.4 us (46%)
  starting transfers between devices  12.8 us (44%)
  between operations  2.64 us (9%)
    pallas_call x7, Pallas kernels, call(): pl.pallas_call(kernel, in_specs=[spec for spec, _ in ins], out_specs=[spe...  13.4 us
    ppermute x6, starting transfers between devices, swap(): return lax.ppermute(x, 'resp', [(i, i ^ k) for i in range(n)])  8.16 us
    ppermute x3, starting transfers between devices, across(): return lax.ppermute(x, 'prompt', [(i, i ^ k) for i in range(n_prompt)])  4.64 us
  transfers between devices with their start and end apart: 9, of which 1 were waited for; matrix products, arithmetic and copies ran while one was open for 0% of the time, Pallas kernels for 35%

profile of v9, /device:TPU:0, one launch (start us, length us, event | category | flops | bytes accessed | tf_op | source)
XLA Modules:
  0.0 29.0 jit_solution(9201736662491385950)
XLA Ops:
  0.6 1.9 %shard_map.145 = (bf16[128,512]{1,0:T(8,128)(2,1)S(1)}, bf16[256,512]{1,0:T(8,128)(2,1)S(1)}, bf16[256,512]{1,0:T(8,128)(2,1)S(1)}, bf16[4,256,512]{2,1,0:T(8,128)(2,1)S(1)}, bf16[4,256,512]{2,1,0:T(8,128)(2,1)S(1)}) custom-call(bf16[64,512]{1,0:T(8,128)(2,1)} %bitcast.16, bf16[64,512]{1,0:T(8,128)(2,1)} %bitcast.17, bf16[256,512]{1,0:T(8,128)(2,1)} %bitcast.14, ...), custom_call_target="tpu_custom_call" | custom-call | bytes 1048576 | tf_op jit(solution)/shard_map/pallas_call | solution.py:320
  2.6 4.0 %collective-permute-start.1 = (bf16[128,512]{1,0:T(8,128)(2,1)S(1)}, bf16[128,512]{1,0:T(8,128)(2,1)S(1)}, u32[]{:S(2)}, u32[]{:S(2)}) collective-permute-start(bf16[128,512]{1,0:T(8,128)(2,1)S(1)} %get-tuple-element.49.refs_8_.refs_10_), channel_id=1, source_target_pairs={{0,3},{1,2},{2,1},{3,0},{4,7},{5,6},{6,5},{7,4},{8,11},{9,10},{10,... | collective-permute-start | bytes 393224 | tf_op jit(solution)/shard_map/ppermute | solution.py:25
  6.5 0.5 %collective-permute-start.2 = (bf16[128,512]{1,0:T(8,128)(2,1)S(1)}, bf16[128,512]{1,0:T(8,128)(2,1)S(1)}, u32[]{:S(2)}, u32[]{:S(2)}) collective-permute-start(bf16[128,512]{1,0:T(8,128)(2,1)S(1)} %get-tuple-element.49.refs_8_.refs_10_), channel_id=1, source_target_pairs={{0,1},{1,0},{2,3},{3,2},{4,5},{5,4},{6,7},{7,6},{8,9},{9,8},{10,11... | collective-permute-start | bytes 393224 | tf_op jit(solution)/shard_map/ppermute | solution.py:25
  7.1 0.1 collective-permute-start.3
  7.2 0.0 collective-permute-start
  9.1 0.0 collective-permute-done.refs_4_
  9.1 2.9 %shard_map.146 = (f32[4,1024,128]{2,1,0:T(8,128)S(1)}, f32[4,1024,128]{2,1,0:T(8,128)S(1)}, f32[8,128]{1,0:T(8,128)S(1)}, f32[8,128]{1,0:T(8,128)S(1)}, f32[8,12...) custom-call(s32[1]{0:T(128)S(6)} %copy.16.refs_0_, ...), custom_call_target="tpu_custom_call" | custom-call | flops 536870912 | bytes 1048576 | tf_op jit(solution)/shard_map/pallas_call | solution.py:320
  12.0 2.0 %collective-permute-start.4 = (f32[8,128]{1,0:T(8,128)S(1)}, f32[8,128]{1,0:T(8,128)S(1)}, u32[]{:S(2)}, u32[]{:S(2)}) collective-permute-start(f32[8,128]{1,0:T(8,128)S(1)} %get-tuple-element.59.tile_ref), channel_id=1, source_target_pairs={{0,8},{4,12},{8,0},{12,4},{16,24},{20,28},{24,16},{28,20},{1,9},{5... | collective-permute-start | bytes 12296 | tf_op jit(solution)/shard_map/ppermute | solution.py:360
  14.1 0.0 collective-permute-done.1.refs_9_.refs_11_
  14.1 0.0 collective-permute-done.2.refs_10_.refs_12_
  14.1 0.0 collective-permute-done.3.refs_11_.refs_13_
  14.1 3.7 %shard_map.147 = (bf16[4,256,512]{2,1,0:T(8,128)(2,1)S(1)}, bf16[4,1024,256]{2,1,0:T(8,128)(2,1)S(1)}, f32[4,1024,128]{2,1,0:T(8,128)S(1)}, f32[4,1024,128]{2,1,...) custom-call(bf16[4,256,512]{2,1,0:T(8,128)(2,1)S(1)} %get-tuple-elem, ...), custom_call_target="tpu_custom_call" | custom-call | flops 1342177280 | bytes 1048576 | tf_op jit(solution)/shard_map/pallas_call | solution.py:320
  17.8 2.5 %collective-permute-start.5 = (bf16[528,128]{1,0:T(8,128)(2,1)S(1)}, bf16[528,128]{1,0:T(8,128)(2,1)S(1)}, u32[]{:S(2)}, u32[]{:S(2)}) collective-permute-start(bf16[528,128]{1,0:T(8,128)(2,1)S(1)} %get-tuple-element.62), channel_id=1, source_target_pairs={{0,3},{1,2},{2,1},{3,0},{4,7},{5,6},{6,5},{7,4},{8,11},{9,10},{10,... | collective-permute-start | bytes 405512 | tf_op jit(solution)/shard_map/ppermute | solution.py:25
  20.3 0.5 %collective-permute-start.6 = (bf16[528,128]{1,0:T(8,128)(2,1)S(1)}, bf16[528,128]{1,0:T(8,128)(2,1)S(1)}, u32[]{:S(2)}, u32[]{:S(2)}) collective-permute-start(bf16[528,128]{1,0:T(8,128)(2,1)S(1)} %get-tuple-element.63), channel_id=1, source_target_pairs={{0,1},{1,0},{2,3},{3,2},{4,5},{5,4},{6,7},{7,6},{8,9},{9,8},{10,11... | collective-permute-start | bytes 405512 | tf_op jit(solution)/shard_map/ppermute | solution.py:25
  20.8 0.5 %collective-permute-start.7 = (bf16[528,128]{1,0:T(8,128)(2,1)S(1)}, bf16[528,128]{1,0:T(8,128)(2,1)S(1)}, u32[]{:S(2)}, u32[]{:S(2)}) collective-permute-start(bf16[528,128]{1,0:T(8,128)(2,1)S(1)} %get-tuple-element.64), channel_id=1, source_target_pairs={{0,2},{1,3},{2,0},{3,1},{4,6},{5,7},{6,4},{7,5},{8,10},{9,11},{10,... | collective-permute-start | bytes 405512 | tf_op jit(solution)/shard_map/ppermute | solution.py:25
  21.4 0.0 collective-permute-done.4.recv_ref
  21.4 2.6 %collective-permute-start.8 = (f32[8,128]{1,0:T(8,128)S(1)}, f32[8,128]{1,0:T(8,128)S(1)}, u32[]{:S(2)}, u32[]{:S(2)}) collective-permute-start(f32[8,128]{1,0:T(8,128)S(1)} %shard_map.149.refs_3_), channel_id=1, source_target_pairs={{0,16},{4,20},{8,24},{12,28},{16,0},{20,4},{24,8},{28,12},{1,17},{... | collective-permute-start | bytes 12296 | tf_op jit(solution)/shard_map/ppermute | solution.py:360
  23.9 3.4 %shard_map.148 = (f32[4,1024,128]{2,1,0:T(8,128)S(1)}, f32[4,256,128]{2,1,0:T(8,128)S(1)}, f32[4,256,128]{2,1,0:T(8,128)S(1)}, bf16[256,2048]{1,0:T(8,128)(2,1)}) custom-call(bf16[4,256,512]{2,1,0:T(8,128)(2,1)S(1)} %get-tuple-element.39.refs_5_.refs_1_.refs_0_, bf16[256,512]{1,0:T(8,128)(2,1)S(1)} %get-tuple-element.40.refs_7_.refs_1_, ...), custom_call_target="tpu_custom_call" | custom-call | flops 1610612736 | bytes 1048576 | tf_op jit(solution)/shard_map/pallas_call | solution.py:320
  27.3 0.0 collective-permute-done.5.refs_1_
  27.3 0.1 collective-permute-done.6.refs_2_
  27.5 0.0 collective-permute-done.7.refs_3_
  27.5 0.1 shard_map.150
  27.6 0.0 collective-permute-done.8.refs_6_
  27.6 1.4 %shard_map.151 = (bf16[256,2048]{1,0:T(8,128)(2,1)}, bf16[256,512]{1,0:T(8,128)(2,1)}, bf16[256,512]{1,0:T(8,128)(2,1)}, bf16[64,512]{1,0:T(8,128)(2,1)}, bf16[64,512]{1,0:T(8,128)(2,1)}) custom-call(f32[4,1024,128]{2,1,0:T(8,128)S(1)} %get-tuple-element.56.refs_0_, f32[4,256,128]{2,1,0:T(8,128)S(1)} %get-tuple-element.57.refs_1_, ...), custom_call_target="tpu_custom_call" | custom-call | bytes 1048576 | tf_op jit(solution)/shard_map/pallas_call | solution.py:320
  (1 shorter events, 0.0 us)
Async XLA Ops:
  2.6 11.5 %collective-permute-start.1 = (bf16[128,512]{1,0:T(8,128)(2,1)S(1)}, bf16[128,512]{1,0:T(8,128)(2,1)S(1)}, u32[]{:S(2)}, u32[]{:S(2)}) collective-permute-start(bf16[128,512]{1,0:T(8,128)(2,1)S(1)} %get-tuple-element.49.refs_8_.refs_10_), channel_id=1, source_target_pairs={{0,3},{1,2},{2,1},{3,0},{4,7},{5,6},{6,5},{7,4},{8,11},{9,10},{10,... | collective-permute-start | bytes 393224 | tf_op jit(solution)/shard_map/ppermute | solution.py:25
  6.5 7.5 %collective-permute-start.2 = (bf16[128,512]{1,0:T(8,128)(2,1)S(1)}, bf16[128,512]{1,0:T(8,128)(2,1)S(1)}, u32[]{:S(2)}, u32[]{:S(2)}) collective-permute-start(bf16[128,512]{1,0:T(8,128)(2,1)S(1)} %get-tuple-element.49.refs_8_.refs_10_), channel_id=1, source_target_pairs={{0,1},{1,0},{2,3},{3,2},{4,5},{5,4},{6,7},{7,6},{8,9},{9,8},{10,11... | collective-permute-start | bytes 393224 | tf_op jit(solution)/shard_map/ppermute | solution.py:25
  7.1 7.0 %collective-permute-start.3 = (bf16[128,512]{1,0:T(8,128)(2,1)S(1)}, bf16[128,512]{1,0:T(8,128)(2,1)S(1)}, u32[]{:S(2)}, u32[]{:S(2)}) collective-permute-start(bf16[128,512]{1,0:T(8,128)(2,1)S(1)} %get-tuple-element.49.refs_8_.refs_10_), channel_id=1, source_target_pairs={{0,2},{1,3},{2,0},{3,1},{4,6},{5,7},{6,4},{7,5},{8,10},{9,11},{10,... | collective-permute-start | bytes 393224 | tf_op jit(solution)/shard_map/ppermute | solution.py:25
  7.2 2.0 %collective-permute-start = (s32[1]{0:T(128)}, s32[1]{0:T(128)}, u32[]{:S(2)}, u32[]{:S(2)}) collective-permute-start(s32[1]{0:T(128)} %param.16), channel_id=1, source_target_pairs={{0,4},{4,0},{8,12},{12,8},{16,20},{20,16},{24,28},{28,24},{1,5},{5... | collective-permute-start | bytes 20 | tf_op jit(solution)/shard_map/ppermute | solution.py:360
  12.0 9.3 %collective-permute-start.4 = (f32[8,128]{1,0:T(8,128)S(1)}, f32[8,128]{1,0:T(8,128)S(1)}, u32[]{:S(2)}, u32[]{:S(2)}) collective-permute-start(f32[8,128]{1,0:T(8,128)S(1)} %get-tuple-element.59.tile_ref), channel_id=1, source_target_pairs={{0,8},{4,12},{8,0},{12,4},{16,24},{20,28},{24,16},{28,20},{1,9},{5... | collective-permute-start | bytes 12296 | tf_op jit(solution)/shard_map/ppermute | solution.py:360
  17.8 9.5 %collective-permute-start.5 = (bf16[528,128]{1,0:T(8,128)(2,1)S(1)}, bf16[528,128]{1,0:T(8,128)(2,1)S(1)}, u32[]{:S(2)}, u32[]{:S(2)}) collective-permute-start(bf16[528,128]{1,0:T(8,128)(2,1)S(1)} %get-tuple-element.62), channel_id=1, source_target_pairs={{0,3},{1,2},{2,1},{3,0},{4,7},{5,6},{6,5},{7,4},{8,11},{9,10},{10,... | collective-permute-start | bytes 405512 | tf_op jit(solution)/shard_map/ppermute | solution.py:25
  20.3 7.1 %collective-permute-start.6 = (bf16[528,128]{1,0:T(8,128)(2,1)S(1)}, bf16[528,128]{1,0:T(8,128)(2,1)S(1)}, u32[]{:S(2)}, u32[]{:S(2)}) collective-permute-start(bf16[528,128]{1,0:T(8,128)(2,1)S(1)} %get-tuple-element.63), channel_id=1, source_target_pairs={{0,1},{1,0},{2,3},{3,2},{4,5},{5,4},{6,7},{7,6},{8,9},{9,8},{10,11... | collective-permute-start | bytes 405512 | tf_op jit(solution)/shard_map/ppermute | solution.py:25
  20.8 6.6 %collective-permute-start.7 = (bf16[528,128]{1,0:T(8,128)(2,1)S(1)}, bf16[528,128]{1,0:T(8,128)(2,1)S(1)}, u32[]{:S(2)}, u32[]{:S(2)}) collective-permute-start(bf16[528,128]{1,0:T(8,128)(2,1)S(1)} %get-tuple-element.64), channel_id=1, source_target_pairs={{0,2},{1,3},{2,0},{3,1},{4,6},{5,7},{6,4},{7,5},{8,10},{9,11},{10,... | collective-permute-start | bytes 405512 | tf_op jit(solution)/shard_map/ppermute | solution.py:25
  21.4 6.2 %collective-permute-start.8 = (f32[8,128]{1,0:T(8,128)S(1)}, f32[8,128]{1,0:T(8,128)S(1)}, u32[]{:S(2)}, u32[]{:S(2)}) collective-permute-start(f32[8,128]{1,0:T(8,128)S(1)} %shard_map.149.refs_3_), channel_id=1, source_target_pairs={{0,16},{4,20},{8,24},{12,28},{16,0},{20,4},{24,8},{28,12},{1,17},{... | collective-permute-start | bytes 12296 | tf_op jit(solution)/shard_map/ppermute | solution.py:360

commit v10 on v9

--- a/solution.py
+++ b/solution.py
@@ -75,19 +75,12 @@
     return jnp.sum(jnp.where(row == index, tile, 0.0), 0, keepdims=True)
 
 
-def pack_kernel(kp_hbm, vp_hbm, ko_hbm, vo_hbm, q_hbm, u_hbm, payload_ref, ko_ref, vo_ref, q_ref, u_ref, sems):
+def pack_kernel(kp_hbm, vp_hbm, payload_ref, sems):
     part = kp_hbm.shape[0]
-    width = q_ref.shape[2]
     copies = [
         pltpu.make_async_copy(kp_hbm, payload_ref.at[:part], sems.at[0, 0]),
         pltpu.make_async_copy(vp_hbm, payload_ref.at[part:], sems.at[0, 1]),
     ]
-    for g in range(q_ref.shape[0]):
-        cols = columns_of(g, width)
-        copies.append(pltpu.make_async_copy(q_hbm.at[:, cols], q_ref.at[g], sems.at[2, g]))
-        copies.append(pltpu.make_async_copy(u_hbm.at[:, cols], u_ref.at[g], sems.at[1, g]))
-    copies.append(pltpu.make_async_copy(ko_hbm, ko_ref, sems.at[3, 0]))
-    copies.append(pltpu.make_async_copy(vo_hbm, vo_ref, sems.at[4, 0]))
     for copy in copies:
         copy.start()
     for copy in copies:
@@ -105,12 +98,14 @@
 
 def own_kernel(group, counts, *refs):
     kept_ref, spans_ref, payoff_ref = refs[:3]
+    width = group * HEAD_SIZE
     small_hbm, refs = refs[3 : 4 + counts], refs[4 + counts :]
     u_ref, q_ref, ko_ref, vo_ref = refs[:4]
     att_ref, lse_ref, tile_ref, alive_ref, length_ref = refs[4:9]
     qt_ref, ut_ref, s_ref, reward_ref = refs[9:13]
     small_refs, small_sems = refs[13:-1], refs[-1]
-    heads, tokens, width = q_ref.shape
+    tokens = q_ref.shape[0]
+    heads = q_ref.shape[1] // width
 
     small = [
         pltpu.make_async_copy(a, b, small_sems.at[i])
@@ -123,7 +118,7 @@
 
     def step(g, carry):
         cols = columns_of(g, HEAD_SIZE)
-        q, ko, vo = stacked(q_ref[g]), ko_ref[:, cols], vo_ref[:, cols]
+        q, ko, vo = stacked(q_ref[:, columns_of(g, width)]), ko_ref[:, cols], vo_ref[:, cols]
         s = jnp.where(mask, dot(q, ko, 1, 1) * POWER, -1e30)
         s_ref[g] = s
         top = jnp.max(s, 1, keepdims=True)
@@ -133,7 +128,7 @@
         att_ref[g] = both[:, :HEAD_SIZE] / mass
         lse_ref[g] = jnp.log2(mass) + top
         qt_ref[g] = q.T
-        ut_ref[g] = stacked(u_ref[g]).T
+        ut_ref[g] = stacked(u_ref[:, columns_of(g, width)]).T
         return carry
 
     lax.fori_loop(0, heads, step, 0, unroll=True)
@@ -163,7 +158,7 @@
     term_refs = refs[12 + n :]
     for ref in term_refs:
         ref[-EXTRA:] = reward_ref[...].astype(ref.dtype)
-    heads, tokens, width = q_ref.shape
+    heads, tokens, width = out_ref.shape
     group = width // HEAD_SIZE
     part = pay_refs[0].shape[0] // 2
     token = lax.broadcasted_iota(i32, (tokens, HEAD_SIZE), 0).astype(f32)
@@ -176,9 +171,9 @@
         cols = columns_of(g, HEAD_SIZE)
         keys = jnp.concatenate([r[:part, cols] for r in pay_refs], 0)
         values = jnp.concatenate([r[part : 2 * part, cols] for r in pay_refs], 0)
-        q = stacked(q_ref[g])
+        q = stacked(q_ref[:, columns_of(g, width)])
         s = dot(q, keys, 1, 1)
-        u = stacked(u_ref[g])
+        u = stacked(u_ref[:, columns_of(g, width)])
         dp = dot(u, values, 1, 1)
         own_lse = lse_ref[g]
         top = jnp.maximum(jnp.max(s, 1, keepdims=True) * POWER, own_lse)
@@ -216,20 +211,20 @@
     pay_refs = refs[10 : 10 + n]
     dq_ref, dko_ref, dvo_ref = refs[10 + n : 13 + n]
     out_hbm, sems = refs[13 + n :] if len(refs) > 13 + n else (None, None)
-    _, tokens, width = u_ref.shape
+    heads, tokens, width = att_ref.shape
     part = pay_refs[0].shape[0] // 2
 
     def store(g):
         return pltpu.make_async_copy(att_ref.at[g], out_hbm.at[:, columns_of(g, width)], sems.at[0, g])
 
-    stored = range(u_ref.shape[0]) if out_hbm is not None else ()
+    stored = range(heads) if out_hbm is not None else ()
     for g in stored:
         store(g).start()
 
     def step(g, carry):
         cols = columns_of(g, HEAD_SIZE)
         keys = jnp.concatenate([r[:part, cols] for r in pay_refs], 0)
-        u, ko, vo = stacked(u_ref[g]), ko_ref[:, cols], vo_ref[:, cols]
+        u, ko, vo = stacked(u_ref[:, columns_of(g, width)]), ko_ref[:, cols], vo_ref[:, cols]
         p = jnp.exp2(s_ref[g] - spread(line_ref[g], tokens))
         dp = dot(u, vo, 1, 1)
         ds = (p * (dp - spread(delta_ref[g], tokens))).astype(bf16)
@@ -344,15 +339,14 @@
     wide, slim = (heads, tokens, width), (heads, tokens, HEAD_SIZE)
     q, ko, vo, u = q[0, 0], ko[0, 0], vo[0, 0], u[0, 0]
 
-    payload, ko_in, vo_in, q_in, u_in = call(
+    (payload,) = call(
         pack_kernel,
-        0,
-        [(hbm, pinned(x)) for x in (kp[0], vp[0], ko, vo, q, u)],
-        [kept_in((2 * part, kv_width), bf16)]
-        + [kept_in((tokens, kv_width), bf16)] * 2
-        + [kept_in(wide, bf16)] * 2,
+        20,
+        [(hbm, pinned(kp[0])), (hbm, pinned(vp[0]))],
+        [kept_in((2 * part, kv_width), bf16)],
         [sems],
     )
+    q_in, u_in, ko_in, vo_in = q, u, ko, vo
     order = [0] + sorted(range(1, n), key=lambda k: -bin(k).count("1"))
     pays = [payload] + [swap(payload, n, k) for k in order[1:]]
 

time: 29.2 us -> 28.6 us (0.979)
  Pallas kernels: 13.4 us -> 12.8 us
    pallas_call x7, Pallas kernels: 13.4 us -> 12.8 us  [call(): pl.pallas_call(kernel, in_specs=[spec for spec, _ in ins], out_specs=[spe...]
  transfers between devices with their start and end apart: 9 -> 9, of which waited for: 1 -> 1; matrix products, arithmetic and copies ran while one was open for 0% -> 0% of each run, Pallas kernels for 35% -> 36%
where the time goes in v10:
time: 28.6 us; the launch traced here: 28.5 us
  Pallas kernels  12.8 us (45%)
  starting transfers between devices  12.8 us (45%)
  between operations  2.71 us (9%)
    pallas_call x7, Pallas kernels, call(): pl.pallas_call(kernel, in_specs=[spec for spec, _ in ins], out_specs=[spe...  12.8 us
    ppermute x6, starting transfers between devices, swap(): return lax.ppermute(x, 'resp', [(i, i ^ k) for i in range(n)])  8.16 us
    ppermute x3, starting transfers between devices, across(): return lax.ppermute(x, 'prompt', [(i, i ^ k) for i in range(n_prompt)])  4.64 us
  transfers between devices with their start and end apart: 9, of which 1 were waited for; matrix products, arithmetic and copies ran while one was open for 0% of the time, Pallas kernels for 36%

profile of v10, /device:TPU:0, one launch (start us, length us, event | category | flops | bytes accessed | tf_op | source)
XLA Modules:
  0.0 28.5 jit_solution(16590220828735917807)
XLA Ops:
  0.7 1.2 %shard_map.146.refs_8_.refs_10_ = bf16[128,512]{1,0:T(8,128)(2,1)S(1)} custom-call(bf16[64,512]{1,0:T(8,128)(2,1)} %bitcast.25, bf16[64,512]{1,0:T(8,128)(2,1)} %bitcast.26), custom_call_target="tpu_custom_call" | custom-call | flops 5368709120 | bytes 1048576 | tf_op jit(solution)/shard_map/pallas_call | solution.py:315
  1.9 4.0 %collective-permute-start.1 = (bf16[128,512]{1,0:T(8,128)(2,1)S(1)}, bf16[128,512]{1,0:T(8,128)(2,1)S(1)}, u32[]{:S(2)}, u32[]{:S(2)}) collective-permute-start(bf16[128,512]{1,0:T(8,128)(2,1)S(1)} %shard_map.146.refs_8_.refs_10_), channel_id=1, source_target_pairs={{0,3},{1,2},{2,1},{3,0},{4,7},{5,6},{6,5},{7,4},{8,11},{9,10},{10,... | collective-permute-start | bytes 393224 | tf_op jit(solution)/shard_map/ppermute | solution.py:25
  5.8 0.5 %collective-permute-start.2 = (bf16[128,512]{1,0:T(8,128)(2,1)S(1)}, bf16[128,512]{1,0:T(8,128)(2,1)S(1)}, u32[]{:S(2)}, u32[]{:S(2)}) collective-permute-start(bf16[128,512]{1,0:T(8,128)(2,1)S(1)} %shard_map.146.refs_8_.refs_10_), channel_id=1, source_target_pairs={{0,1},{1,0},{2,3},{3,2},{4,5},{5,4},{6,7},{7,6},{8,9},{9,8},{10,11... | collective-permute-start | bytes 393224 | tf_op jit(solution)/shard_map/ppermute | solution.py:25
  6.4 0.1 collective-permute-start.3
  6.5 0.0 collective-permute-start
  8.4 0.0 collective-permute-done.refs_4_
  8.5 2.8 %shard_map.145 = (f32[4,1024,128]{2,1,0:T(8,128)S(1)}, f32[4,1024,128]{2,1,0:T(8,128)S(1)}, f32[8,128]{1,0:T(8,128)S(1)}, f32[8,128]{1,0:T(8,128)S(1)}, f32[8,12...) custom-call(s32[1]{0:T(128)S(6)} %copy.16.refs_0_, ...), custom_call_target="tpu_custom_call" | custom-call | flops 536870912 | bytes 1048576 | tf_op jit(solution)/shard_map/pallas_call | solution.py:315
  11.3 2.0 %collective-permute-start.4 = (f32[8,128]{1,0:T(8,128)S(1)}, f32[8,128]{1,0:T(8,128)S(1)}, u32[]{:S(2)}, u32[]{:S(2)}) collective-permute-start(f32[8,128]{1,0:T(8,128)S(1)} %get-tuple-element.49.tile_ref), channel_id=1, source_target_pairs={{0,8},{4,12},{8,0},{12,4},{16,24},{20,28},{24,16},{28,20},{1,9},{5... | collective-permute-start | bytes 12296 | tf_op jit(solution)/shard_map/ppermute | solution.py:354
  13.4 0.0 collective-permute-done.1.refs_9_.refs_11_
  13.4 0.0 collective-permute-done.2.refs_10_.refs_12_
  13.4 0.0 collective-permute-done.3.refs_11_.refs_13_
  13.4 3.9 %shard_map.147 = (bf16[4,256,512]{2,1,0:T(8,128)(2,1)S(1)}, bf16[4,1024,256]{2,1,0:T(8,128)(2,1)S(1)}, f32[4,1024,128]{2,1,0:T(8,128)S(1)}, f32[4,1024,128]{2,1,...) custom-call(bf16[256,2048]{1,0:T(8,128)(2,1)S(1)} %bitcast.16, ...), custom_call_target="tpu_custom_call" | custom-call | flops 1342177280 | bytes 1048576 | tf_op jit(solution)/shard_map/pallas_call | solution.py:315
  17.3 2.5 %collective-permute-start.5 = (bf16[528,128]{1,0:T(8,128)(2,1)S(1)}, bf16[528,128]{1,0:T(8,128)(2,1)S(1)}, u32[]{:S(2)}, u32[]{:S(2)}) collective-permute-start(bf16[528,128]{1,0:T(8,128)(2,1)S(1)} %get-tuple-element.52), channel_id=1, source_target_pairs={{0,3},{1,2},{2,1},{3,0},{4,7},{5,6},{6,5},{7,4},{8,11},{9,10},{10,... | collective-permute-start | bytes 405512 | tf_op jit(solution)/shard_map/ppermute | solution.py:25
  19.8 0.5 %collective-permute-start.6 = (bf16[528,128]{1,0:T(8,128)(2,1)S(1)}, bf16[528,128]{1,0:T(8,128)(2,1)S(1)}, u32[]{:S(2)}, u32[]{:S(2)}) collective-permute-start(bf16[528,128]{1,0:T(8,128)(2,1)S(1)} %get-tuple-element.53), channel_id=1, source_target_pairs={{0,1},{1,0},{2,3},{3,2},{4,5},{5,4},{6,7},{7,6},{8,9},{9,8},{10,11... | collective-permute-start | bytes 405512 | tf_op jit(solution)/shard_map/ppermute | solution.py:25
  20.3 0.5 %collective-permute-start.7 = (bf16[528,128]{1,0:T(8,128)(2,1)S(1)}, bf16[528,128]{1,0:T(8,128)(2,1)S(1)}, u32[]{:S(2)}, u32[]{:S(2)}) collective-permute-start(bf16[528,128]{1,0:T(8,128)(2,1)S(1)} %get-tuple-element.54), channel_id=1, source_target_pairs={{0,2},{1,3},{2,0},{3,1},{4,6},{5,7},{6,4},{7,5},{8,10},{9,11},{10,... | collective-permute-start | bytes 405512 | tf_op jit(solution)/shard_map/ppermute | solution.py:25
  20.8 0.0 collective-permute-done.4.recv_ref
  20.8 2.6 %collective-permute-start.8 = (f32[8,128]{1,0:T(8,128)S(1)}, f32[8,128]{1,0:T(8,128)S(1)}, u32[]{:S(2)}, u32[]{:S(2)}) collective-permute-start(f32[8,128]{1,0:T(8,128)S(1)} %shard_map.149.refs_3_), channel_id=1, source_target_pairs={{0,16},{4,20},{8,24},{12,28},{16,0},{20,4},{24,8},{28,12},{1,17},{... | collective-permute-start | bytes 12296 | tf_op jit(solution)/shard_map/ppermute | solution.py:354
  23.4 3.4 %shard_map.148 = (f32[4,1024,128]{2,1,0:T(8,128)S(1)}, f32[4,256,128]{2,1,0:T(8,128)S(1)}, f32[4,256,128]{2,1,0:T(8,128)S(1)}, bf16[256,2048]{1,0:T(8,128)(2,1)}) custom-call(bf16[256,2048]{1,0:T(8,128)(2,1)S(1)} %bitcast.14, bf16[256,512]{1,0:T(8,128)(2,1)S(1)} %bitcast.18, bf16[256,512]{1,0:T(8,128)(2,1)S(1)} %bitcast.20, ...), custom_call_target="tpu_custom_call" | custom-call | flops 1610612736 | bytes 1048576 | tf_op jit(solution)/shard_map/pallas_call | solution.py:315
  26.8 0.0 collective-permute-done.5.refs_1_
  26.8 0.1 collective-permute-done.6.refs_2_
  26.9 0.0 collective-permute-done.7.refs_3_
  26.9 0.1 shard_map.150
  27.1 0.0 collective-permute-done.8.refs_6_
  27.1 1.4 %shard_map.151 = (bf16[256,2048]{1,0:T(8,128)(2,1)}, bf16[256,512]{1,0:T(8,128)(2,1)}, bf16[256,512]{1,0:T(8,128)(2,1)}, bf16[64,512]{1,0:T(8,128)(2,1)}, bf16[64,512]{1,0:T(8,128)(2,1)}) custom-call(f32[4,1024,128]{2,1,0:T(8,128)S(1)} %get-tuple-element.46.refs_0_, f32[4,256,128]{2,1,0:T(8,128)S(1)} %get-tuple-element.47.refs_1_, ...), custom_call_target="tpu_custom_call" | custom-call | bytes 1048576 | tf_op jit(solution)/shard_map/pallas_call | solution.py:315
  (9 shorter events, 0.0 us)
Async XLA Ops:
  0.6 7.8 %copy-start = (bf16[1,1,256,2048]{3,2,1,0:T(8,128)(2,1)S(1)}, bf16[1,1,256,2048]{3,2,1,0:T(8,128)(2,1)}, u32[]{:S(2)}) copy-start(bf16[1,1,256,2048]{3,2,1,0:T(8,128)(2,1)} %param.13) | copy-start | bytes 3145732
  0.6 7.8 %copy-start.1 = (bf16[1,1,256,2048]{3,2,1,0:T(8,128)(2,1)S(1)}, bf16[1,1,256,2048]{3,2,1,0:T(8,128)(2,1)}, u32[]{:S(2)}) copy-start(bf16[1,1,256,2048]{3,2,1,0:T(8,128)(2,1)} %param.10) | copy-start | bytes 3145732
  0.7 7.8 %copy-start.2 = (bf16[1,1,256,512]{3,2,1,0:T(8,128)(2,1)S(1)}, bf16[1,1,256,512]{3,2,1,0:T(8,128)(2,1)}, u32[]{:S(2)}) copy-start(bf16[1,1,256,512]{3,2,1,0:T(8,128)(2,1)} %param.11) | copy-start | bytes 786436
  0.7 7.8 %copy-start.3 = (bf16[1,1,256,512]{3,2,1,0:T(8,128)(2,1)S(1)}, bf16[1,1,256,512]{3,2,1,0:T(8,128)(2,1)}, u32[]{:S(2)}) copy-start(bf16[1,1,256,512]{3,2,1,0:T(8,128)(2,1)} %param.12) | copy-start | bytes 786436
  1.9 11.5 %collective-permute-start.1 = (bf16[128,512]{1,0:T(8,128)(2,1)S(1)}, bf16[128,512]{1,0:T(8,128)(2,1)S(1)}, u32[]{:S(2)}, u32[]{:S(2)}) collective-permute-start(bf16[128,512]{1,0:T(8,128)(2,1)S(1)} %shard_map.146.refs_8_.refs_10_), channel_id=1, source_target_pairs={{0,3},{1,2},{2,1},{3,0},{4,7},{5,6},{6,5},{7,4},{8,11},{9,10},{10,... | collective-permute-start | bytes 393224 | tf_op jit(solution)/shard_map/ppermute | solution.py:25
  5.8 7.5 %collective-permute-start.2 = (bf16[128,512]{1,0:T(8,128)(2,1)S(1)}, bf16[128,512]{1,0:T(8,128)(2,1)S(1)}, u32[]{:S(2)}, u32[]{:S(2)}) collective-permute-start(bf16[128,512]{1,0:T(8,128)(2,1)S(1)} %shard_map.146.refs_8_.refs_10_), channel_id=1, source_target_pairs={{0,1},{1,0},{2,3},{3,2},{4,5},{5,4},{6,7},{7,6},{8,9},{9,8},{10,11... | collective-permute-start | bytes 393224 | tf_op jit(solution)/shard_map/ppermute | solution.py:25
  6.4 7.0 %collective-permute-start.3 = (bf16[128,512]{1,0:T(8,128)(2,1)S(1)}, bf16[128,512]{1,0:T(8,128)(2,1)S(1)}, u32[]{:S(2)}, u32[]{:S(2)}) collective-permute-start(bf16[128,512]{1,0:T(8,128)(2,1)S(1)} %shard_map.146.refs_8_.refs_10_), channel_id=1, source_target_pairs={{0,2},{1,3},{2,0},{3,1},{4,6},{5,7},{6,4},{7,5},{8,10},{9,11},{10,... | collective-permute-start | bytes 393224 | tf_op jit(solution)/shard_map/ppermute | solution.py:25
  6.5 2.0 %collective-permute-start = (s32[1]{0:T(128)}, s32[1]{0:T(128)}, u32[]{:S(2)}, u32[]{:S(2)}) collective-permute-start(s32[1]{0:T(128)} %param.16), channel_id=1, source_target_pairs={{0,4},{4,0},{8,12},{12,8},{16,20},{20,16},{24,28},{28,24},{1,5},{5... | collective-permute-start | bytes 20 | tf_op jit(solution)/shard_map/ppermute | solution.py:354
  11.3 9.5 %collective-permute-start.4 = (f32[8,128]{1,0:T(8,128)S(1)}, f32[8,128]{1,0:T(8,128)S(1)}, u32[]{:S(2)}, u32[]{:S(2)}) collective-permute-start(f32[8,128]{1,0:T(8,128)S(1)} %get-tuple-element.49.tile_ref), channel_id=1, source_target_pairs={{0,8},{4,12},{8,0},{12,4},{16,24},{20,28},{24,16},{28,20},{1,9},{5... | collective-permute-start | bytes 12296 | tf_op jit(solution)/shard_map/ppermute | solution.py:354
  17.3 9.6 %collective-permute-start.5 = (bf16[528,128]{1,0:T(8,128)(2,1)S(1)}, bf16[528,128]{1,0:T(8,128)(2,1)S(1)}, u32[]{:S(2)}, u32[]{:S(2)}) collective-permute-start(bf16[528,128]{1,0:T(8,128)(2,1)S(1)} %get-tuple-element.52), channel_id=1, source_target_pairs={{0,3},{1,2},{2,1},{3,0},{4,7},{5,6},{6,5},{7,4},{8,11},{9,10},{10,... | collective-permute-start | bytes 405512 | tf_op jit(solution)/shard_map/ppermute | solution.py:25
  19.8 7.2 %collective-permute-start.6 = (bf16[528,128]{1,0:T(8,128)(2,1)S(1)}, bf16[528,128]{1,0:T(8,128)(2,1)S(1)}, u32[]{:S(2)}, u32[]{:S(2)}) collective-permute-start(bf16[528,128]{1,0:T(8,128)(2,1)S(1)} %get-tuple-element.53), channel_id=1, source_target_pairs={{0,1},{1,0},{2,3},{3,2},{4,5},{5,4},{6,7},{7,6},{8,9},{9,8},{10,11... | collective-permute-start | bytes 405512 | tf_op jit(solution)/shard_map/ppermute | solution.py:25
  20.3 6.6 %collective-permute-start.7 = (bf16[528,128]{1,0:T(8,128)(2,1)S(1)}, bf16[528,128]{1,0:T(8,128)(2,1)S(1)}, u32[]{:S(2)}, u32[]{:S(2)}) collective-permute-start(bf16[528,128]{1,0:T(8,128)(2,1)S(1)} %get-tuple-element.54), channel_id=1, source_target_pairs={{0,2},{1,3},{2,0},{3,1},{4,6},{5,7},{6,4},{7,5},{8,10},{9,11},{10,... | collective-permute-start | bytes 405512 | tf_op jit(solution)/shard_map/ppermute | solution.py:25
  20.8 6.2 %collective-permute-start.8 = (f32[8,128]{1,0:T(8,128)S(1)}, f32[8,128]{1,0:T(8,128)S(1)}, u32[]{:S(2)}, u32[]{:S(2)}) collective-permute-start(f32[8,128]{1,0:T(8,128)S(1)} %shard_map.149.refs_3_), channel_id=1, source_target_pairs={{0,16},{4,20},{8,24},{12,28},{16,0},{20,4},{24,8},{28,12},{1,17},{... | collective-permute-start | bytes 12296 | tf_op jit(solution)/shard_map/ppermute | solution.py:354

commit v11 on v10

--- a/solution.py
+++ b/solution.py
@@ -227,11 +227,11 @@
         u, ko, vo = stacked(u_ref[:, columns_of(g, width)]), ko_ref[:, cols], vo_ref[:, cols]
         p = jnp.exp2(s_ref[g] - spread(line_ref[g], tokens))
         dp = dot(u, vo, 1, 1)
+        dv = dot(ut_ref[g], p.astype(bf16), 1, 0)
         ds = (p * (dp - spread(delta_ref[g], tokens))).astype(bf16)
         all_ds = jnp.concatenate([ds_ref[g], ds], 1)
         dq_ref[g - begin] = dot(all_ds, jnp.concatenate([keys, ko], 0), 1, 0)
         dk = dot(qt_ref[g], ds, 1, 0)
-        dv = dot(ut_ref[g], p.astype(bf16), 1, 0)
         dko_ref[g - begin] = dk.T
         dvo_ref[g - begin] = dv.T
         return carry

time: 28.6 us -> 28.6 us (level)
  transfers between devices with their start and end apart: 9 -> 9, of which waited for: 1 -> 1; matrix products, arithmetic and copies ran while one was open for 0% -> 0% of each run, Pallas kernels for 36% -> 35%
where the time goes in v11:
time: 28.6 us; the launch traced here: 28.5 us
  starting transfers between devices  12.8 us (45%)
  Pallas kernels  12.6 us (44%)
  between operations  2.71 us (9%)
  waiting for transfers between devices  0.34 us (1%)
    pallas_call x7, Pallas kernels, call(): pl.pallas_call(kernel, in_specs=[spec for spec, _ in ins], out_specs=[spe...  12.6 us
    ppermute x6, starting transfers between devices, swap(): return lax.ppermute(x, 'resp', [(i, i ^ k) for i in range(n)])  8.16 us
    ppermute x3, starting transfers between devices, across(): return lax.ppermute(x, 'prompt', [(i, i ^ k) for i in range(n_prompt)])  4.64 us
  transfers between devices with their start and end apart: 9, of which 1 were waited for; matrix products, arithmetic and copies ran while one was open for 0% of the time, Pallas kernels for 35%

profile of v11, /device:TPU:0, one launch (start us, length us, event | category | flops | bytes accessed | tf_op | source)
XLA Modules:
  0.0 28.5 jit_solution(16467635929803113651)
XLA Ops:
  0.7 1.2 %shard_map.146.refs_8_.refs_10_ = bf16[128,512]{1,0:T(8,128)(2,1)S(1)} custom-call(bf16[64,512]{1,0:T(8,128)(2,1)} %bitcast.25, bf16[64,512]{1,0:T(8,128)(2,1)} %bitcast.26), custom_call_target="tpu_custom_call" | custom-call | flops 5368709120 | bytes 1048576 | tf_op jit(solution)/shard_map/pallas_call | solution.py:315
  1.9 4.0 %collective-permute-start.1 = (bf16[128,512]{1,0:T(8,128)(2,1)S(1)}, bf16[128,512]{1,0:T(8,128)(2,1)S(1)}, u32[]{:S(2)}, u32[]{:S(2)}) collective-permute-start(bf16[128,512]{1,0:T(8,128)(2,1)S(1)} %shard_map.146.refs_8_.refs_10_), channel_id=1, source_target_pairs={{0,3},{1,2},{2,1},{3,0},{4,7},{5,6},{6,5},{7,4},{8,11},{9,10},{10,... | collective-permute-start | bytes 393224 | tf_op jit(solution)/shard_map/ppermute | solution.py:25
  5.8 0.5 %collective-permute-start.2 = (bf16[128,512]{1,0:T(8,128)(2,1)S(1)}, bf16[128,512]{1,0:T(8,128)(2,1)S(1)}, u32[]{:S(2)}, u32[]{:S(2)}) collective-permute-start(bf16[128,512]{1,0:T(8,128)(2,1)S(1)} %shard_map.146.refs_8_.refs_10_), channel_id=1, source_target_pairs={{0,1},{1,0},{2,3},{3,2},{4,5},{5,4},{6,7},{7,6},{8,9},{9,8},{10,11... | collective-permute-start | bytes 393224 | tf_op jit(solution)/shard_map/ppermute | solution.py:25
  6.4 0.1 collective-permute-start.3
  6.5 0.0 collective-permute-start
  8.4 0.0 collective-permute-done.refs_4_
  8.5 2.8 %shard_map.145 = (f32[4,1024,128]{2,1,0:T(8,128)S(1)}, f32[4,1024,128]{2,1,0:T(8,128)S(1)}, f32[8,128]{1,0:T(8,128)S(1)}, f32[8,128]{1,0:T(8,128)S(1)}, f32[8,12...) custom-call(s32[1]{0:T(128)S(6)} %copy.16.refs_0_, ...), custom_call_target="tpu_custom_call" | custom-call | flops 536870912 | bytes 1048576 | tf_op jit(solution)/shard_map/pallas_call | solution.py:315
  11.3 2.0 %collective-permute-start.4 = (f32[8,128]{1,0:T(8,128)S(1)}, f32[8,128]{1,0:T(8,128)S(1)}, u32[]{:S(2)}, u32[]{:S(2)}) collective-permute-start(f32[8,128]{1,0:T(8,128)S(1)} %get-tuple-element.49.tile_ref), channel_id=1, source_target_pairs={{0,8},{4,12},{8,0},{12,4},{16,24},{20,28},{24,16},{28,20},{1,9},{5... | collective-permute-start | bytes 12296 | tf_op jit(solution)/shard_map/ppermute | solution.py:354
  13.4 0.0 collective-permute-done.1.refs_9_.refs_11_
  13.4 0.0 collective-permute-done.2.refs_10_.refs_12_
  13.4 0.0 collective-permute-done.3.refs_11_.refs_13_
  13.4 3.9 %shard_map.147 = (bf16[4,256,512]{2,1,0:T(8,128)(2,1)S(1)}, bf16[4,1024,256]{2,1,0:T(8,128)(2,1)S(1)}, f32[4,1024,128]{2,1,0:T(8,128)S(1)}, f32[4,1024,128]{2,1,...) custom-call(bf16[256,2048]{1,0:T(8,128)(2,1)S(1)} %bitcast.16, ...), custom_call_target="tpu_custom_call" | custom-call | flops 1342177280 | bytes 1048576 | tf_op jit(solution)/shard_map/pallas_call | solution.py:315
  17.3 2.5 %collective-permute-start.5 = (bf16[528,128]{1,0:T(8,128)(2,1)S(1)}, bf16[528,128]{1,0:T(8,128)(2,1)S(1)}, u32[]{:S(2)}, u32[]{:S(2)}) collective-permute-start(bf16[528,128]{1,0:T(8,128)(2,1)S(1)} %get-tuple-element.52), channel_id=1, source_target_pairs={{0,3},{1,2},{2,1},{3,0},{4,7},{5,6},{6,5},{7,4},{8,11},{9,10},{10,... | collective-permute-start | bytes 405512 | tf_op jit(solution)/shard_map/ppermute | solution.py:25
  19.8 0.5 %collective-permute-start.6 = (bf16[528,128]{1,0:T(8,128)(2,1)S(1)}, bf16[528,128]{1,0:T(8,128)(2,1)S(1)}, u32[]{:S(2)}, u32[]{:S(2)}) collective-permute-start(bf16[528,128]{1,0:T(8,128)(2,1)S(1)} %get-tuple-element.53), channel_id=1, source_target_pairs={{0,1},{1,0},{2,3},{3,2},{4,5},{5,4},{6,7},{7,6},{8,9},{9,8},{10,11... | collective-permute-start | bytes 405512 | tf_op jit(solution)/shard_map/ppermute | solution.py:25
  20.3 0.5 %collective-permute-start.7 = (bf16[528,128]{1,0:T(8,128)(2,1)S(1)}, bf16[528,128]{1,0:T(8,128)(2,1)S(1)}, u32[]{:S(2)}, u32[]{:S(2)}) collective-permute-start(bf16[528,128]{1,0:T(8,128)(2,1)S(1)} %get-tuple-element.54), channel_id=1, source_target_pairs={{0,2},{1,3},{2,0},{3,1},{4,6},{5,7},{6,4},{7,5},{8,10},{9,11},{10,... | collective-permute-start | bytes 405512 | tf_op jit(solution)/shard_map/ppermute | solution.py:25
  20.8 0.0 collective-permute-done.4.recv_ref
  20.8 2.6 %collective-permute-start.8 = (f32[8,128]{1,0:T(8,128)S(1)}, f32[8,128]{1,0:T(8,128)S(1)}, u32[]{:S(2)}, u32[]{:S(2)}) collective-permute-start(f32[8,128]{1,0:T(8,128)S(1)} %shard_map.149.refs_3_), channel_id=1, source_target_pairs={{0,16},{4,20},{8,24},{12,28},{16,0},{20,4},{24,8},{28,12},{1,17},{... | collective-permute-start | bytes 12296 | tf_op jit(solution)/shard_map/ppermute | solution.py:354
  23.4 3.2 %shard_map.148 = (f32[4,1024,128]{2,1,0:T(8,128)S(1)}, f32[4,256,128]{2,1,0:T(8,128)S(1)}, f32[4,256,128]{2,1,0:T(8,128)S(1)}, bf16[256,2048]{1,0:T(8,128)(2,1)}) custom-call(bf16[256,2048]{1,0:T(8,128)(2,1)S(1)} %bitcast.14, bf16[256,512]{1,0:T(8,128)(2,1)S(1)} %bitcast.18, bf16[256,512]{1,0:T(8,128)(2,1)S(1)} %bitcast.20, ...), custom_call_target="tpu_custom_call" | custom-call | flops 1610612736 | bytes 1048576 | tf_op jit(solution)/shard_map/pallas_call | solution.py:315
  26.6 0.0 collective-permute-done.5.refs_1_
  26.6 0.3 %collective-permute-done.6.refs_2_ = bf16[528,128]{1,0:T(8,128)(2,1)S(1)} collective-permute-done((bf16[528,128]{1,0:T(8,128)(2,1)S(1)}, bf16[528,128]{1,0:T(8,128)(2,1)S(1)}, u32[]{:S(2)}, u32[]{:S(2)}) %collective-permute-start.6) | collective-permute-done | bytes 135200 | tf_op jit(solution)/shard_map/ppermute | solution.py:25
  26.9 0.0 collective-permute-done.7.refs_3_
  26.9 0.1 shard_map.150
  27.1 0.0 collective-permute-done.8.refs_6_
  27.1 1.4 %shard_map.151 = (bf16[256,2048]{1,0:T(8,128)(2,1)}, bf16[256,512]{1,0:T(8,128)(2,1)}, bf16[256,512]{1,0:T(8,128)(2,1)}, bf16[64,512]{1,0:T(8,128)(2,1)}, bf16[64,512]{1,0:T(8,128)(2,1)}) custom-call(f32[4,1024,128]{2,1,0:T(8,128)S(1)} %get-tuple-element.46.refs_0_, f32[4,256,128]{2,1,0:T(8,128)S(1)} %get-tuple-element.47.refs_1_, ...), custom_call_target="tpu_custom_call" | custom-call | bytes 1048576 | tf_op jit(solution)/shard_map/pallas_call | solution.py:315
  (9 shorter events, 0.0 us)
Async XLA Ops:
  0.6 7.8 %copy-start = (bf16[1,1,256,2048]{3,2,1,0:T(8,128)(2,1)S(1)}, bf16[1,1,256,2048]{3,2,1,0:T(8,128)(2,1)}, u32[]{:S(2)}) copy-start(bf16[1,1,256,2048]{3,2,1,0:T(8,128)(2,1)} %param.13) | copy-start | bytes 3145732
  0.6 7.8 %copy-start.1 = (bf16[1,1,256,2048]{3,2,1,0:T(8,128)(2,1)S(1)}, bf16[1,1,256,2048]{3,2,1,0:T(8,128)(2,1)}, u32[]{:S(2)}) copy-start(bf16[1,1,256,2048]{3,2,1,0:T(8,128)(2,1)} %param.10) | copy-start | bytes 3145732
  0.7 7.8 %copy-start.2 = (bf16[1,1,256,512]{3,2,1,0:T(8,128)(2,1)S(1)}, bf16[1,1,256,512]{3,2,1,0:T(8,128)(2,1)}, u32[]{:S(2)}) copy-start(bf16[1,1,256,512]{3,2,1,0:T(8,128)(2,1)} %param.11) | copy-start | bytes 786436
  0.7 7.8 %copy-start.3 = (bf16[1,1,256,512]{3,2,1,0:T(8,128)(2,1)S(1)}, bf16[1,1,256,512]{3,2,1,0:T(8,128)(2,1)}, u32[]{:S(2)}) copy-start(bf16[1,1,256,512]{3,2,1,0:T(8,128)(2,1)} %param.12) | copy-start | bytes 786436
  1.9 11.5 %collective-permute-start.1 = (bf16[128,512]{1,0:T(8,128)(2,1)S(1)}, bf16[128,512]{1,0:T(8,128)(2,1)S(1)}, u32[]{:S(2)}, u32[]{:S(2)}) collective-permute-start(bf16[128,512]{1,0:T(8,128)(2,1)S(1)} %shard_map.146.refs_8_.refs_10_), channel_id=1, source_target_pairs={{0,3},{1,2},{2,1},{3,0},{4,7},{5,6},{6,5},{7,4},{8,11},{9,10},{10,... | collective-permute-start | bytes 393224 | tf_op jit(solution)/shard_map/ppermute | solution.py:25
  5.8 7.5 %collective-permute-start.2 = (bf16[128,512]{1,0:T(8,128)(2,1)S(1)}, bf16[128,512]{1,0:T(8,128)(2,1)S(1)}, u32[]{:S(2)}, u32[]{:S(2)}) collective-permute-start(bf16[128,512]{1,0:T(8,128)(2,1)S(1)} %shard_map.146.refs_8_.refs_10_), channel_id=1, source_target_pairs={{0,1},{1,0},{2,3},{3,2},{4,5},{5,4},{6,7},{7,6},{8,9},{9,8},{10,11... | collective-permute-start | bytes 393224 | tf_op jit(solution)/shard_map/ppermute | solution.py:25
  6.4 7.0 %collective-permute-start.3 = (bf16[128,512]{1,0:T(8,128)(2,1)S(1)}, bf16[128,512]{1,0:T(8,128)(2,1)S(1)}, u32[]{:S(2)}, u32[]{:S(2)}) collective-permute-start(bf16[128,512]{1,0:T(8,128)(2,1)S(1)} %shard_map.146.refs_8_.refs_10_), channel_id=1, source_target_pairs={{0,2},{1,3},{2,0},{3,1},{4,6},{5,7},{6,4},{7,5},{8,10},{9,11},{10,... | collective-permute-start | bytes 393224 | tf_op jit(solution)/shard_map/ppermute | solution.py:25
  6.5 2.0 %collective-permute-start = (s32[1]{0:T(128)}, s32[1]{0:T(128)}, u32[]{:S(2)}, u32[]{:S(2)}) collective-permute-start(s32[1]{0:T(128)} %param.16), channel_id=1, source_target_pairs={{0,4},{4,0},{8,12},{12,8},{16,20},{20,16},{24,28},{28,24},{1,5},{5... | collective-permute-start | bytes 20 | tf_op jit(solution)/shard_map/ppermute | solution.py:354
  11.3 9.5 %collective-permute-start.4 = (f32[8,128]{1,0:T(8,128)S(1)}, f32[8,128]{1,0:T(8,128)S(1)}, u32[]{:S(2)}, u32[]{:S(2)}) collective-permute-start(f32[8,128]{1,0:T(8,128)S(1)} %get-tuple-element.49.tile_ref), channel_id=1, source_target_pairs={{0,8},{4,12},{8,0},{12,4},{16,24},{20,28},{24,16},{28,20},{1,9},{5... | collective-permute-start | bytes 12296 | tf_op jit(solution)/shard_map/ppermute | solution.py:354
  17.3 9.3 %collective-permute-start.5 = (bf16[528,128]{1,0:T(8,128)(2,1)S(1)}, bf16[528,128]{1,0:T(8,128)(2,1)S(1)}, u32[]{:S(2)}, u32[]{:S(2)}) collective-permute-start(bf16[528,128]{1,0:T(8,128)(2,1)S(1)} %get-tuple-element.52), channel_id=1, source_target_pairs={{0,3},{1,2},{2,1},{3,0},{4,7},{5,6},{6,5},{7,4},{8,11},{9,10},{10,... | collective-permute-start | bytes 405512 | tf_op jit(solution)/shard_map/ppermute | solution.py:25
  19.8 7.2 %collective-permute-start.6 = (bf16[528,128]{1,0:T(8,128)(2,1)S(1)}, bf16[528,128]{1,0:T(8,128)(2,1)S(1)}, u32[]{:S(2)}, u32[]{:S(2)}) collective-permute-start(bf16[528,128]{1,0:T(8,128)(2,1)S(1)} %get-tuple-element.53), channel_id=1, source_target_pairs={{0,1},{1,0},{2,3},{3,2},{4,5},{5,4},{6,7},{7,6},{8,9},{9,8},{10,11... | collective-permute-start | bytes 405512 | tf_op jit(solution)/shard_map/ppermute | solution.py:25
  20.3 6.6 %collective-permute-start.7 = (bf16[528,128]{1,0:T(8,128)(2,1)S(1)}, bf16[528,128]{1,0:T(8,128)(2,1)S(1)}, u32[]{:S(2)}, u32[]{:S(2)}) collective-permute-start(bf16[528,128]{1,0:T(8,128)(2,1)S(1)} %get-tuple-element.54), channel_id=1, source_target_pairs={{0,2},{1,3},{2,0},{3,1},{4,6},{5,7},{6,4},{7,5},{8,10},{9,11},{10,... | collective-permute-start | bytes 405512 | tf_op jit(solution)/shard_map/ppermute | solution.py:25
  20.8 6.2 %collective-permute-start.8 = (f32[8,128]{1,0:T(8,128)S(1)}, f32[8,128]{1,0:T(8,128)S(1)}, u32[]{:S(2)}, u32[]{:S(2)}) collective-permute-start(f32[8,128]{1,0:T(8,128)S(1)} %shard_map.149.refs_3_), channel_id=1, source_target_pairs={{0,16},{4,20},{8,24},{12,28},{16,0},{20,4},{24,8},{28,12},{1,17},{... | collective-permute-start | bytes 12296 | tf_op jit(solution)/shard_map/ppermute | solution.py:354
